TPU v7x, 32 devices: a whole 2x2x4 slice. The times are simulated.
32 devices in a mesh: groups: 2 (over x), gx: 16 (over z, y, core).
Axes of the slice: x: 2, y: 2, z: 4, core: 2. Of those that a mesh axis runs over, the one named last changes fastest.
Arguments:
- snapshots: bfloat16 [256, 4, 512, 128], P('gx', None, 'groups'), parts along dimension 2, may hold values from -20 to 20
- cell_weights: float32 [512, 128], P(('groups', 'gx')), parts along dimension 0, may hold values from 0.5 to 4.5
- diffusivity: float32 [4, 512, 128], P(None, ('groups', 'gx')), parts along dimension 1, may hold values from 0.2 to 2
Outputs:
- diffused_modes: bfloat16 [256, 4, 512, 128], P(None, None, ('groups', 'gx')), parts along dimension 2
- reduced_operator: float32 [512, 256], P('groups'), parts along dimension 0
There are 2 independent parts, one for each index of `groups`. A program takes and returns all parts, laid end to end along the dimension named above; each array names one. Nothing has to cross between parts.
All inputs are finite; a program needn't handle non-finite values.
Results may differ from a plain program's by a relative error of at most 0.0005.
Values may be sent and summed in bfloat16 or wider, within the bound.
No kernel may reach another device: no remote copies, remote signals or barrier semaphores. Data moves between devices by JAX's collectives and lax.ppermute only.
A program may use at most 128 MiB of HBM per device.

v0:
```python
import jax
import jax.numpy as jnp
from jax import lax
from jax.sharding import PartitionSpec as P


def extended(block, sides, width):
    for axis, dim in sides:
        count = lax.axis_size(axis)
        forward = [(i, i + 1) for i in range(count - 1)]
        backward = [(target, source) for source, target in forward]
        low = lax.ppermute(
            lax.slice_in_dim(block, block.shape[dim] - width, None, axis=dim), axis, forward
        )
        high = lax.ppermute(lax.slice_in_dim(block, 0, width, axis=dim), axis, backward)
        block = jnp.concatenate([low, block, high], axis=dim)
    return block


def stencil_apply(padded_x, diffusivity):
    field = padded_x[:, :, 2:-2]
    along_x = (
        -padded_x[:, :, :-4]
        + 16.0 * padded_x[:, :, 1:-3]
        - 30.0 * field
        + 16.0 * padded_x[:, :, 3:-1]
        - padded_x[:, :, 4:]
    ) / 12.0
    padded_y = jnp.pad(field, ((0, 0), (0, 0), (0, 0), (2, 2)))
    along_y = (
        -padded_y[..., :-4]
        + 16.0 * padded_y[..., 1:-3]
        - 30.0 * field
        + 16.0 * padded_y[..., 3:-1]
        - padded_y[..., 4:]
    ) / 12.0
    return diffusivity * (along_x + along_y)


def make_rotation(gram_total):
    lower_factor = jnp.linalg.cholesky(gram_total)
    identity = jnp.eye(gram_total.shape[0], dtype=jnp.float32)
    return jax.scipy.linalg.solve_triangular(lower_factor, identity, lower=True)


def on_device(snapshots, cell_weights, diffusivity):
    highest = lax.Precision.HIGHEST
    pod_block = lax.all_to_all(snapshots, "gx", split_axis=2, concat_axis=0, tiled=True)
    snap_float = pod_block.astype(jnp.float32)
    gram_part = jnp.einsum(
        "svxy,tvxy->st", snap_float, snap_float * cell_weights, precision=highest
    )
    cell_count = pod_block.shape[1] * pod_block.shape[2] * pod_block.shape[3] * lax.axis_size("gx")
    padded_raw = extended(pod_block, (("gx", 2),), 2)
    diffused_raw = stencil_apply(padded_raw.astype(jnp.float32), diffusivity)
    cross_part = jnp.einsum(
        "svxy,tvxy->st", snap_float * cell_weights, diffused_raw, precision=highest
    )
    gram_sum_all, cross_sum_all = lax.psum((gram_part, cross_part), "gx")
    rotation = make_rotation(gram_sum_all / cell_count)
    cross_total = cross_sum_all / cell_count
    reduced = jnp.dot(
        jnp.dot(rotation, cross_total, precision=highest), rotation.T, precision=highest
    )
    diffused = jnp.einsum("st,tvxy->svxy", rotation, diffused_raw, precision=highest)
    return (diffused.astype(jnp.bfloat16), reduced)


def solution(mesh):
    in_specs = (
        P("gx", None, "groups", None),
        P(("groups", "gx"), None),
        P(None, ("groups", "gx"), None),
    )
    out_specs = (P(None, None, ("groups", "gx"), None), P("groups", None))
    return jax.shard_map(
        on_device, mesh=mesh, in_specs=in_specs, out_specs=out_specs, check_vma=False
    )
```

profile of v0, /device:TPU:1, one launch (start us, length us, event | category | flops | bytes accessed | tf_op | source)
XLA Modules:
  0.0 352.5 jit_solution(6415887800945460660)
XLA Ops:
  7.2 0.0 copy-start.3
  7.2 6.9 %copy.12 = bf16[16,4,256,128]{3,0,1,2:T(8,128)(2,1)} copy(bf16[16,4,256,128]{3,2,1,0:T(8,128)(2,1)} %param.3) | data formatting | bytes 8388608 | tf_op args[0]
  14.1 0.0 copy-start.2
  14.1 7.5 %all-to-all-start = ((bf16[16,4,256,128]{3,0,1,2:T(8,128)(2,1)}), bf16[16,4,256,128]{3,0,1,2:T(8,128)(2,1)}, u32[]{:S(2)}, u32[]{:S(2)}) async-start(bf16[16,4,256,128]{3,0,1,2:T(8,128)(2,1)} %copy.12), calls=%async_computation | async-start | bytes 8388608 | tf_op jit(solution)/shard_map/all_to_all | solution.py:48
  21.6 0.0 all-reduce.5.cloned.1.call-start
  21.6 0.0 copy-done.3
  21.6 78.0 %all-to-all-done = bf16[16,4,256,128]{3,0,1,2:T(8,128)(2,1)} async-done(((bf16[16,4,256,128]{3,0,1,2:T(8,128)(2,1)}), bf16[16,4,256,128]{3,0,1,2:T(8,128)(2,1)}, u32[]{:S(2)}, u32[]{:S(2)}) %all-to-all-start) | async-done | bytes 4194336 | tf_op jit(solution)/shard_map/all_to_all | solution.py:48
  99.7 3.4 copy.13
  103.1 0.0 copy-start
  103.1 0.1 fusion.37
  103.2 7.4 %collective-permute-start = (bf16[256,4,2,128]{3,0,2,1:T(8,128)(2,1)S(1)}, bf16[256,4,2,128]{3,0,2,1:T(8,128)(2,1)S(1)}, u32[]{:S(2)}, u32[]{:S(2)}) collective-permute-start(bf16[256,4,2,128]{3,0,2,1:T(8,128)(2,1)S(1)} %get-tuple-element.28), channel_id=1, source_target_pairs={{0,1},{1,2},{2,3},{3,4},{4,5},{5,6},{6,7},{7,8},{8,9},{9,10},{10,1... | collective-permute-start | bytes 1572872 | tf_op jit(solution)/shard_map/ppermute | solution.py:12
  110.6 2.1 collective-permute-start.1
  112.7 0.0 copy-done.2
  112.7 3.3 convert_multiply_fusion
  116.0 4.5 %convolution_bitcast_fusion = f32[256,256]{0,1:T(8,128)} fusion(f32[256,4,16,128]{3,0,2,1:T(8,128)S(1)} %bitcast.59, bf16[256,4,16,128]{3,0,2,1:T(8,128)(2,1)S(1)} %bitcast.56), kind=kOutput, calls=%fused_computation.30 | convolution fusion | flops 6442450944 | bytes 12845056 | tf_op jit(solution)/shard_map/svxy,tvxy->st/dot_general | solution.py:50
  120.5 0.0 copy-done
  120.5 0.0 collective-permute-done
  120.5 0.6 collective-permute-done.1
  121.1 2.6 maximum_convert_fusion
  123.8 3.8 %slice.107 = f32[256,4,16,128]{3,0,2,1:T(8,128)} slice(f32[256,4,20,128]{3,0,2,1:T(8,128)S(1)} %maximum_convert_fusion), slice={[0:256], [0:4], [2:18], [0:128]} | slice | bytes 16777216 | tf_op jit(solution)/shard_map/slice | solution.py:21
  127.5 24.1 %fusion.6 = f32[256,4,16,128]{3,0,2,1:T(8,128)} fusion(f32[256,4,16,128]{3,0,2,1:T(8,128)} %slice.107, f32[256,4,20,128]{3,0,2,1:T(8,128)S(1)} %maximum_convert_fusion, f32[4,16,128]{2,1,0:T(8,128)S(1)} %broadcast_multiply_fusion.1), kind=kLoop, calls=%fused_computation.12 | loop fusion | flops 35651584 | bytes 50364416 | tf_op jit(solution)/shard_map/mul | solution.py:37
  151.6 11.3 %fusion.16 = f32[256,256]{0,1:T(8,128)} fusion(f32[256,4,16,128]{3,0,2,1:T(8,128)} %fusion.6, bf16[256,4,16,128]{3,0,2,1:T(8,128)(2,1)} %bitcast.58, f32[16,128]{1,0:T(8,128)S(1)} %copy-done.2), kind=kOutput, calls=%fused_computation.29 | convolution fusion | flops 6446645248 | bytes 12853248 | tf_op jit(solution)/shard_map/svxy,tvxy->st/dot_general | solution.py:56
  162.9 0.0 all-reduce.5.cloned.1.call-update
  163.0 103.0 %all-reduce.5.cloned.1.call-done = (f32[256,256]{0,1:T(8,128)}, f32[256,256]{0,1:T(8,128)}) async-done(((f32[256,256]{0,1:T(8,128)}, f32[256,256]{0,1:T(8,128)}), (f32[256,256]{0,1:T(8,128)}, f32[256,256]{0,1:T(8,128)})) %all-reduce.5.cloned.1.call-update) | async-done | bytes 524304 | tf_op jit(solution)/shard_map/psum | solution.py:59
  266.0 1.0 broadcast_multiply_fusion
  267.0 0.1 copy.14
  267.1 1.0 fusion.20
  268.1 11.7 %cholesky.50 = f32[128,128]{1,0:T(8,128)S(1)} custom-call(f32[128,128]{1,0:T(8,128)S(1)} %cholesky.118), custom_call_target="Cholesky" | custom-call | tf_op jit(solution)/shard_map/jit(cholesky)/cholesky | solution.py:41
  279.9 9.8 %custom-call.15 = f32[1,128,128]{1,2,0:T(8,128)S(1)} custom-call(f32[1,128,128]{2,1,0:T(8,128)S(1)} %get-tuple-element.33), custom_call_target="InvertDiagBlocksLowerTriangular" | custom-call | tf_op jit(solution)/shard_map/jit(cholesky)/cholesky | solution.py:41
  289.7 0.2 constant_dynamic-update-slice_fusion.1
  289.9 0.3 convolution_subtract_fusion.1
  290.2 11.7 %cholesky.105 = f32[128,128]{1,0:T(8,128)S(1)} custom-call(f32[128,128]{1,0:T(8,128)S(1)} %convolution_subtract_fusion.1), custom_call_target="Cholesky" | custom-call | tf_op jit(solution)/shard_map/jit(cholesky)/cholesky | solution.py:41
  301.9 0.7 compare_reduce_fusion
  304.0 0.1 triangular_solve.63
  304.1 4.1 %while.1 = (s32[]{:T(128)}, f32[256,256]{1,0:T(8,128)S(1)}, s32[2,2]{1,0:T(2,128)S(1)}, f32[2,128,128]{2,1,0:T(8,128)S(1)}, s32[]{:T(128)}) while((s32[]{:T(128)}, f32[256,256]{1,0:T(8,128)S(1)}, s32[2,2]{1,0:T(2,128)S(1)}, f32[2,128,128]{2,1,0:T(8,128)S(1)}, s32[]{:T(128)}) %tuple.31), condition=%wide.while_cond, body=%wide.while_body.sunk | while | flops 2 | bytes 131189 | solution.py:43
  304.1 0.6 fusion.48
  304.7 1.4 bitcast_dynamic-update-slice_fusion.2
  306.1 0.6 fusion.48
  306.7 1.4 bitcast_dynamic-update-slice_fusion.2
  308.1 19.9 %custom-call.16 = f32[2,128,128]{1,2,0:T(8,128)S(1)} custom-call(f32[2,128,128]{2,1,0:T(8,128)S(1)} %get-tuple-element.9), custom_call_target="InvertDiagBlocksLowerTriangular" | custom-call | tf_op jit(solution)/shard_map/jit(_solve_triangular)/triangular_solve | solution.py:43
  328.1 0.3 fusion.25
  328.4 0.3 convolution_subtract_fusion
  328.6 0.3 fusion.28
  328.9 0.0 copy-start.1
  329.0 10.0 %convolution_convert_fusion = bf16[256,4,16,128]{3,0,2,1:T(8,128)(2,1)S(1)} fusion(f32[256,4,16,128]{3,0,2,1:T(8,128)} %fusion.6, f32[128,256]{1,0:T(8,128)S(1)} %fusion.28, f32[128,256]{1,0:T(8,128)S(1)} %fusion.25), kind=kOutput, calls=%fused_computation.28 | convolution fusion | flops 6444613632 | bytes 12845056 | tf_op jit(solution)/shard_map/st,tvxy->svxy/dot_general | solution.py:65
  339.0 4.7 %copy.16 = bf16[256,4,16,128]{3,2,1,0:T(8,128)(2,1)} copy(bf16[256,4,16,128]{3,0,2,1:T(8,128)(2,1)S(1)} %convolution_convert_fusion) | data formatting | bytes 8388608
  343.7 0.0 copy-done.1
  343.7 0.4 fusion.21
  344.1 1.1 fusion.23
  (11 shorter events, 0.2 us)
Async XLA Ops:
  7.2 14.4 %copy-start.3 = (f32[4,16,128]{2,1,0:T(8,128)S(1)}, f32[4,16,128]{2,1,0:T(8,128)}, u32[]{:S(2)}) copy-start(f32[4,16,128]{2,1,0:T(8,128)} %param.5) | copy-start | bytes 98308
  14.1 98.6 %copy-start.2 = (f32[16,128]{1,0:T(8,128)S(1)}, f32[16,128]{1,0:T(8,128)}, u32[]{:S(2)}) copy-start(f32[16,128]{1,0:T(8,128)} %param.4) | copy-start | bytes 24580
  14.1 85.6 %all-to-all-start = ((bf16[16,4,256,128]{3,0,1,2:T(8,128)(2,1)}), bf16[16,4,256,128]{3,0,1,2:T(8,128)(2,1)}, u32[]{:S(2)}, u32[]{:S(2)}) async-start(bf16[16,4,256,128]{3,0,1,2:T(8,128)(2,1)} %copy.12), calls=%async_computation | async-start | bytes 8388608 | tf_op jit(solution)/shard_map/all_to_all | solution.py:48
  21.6 244.4 %all-reduce.5.cloned.1.call-start = ((), (), s32[]{:S(2)}) async-start(), calls=%async_computation.1 | async-start | bytes 1048576 | tf_op jit(solution)/shard_map/psum | solution.py:59
  103.1 17.5 %copy-start = (bf16[16,4,16,16,128]{4,0,2,3,1:T(8,128)(2,1)}, bf16[16,4,16,16,128]{4,0,2,3,1:T(8,128)(2,1)S(1)}, u32[]{:S(2)}) copy-start(bf16[16,4,16,16,128]{4,0,2,3,1:T(8,128)(2,1)S(1)} %copy.13) | copy-start | bytes 12582916
  103.2 17.3 %collective-permute-start = (bf16[256,4,2,128]{3,0,2,1:T(8,128)(2,1)S(1)}, bf16[256,4,2,128]{3,0,2,1:T(8,128)(2,1)S(1)}, u32[]{:S(2)}, u32[]{:S(2)}) collective-permute-start(bf16[256,4,2,128]{3,0,2,1:T(8,128)(2,1)S(1)} %get-tuple-element.28), channel_id=1, source_target_pairs={{0,1},{1,2},{2,3},{3,4},{4,5},{5,6},{6,7},{7,8},{8,9},{9,10},{10,1... | collective-permute-start | bytes 1572872 | tf_op jit(solution)/shard_map/ppermute | solution.py:12
  110.6 10.5 %collective-permute-start.1 = (bf16[256,4,2,128]{3,0,2,1:T(8,128)(2,1)S(1)}, bf16[256,4,2,128]{3,0,2,1:T(8,128)(2,1)S(1)}, u32[]{:S(2)}, u32[]{:S(2)}) collective-permute-start(bf16[256,4,2,128]{3,0,2,1:T(8,128)(2,1)S(1)} %get-tuple-element.29), channel_id=1, source_target_pairs={{1,0},{2,1},{3,2},{4,3},{5,4},{6,5},{7,6},{8,7},{9,8},{10,9},{11,1... | collective-permute-start | bytes 1572872 | tf_op jit(solution)/shard_map/ppermute | solution.py:15
  328.9 14.8 %copy-start.1 = (f32[256,256]{0,1:T(8,128)S(1)}, f32[256,256]{0,1:T(8,128)}, u32[]{:S(2)}) copy-start(f32[256,256]{0,1:T(8,128)} %get-tuple-element.25) | copy-start | bytes 786436
Sparse Core Ops, SparseCore 0:
  163.0 102.9 all-reduce.4
where the time goes:
time: 356 us; the launch traced here: 353 us
  waiting for transfers between devices  182 us (51%)
  other arithmetic  86 us (24%)
  matrix products  28.6 us (8%)
  local copies, waits for them, and re-layouts  23.1 us (6%)
  starting transfers between devices  17 us (5%)
  between operations  16 us (4%)
    psum x1, waiting for transfers between devices, on_device(): gram_sum_all, cross_sum_all = lax.psum((gram_part, cross_part), 'gx')  103 us
    all_to_all x1, waiting for transfers between devices, on_device(): lax.all_to_all(snapshots, 'gx', split_axis=2, concat_axis=0, tiled=True)  78 us
    another operation x6, other arithmetic, make_rotation(): lower_factor = jnp.linalg.cholesky(gram_total)  34 us
    mul x2, other arithmetic, stencil_apply(): return diffusivity * (along_x + along_y)  24.1 us
    another operation x3, other arithmetic, make_rotation(): return jax.scipy.linalg.solve_triangular(lower_factor, identity, lower=True)  20 us
    unnamed x10, local copies, waits for them, and re-layouts  11.6 us
    dot_general x1, matrix products, on_device(): jnp.einsum('svxy,tvxy->st', snap_float * cell_weights, diffused_raw, prec...  11.3 us
    dot_general x1, matrix products, on_device(): jnp.einsum('st,tvxy->svxy', rotation, diffused_raw, precision=highest)  10 us
  transfers between devices with their start and end apart: 4, of which 3 were waited for; matrix products, arithmetic and copies ran while one was open for 2% of the time, Pallas kernels for 0%

commit v1 on v0

v1 whole, which is shorter than its diff:
```python
import jax
import jax.numpy as jnp
from jax import lax
from jax.experimental import pallas as pl
from jax.experimental.pallas import tpu as pltpu
from jax.sharding import PartitionSpec as P

VMEM_LIMIT = 48 * 1024 * 1024
NT = (((1,), (1,)), ((), ()))


def params():
    return pltpu.CompilerParams(vmem_limit_bytes=VMEM_LIMIT)


def split(value):
    high = value.astype(jnp.bfloat16)
    low = (value - high.astype(jnp.float32)).astype(jnp.bfloat16)
    return high, low


def matmul(a, b):
    return jnp.dot(a, b, preferred_element_type=jnp.float32)


def matmul_nt(a, b):
    return lax.dot_general(a, b, NT, preferred_element_type=jnp.float32)


def relayout_kernel(in_ref, out_ref):
    variables = in_ref.shape[1]
    for v in range(variables):
        block = in_ref[:, v].astype(jnp.float32)
        out_ref[0, :, v] = jnp.swapaxes(block, 0, 1).astype(out_ref.dtype)


def relayout(snapshots, owners):
    count, variables, cells, width = snapshots.shape
    rows = cells // owners
    if count % 16 or rows % 16:
        block = snapshots.reshape(count, variables, owners, rows, width)
        return block.transpose(2, 3, 1, 0, 4)
    return pl.pallas_call(
        relayout_kernel,
        grid=(owners,),
        in_specs=[pl.BlockSpec((count, variables, rows, width), lambda i: (0, 0, i, 0))],
        out_specs=pl.BlockSpec((1, rows, variables, count, width), lambda i: (i, 0, 0, 0, 0)),
        out_shape=jax.ShapeDtypeStruct((owners, rows, variables, count, width), snapshots.dtype),
        compiler_params=params(),
        name="relayout",
    )(snapshots)


def row_of(ref, x):
    value = ref[:, x, 0]
    return value.reshape(value.shape[0] * value.shape[1], value.shape[2])


def gram_kernel(x_ref, w_ref, out_ref):
    rows = x_ref.shape[1]

    @pl.when(pl.program_id(0) == 0)
    def _():
        out_ref[...] = jnp.zeros_like(out_ref)

    total = None
    for first in range(0, rows, 4):
        group = range(first, first + 4)
        plain = jnp.concatenate([row_of(x_ref, x) for x in group], axis=1)
        weight = jnp.concatenate([w_ref[x : x + 1, :] for x in group], axis=1)
        high, low = split(plain.astype(jnp.float32) * weight)
        term = matmul_nt(high, plain) + matmul_nt(low, plain)
        total = term if total is None else total + term
    out_ref[...] += total


def gram_of(block, weights):
    owners, rows, variables, count, width = block.shape
    size = owners * count
    return pl.pallas_call(
        gram_kernel,
        grid=(variables,),
        in_specs=[
            pl.BlockSpec((owners, rows, 1, count, width), lambda v: (0, 0, v, 0, 0)),
            pl.BlockSpec((rows, width), lambda v: (0, 0)),
        ],
        out_specs=pl.BlockSpec((size, size), lambda v: (0, 0)),
        out_shape=jax.ShapeDtypeStruct((size, size), jnp.float32),
        compiler_params=params(),
        cost_estimate=pl.CostEstimate(
            flops=4 * size * size * rows * variables * width,
            bytes_accessed=2 * size * rows * variables * width,
            transcendentals=0,
        ),
        name="gram",
    )(block, weights)


def cross_kernel(x_ref, low_ref, high_ref, w_ref, d_ref, band_ref, cross_ref, f_ref):
    rows = x_ref.shape[1]

    @pl.when(pl.program_id(0) == 0)
    def _():
        cross_ref[...] = jnp.zeros_like(cross_ref)

    def row(x):
        if x < 0:
            return row_of(low_ref, x + 2)
        if x >= rows:
            return row_of(high_ref, x - rows)
        return row_of(x_ref, x)

    total = None
    for x in range(0, rows, 2):
        near = jnp.concatenate([row(x + k) for k in range(-2, 4)], axis=1)
        plain = jnp.concatenate([row(x), row(x + 1)], axis=1)
        scale = jnp.concatenate([d_ref[0, x : x + 1, :], d_ref[0, x + 1 : x + 2, :]], axis=1)
        weight = jnp.concatenate([w_ref[x : x + 1, :], w_ref[x + 1 : x + 2, :]], axis=1)
        field = matmul(near, band_ref[...]) * (scale * (1.0 / 12.0))
        high, low = split(field)
        f_ref[0, 0, x // 2] = high
        f_ref[1, 0, x // 2] = low
        high, low = split(field * weight)
        term = matmul_nt(plain, high) + matmul_nt(plain, low)
        total = term if total is None else total + term
    cross_ref[...] += total


def band_matrix(width):
    i = lax.broadcasted_iota(jnp.int32, (6, width, 2, width), 0)
    y = lax.broadcasted_iota(jnp.int32, (6, width, 2, width), 1)
    j = lax.broadcasted_iota(jnp.int32, (6, width, 2, width), 2)
    z = lax.broadcasted_iota(jnp.int32, (6, width, 2, width), 3)
    dx = jnp.abs(i - j - 2)
    dy = jnp.abs(y - z)

    def line(distance, centre):
        return jnp.where(
            distance == 0, centre, jnp.where(distance == 1, 16.0, jnp.where(distance == 2, -1.0, 0.0))
        )

    value = jnp.where(dx == 0, line(dy, -60.0), jnp.where(dy == 0, line(dx, 0.0), 0.0))
    return value.reshape(6 * width, 2 * width).astype(jnp.bfloat16)


def cross_of(block, low, high, weights, diffusivity):
    owners, rows, variables, count, width = block.shape
    size = owners * count
    halo = pl.BlockSpec((owners, 2, 1, count, width), lambda v: (0, 0, v, 0, 0))
    return pl.pallas_call(
        cross_kernel,
        grid=(variables,),
        in_specs=[
            pl.BlockSpec((owners, rows, 1, count, width), lambda v: (0, 0, v, 0, 0)),
            halo,
            halo,
            pl.BlockSpec((rows, width), lambda v: (0, 0)),
            pl.BlockSpec((1, rows, width), lambda v: (v, 0, 0)),
            pl.BlockSpec((6 * width, 2 * width), lambda v: (0, 0)),
        ],
        out_specs=[
            pl.BlockSpec((size, size), lambda v: (0, 0)),
            pl.BlockSpec((2, 1, rows // 2, size, 2 * width), lambda v: (0, v, 0, 0, 0)),
        ],
        out_shape=[
            jax.ShapeDtypeStruct((size, size), jnp.float32),
            jax.ShapeDtypeStruct((2, variables, rows // 2, size, 2 * width), jnp.bfloat16),
        ],
        compiler_params=params(),
        cost_estimate=pl.CostEstimate(
            flops=10 * size * size * rows * variables * width,
            bytes_accessed=6 * size * rows * variables * width,
            transcendentals=0,
        ),
        name="cross",
    )(block, low, high, weights, diffusivity, band_matrix(width))


def modes_kernel(r_ref, f_ref, out_ref, turn_ref):
    pairs, size, width = f_ref.shape[2], f_ref.shape[3], f_ref.shape[4] // 2
    rows = 2 * pairs
    high, low = split(r_ref[...])
    for p in range(pairs):
        first, second = f_ref[0, 0, p], f_ref[1, 0, p]
        value = matmul(high, first) + matmul(high, second) + matmul(low, first)
        for k in range(2):
            turn_ref[pl.ds(2 * p + k, size, stride=rows), :] = value[:, k * width : (k + 1) * width]
    out_ref[:, 0] = turn_ref[...].reshape(size, rows, width).astype(out_ref.dtype)


def modes_of(rotation, field):
    _, variables, pairs, size, width = field.shape
    rows, width = 2 * pairs, width // 2
    return pl.pallas_call(
        modes_kernel,
        grid=(variables,),
        in_specs=[
            pl.BlockSpec((size, size), lambda v: (0, 0)),
            pl.BlockSpec((2, 1, pairs, size, 2 * width), lambda v: (0, v, 0, 0, 0)),
        ],
        out_specs=pl.BlockSpec((size, 1, rows, width), lambda v: (0, v, 0, 0)),
        out_shape=jax.ShapeDtypeStruct((size, variables, rows, width), jnp.bfloat16),
        scratch_shapes=[pltpu.VMEM((size * rows, width), jnp.float32)],
        compiler_params=params(),
        cost_estimate=pl.CostEstimate(
            flops=6 * size * size * rows * variables * width,
            bytes_accessed=6 * size * rows * variables * width,
            transcendentals=0,
        ),
        name="modes",
    )(rotation, field)


def summed(value, axis):
    count = lax.axis_size(axis)
    rows = value.shape[0] // count
    parts = value.reshape(count, rows, value.shape[1])
    own = jnp.sum(lax.all_to_all(parts, axis, 0, 0, tiled=True), axis=0, keepdims=True)
    every = lax.all_to_all(jnp.broadcast_to(own, parts.shape), axis, 0, 0, tiled=True)
    return every.reshape(value.shape)


def shifted(value, axis, step):
    count = lax.axis_size(axis)
    pairs = [(i, i + step) for i in range(count) if 0 <= i + step < count]
    return lax.ppermute(value, axis, pairs)


def make_rotation(gram_total):
    lower_factor = jnp.linalg.cholesky(gram_total)
    identity = jnp.eye(gram_total.shape[0], dtype=jnp.float32)
    return jax.scipy.linalg.solve_triangular(lower_factor, identity, lower=True)


def on_device(snapshots, cell_weights, diffusivity):
    highest = lax.Precision.HIGHEST
    owners = lax.axis_size("gx")
    block = lax.all_to_all(relayout(snapshots, owners), "gx", 0, 0, tiled=True)
    if snapshots.shape[0] % 16:
        count, rows, variables, each, width = block.shape
        block = block.transpose(1, 2, 0, 3, 4).reshape(1, rows, variables, count * each, width)
    rows, variables, width = block.shape[1], block.shape[2], block.shape[4]
    cell_count = rows * variables * width * owners
    gram_part = gram_of(block, cell_weights)
    low = shifted(block[:, rows - 2 :], "gx", 1)
    high = shifted(block[:, :2], "gx", -1)
    cross_part, field = cross_of(block, low, high, cell_weights, diffusivity)
    gram_total = summed(gram_part, "gx")
    cross_total = summed(cross_part, "gx") / cell_count
    rotation = make_rotation(gram_total / cell_count)
    reduced = jnp.dot(
        jnp.dot(rotation, cross_total, precision=highest), rotation.T, precision=highest
    )
    return (modes_of(rotation, field), reduced)


def solution(mesh):
    in_specs = (
        P("gx", None, "groups", None),
        P(("groups", "gx"), None),
        P(None, ("groups", "gx"), None),
    )
    out_specs = (P(None, None, ("groups", "gx"), None), P("groups", None))
    return jax.shard_map(
        on_device, mesh=mesh, in_specs=in_specs, out_specs=out_specs, check_vma=False
    )
```

time: 356 us -> 241 us (0.68)
  waiting for transfers between devices: 182 us -> 84.5 us
  Pallas kernels: 0 us -> 35.7 us
  starting transfers between devices: 17 us -> 49.8 us
  other arithmetic: 86 us -> 54.8 us
  matrix products: 28.6 us -> 2.8 us
  local copies, waits for them, and re-layouts: 23.1 us -> 9.1 us
  between operations: 16 us -> 2.19 us
    psum x1 -> x0, waiting for transfers between devices: 103 us -> none  [on_device(): gram_sum_all, cross_sum_all = lax.psum((gram_part, cross_part), 'gx')]
    all_to_all x1 -> x5, starting transfers between devices: 7.48 us -> 44.3 us  [the longest x2 26.6 us: summed(): lax.all_to_all(parts, axis, 0, 0, tiled=True)]
    pallas_call x0 -> x4, Pallas kernels: none -> 35.7 us  [the longest x1 12.5 us: cross_of(): pl.pallas_call(cross_kernel, grid=(variables,), in_specs=[pl.BlockSpec((o...]
    mul x3 -> x0, other arithmetic: 27.4 us -> none  [the longest x2 24.1 us: stencil_apply(): return diffusivity * (along_x + along_y)]
    dot_general x3 -> x0, matrix products: 25.8 us -> none  [the longest x1 11.3 us: on_device(): jnp.einsum('svxy,tvxy->st', snap_float * cell_weights, diffused_raw, prec...]
    unnamed x10 -> x6, local copies, waits for them, and re-layouts: 11.6 us -> 2.02 us
    ppermute x2, starting transfers between devices: 9.53 us -> 5.46 us  [shifted(): return lax.ppermute(value, axis, pairs)]
    all_to_all x1 -> x5, waiting for transfers between devices: 78 us -> 80.5 us  [the longest x1 78.1 us: on_device(): block = lax.all_to_all(relayout(snapshots, owners), 'gx', 0, 0, tiled=True)]
  transfers between devices with their start and end apart: 4 -> 7, of which waited for: 3 -> 4; matrix products, arithmetic and copies ran while one was open for 2% -> 26% of each run, Pallas kernels for 0% -> 9%
where the time goes in v1:
time: 241 us; the launch traced here: 239 us
  waiting for transfers between devices  84.5 us (35%)
  other arithmetic  54.8 us (23%)
  starting transfers between devices  49.8 us (21%)
  Pallas kernels  35.7 us (15%)
  local copies, waits for them, and re-layouts  9.1 us (4%)
  matrix products  2.8 us (1%)
    all_to_all x1, waiting for transfers between devices, on_device(): block = lax.all_to_all(relayout(snapshots, owners), 'gx', 0, 0, tiled=True)  78.1 us
    another operation x6, other arithmetic, make_rotation(): lower_factor = jnp.linalg.cholesky(gram_total)  34 us
    all_to_all x2, starting transfers between devices, summed(): lax.all_to_all(parts, axis, 0, 0, tiled=True)  26.6 us
    another operation x4, other arithmetic, make_rotation(): return jax.scipy.linalg.solve_triangular(lower_factor, identity, lower=True)  19.9 us
    pallas_call x1, Pallas kernels, cross_of(): pl.pallas_call(cross_kernel, grid=(variables,), in_specs=[pl.BlockSpec((o...  12.5 us
    all_to_all x2, starting transfers between devices, summed(): lax.all_to_all(jnp.broadcast_to(own, parts.shape), axis, 0, 0, tiled=True)  10.3 us
    pallas_call x1, Pallas kernels, relayout(): pl.pallas_call(relayout_kernel, grid=(owners,), in_specs=[pl.BlockSpec((c...  8.97 us
    pallas_call x1, Pallas kernels, modes_of(): pl.pallas_call(modes_kernel, grid=(variables,), in_specs=[pl.BlockSpec((s...  8.64 us
  transfers between devices with their start and end apart: 7, of which 4 were waited for; matrix products, arithmetic and copies ran while one was open for 26% of the time, Pallas kernels for 9%

profile of v1, /device:TPU:1, one launch (start us, length us, event | category | flops | bytes accessed | tf_op | source)
XLA Modules:
  0.0 238.9 jit_solution(17249846360742996095)
XLA Ops:
  0.6 9.0 %relayout.1 = bf16[16,16,4,16,128]{4,3,2,1,0:T(8,128)(2,1)S(1)} custom-call(bf16[16,4,256,128]{3,2,1,0:T(8,128)(2,1)} %in_ref.1), custom_call_target="tpu_custom_call" | custom-call | tf_op jit(solution)/shard_map/relayout/pallas_call | solution.py:43
  9.6 0.0 copy-start
  9.6 2.0 copy-done
  11.6 0.0 copy-start.2
  11.6 7.5 %all-to-all-start = ((bf16[16,16,4,16,128]{4,3,2,1,0:T(8,128)(2,1)}), bf16[16,16,4,16,128]{4,3,2,1,0:T(8,128)(2,1)}, u32[]{:S(2)}, u32[]{:S(2)}) async-start(bf16[16,16,4,16,128]{4,3,2,1,0:T(8,128)(2,1)} %copy-done), calls=%async_computation | async-start | bytes 8388608 | tf_op jit(solution)/shard_map/all_to_all | solution.py:238
  19.1 0.0 copy-start.1
  19.1 78.1 %all-to-all-done.x_ref = bf16[16,16,4,16,128]{4,3,2,1,0:T(8,128)(2,1)} async-done(((bf16[16,16,4,16,128]{4,3,2,1,0:T(8,128)(2,1)}), bf16[16,16,4,16,128]{4,3,2,1,0:T(8,128)(2,1)}, u32[]{:S(2)}, u32[]{:S(2)}) %all-to-all-start) | async-done | bytes 4194336 | tf_op jit(solution)/shard_map/all_to_all | solution.py:238
  97.2 0.0 copy-done.2
  97.2 5.6 %gram.1 = f32[256,256]{1,0:T(8,128)} custom-call(bf16[16,16,4,16,128]{4,3,2,1,0:T(8,128)(2,1)} %all-to-all-done.x_ref, f32[16,128]{1,0:T(8,128)S(1)} %copy-done.2), custom_call_target="tpu_custom_call" | custom-call | flops 2147483648 | bytes 4194304 | tf_op jit(solution)/shard_map/gram/pallas_call | solution.py:80
  102.8 19.3 %all-to-all-start.1 = ((f32[16,16,256]{2,1,0:T(8,128)}), f32[16,16,256]{2,1,0:T(8,128)S(1)}, u32[]{:S(2)}, u32[]{:S(2)}) async-start(f32[16,16,256]{2,1,0:T(8,128)} %bitcast), calls=%async_computation.1 | async-start | bytes 524288 | tf_op jit(solution)/shard_map/all_to_all | solution.py:218
  122.1 1.4 fusion.17
  123.5 3.5 %collective-permute-start = (bf16[16,2,4,16,128]{4,3,2,1,0:T(8,128)(2,1)S(1)}, bf16[16,2,4,16,128]{4,3,2,1,0:T(8,128)(2,1)S(1)}, u32[]{:S(2)}, u32[]{:S(2)}) collective-permute-start(bf16[16,2,4,16,128]{4,3,2,1,0:T(8,128)(2,1)S(1)} %get-tuple-element.25), channel_id=1, source_target_pairs={{0,1},{1,2},{2,3},{3,4},{4,5},{5,6},{6,7},{7,8},{8,9},{9,10},{10,1... | collective-permute-start | bytes 1572872 | tf_op jit(solution)/shard_map/ppermute | solution.py:226
  127.1 1.9 collective-permute-start.1
  129.1 0.7 select_convert_fusion.band_ref
  129.7 1.9 all-to-all-done.1
  131.6 0.7 broadcast_in_dim.35
  132.4 4.3 %all-to-all-start.2 = ((f32[16,16,256]{2,1,0:T(8,128)}), f32[16,16,256]{2,1,0:T(8,128)S(1)}, u32[]{:S(2)}, u32[]{:S(2)}) async-start(f32[16,16,256]{2,1,0:T(8,128)} %broadcast_in_dim.35), calls=%async_computation.2 | async-start | bytes 524288 | tf_op jit(solution)/shard_map/all_to_all | solution.py:219
  136.6 4.0 %collective-permute-done.low_ref = bf16[16,2,4,16,128]{4,3,2,1,0:T(8,128)(2,1)S(1)} collective-permute-done((bf16[16,2,4,16,128]{4,3,2,1,0:T(8,128)(2,1)S(1)}, bf16[16,2,4,16,128]{4,3,2,1,0:T(8,128)(2,1)S(1)}, u32[]{:S(2)}, u32[]{:S(2)}) %collective-permute-start) | collective-permute-done | bytes 524320 | tf_op jit(solution)/shard_map/ppermute | solution.py:226
  140.7 0.0 collective-permute-done.1.high_ref
  140.7 0.0 copy-done.1
  140.7 12.5 %cross.1 = (f32[256,256]{1,0:T(8,128)}, bf16[2,4,8,256,256]{4,3,2,1,0:T(8,128)(2,1)}) custom-call(bf16[16,16,4,16,128]{4,3,2,1,0:T(8,128)(2,1)} %all-to-all-done.x_ref, bf16[16,2,4,16,128]{4,3,2,1,0:T(8,128)(2,1)S(1)} %collective-permute-done.low_ref, bf16[16,2,4,16,128]{4,3,2,1,0:T(8,128)(2,1)S(1)} %collective-permute-done.1.high_ref, ...), custom_call_target="tpu_custom_call" | custom-call | flops 5368709120 | bytes 12582912 | tf_op jit(solution)/shard_map/cross/pallas_call | solution.py:150
  153.1 0.0 all-to-all-done.2
  153.1 7.3 %all-to-all-start.3 = ((f32[16,16,256]{2,1,0:T(8,128)}), f32[16,16,256]{2,1,0:T(8,128)S(1)}, u32[]{:S(2)}, u32[]{:S(2)}) async-start(f32[16,16,256]{2,1,0:T(8,128)} %bitcast.11), calls=%async_computation.3 | async-start | bytes 524288 | tf_op jit(solution)/shard_map/all_to_all | solution.py:218
  160.4 0.1 copy.6
  160.6 11.7 %cholesky.50 = f32[128,128]{1,0:T(8,128)S(1)} custom-call(f32[128,128]{1,0:T(8,128)S(1)} %cholesky.118), custom_call_target="Cholesky" | custom-call | tf_op jit(solution)/shard_map/jit(cholesky)/cholesky | solution.py:230
  172.4 9.8 %custom-call.15 = f32[1,128,128]{1,2,0:T(8,128)S(1)} custom-call(f32[1,128,128]{2,1,0:T(8,128)S(1)} %get-tuple-element.29), custom_call_target="InvertDiagBlocksLowerTriangular" | custom-call | tf_op jit(solution)/shard_map/jit(cholesky)/cholesky | solution.py:230
  182.2 0.2 constant_dynamic-update-slice_fusion.1
  182.4 0.3 convolution_subtract_fusion.1
  182.7 11.7 %cholesky.105 = f32[128,128]{1,0:T(8,128)S(1)} custom-call(f32[128,128]{1,0:T(8,128)S(1)} %convolution_subtract_fusion.1), custom_call_target="Cholesky" | custom-call | tf_op jit(solution)/shard_map/jit(cholesky)/cholesky | solution.py:230
  194.5 0.7 compare_reduce_fusion
  196.5 0.1 triangular_solve.63
  196.6 4.0 %while.1 = (s32[]{:T(128)}, f32[256,256]{1,0:T(8,128)S(1)}, s32[2,2]{1,0:T(2,128)S(1)}, f32[2,128,128]{2,1,0:T(8,128)S(1)}, s32[]{:T(128)}) while((s32[]{:T(128)}, f32[256,256]{1,0:T(8,128)S(1)}, s32[2,2]{1,0:T(2,128)S(1)}, f32[2,128,128]{2,1,0:T(8,128)S(1)}, s32[]{:T(128)}) %tuple.30), condition=%wide.while_cond, body=%wide.while_body.sunk | while | flops 2 | bytes 131181 | solution.py:232
  196.6 0.6 fusion.25
  197.2 1.4 bitcast_dynamic-update-slice_fusion.2
  198.6 0.6 fusion.25
  199.2 1.4 bitcast_dynamic-update-slice_fusion.2
  200.6 19.9 %custom-call.16 = f32[2,128,128]{1,2,0:T(8,128)S(1)} custom-call(f32[2,128,128]{2,1,0:T(8,128)S(1)} %get-tuple-element.13), custom_call_target="InvertDiagBlocksLowerTriangular" | custom-call | tf_op jit(solution)/shard_map/jit(_solve_triangular)/triangular_solve | solution.py:232
  220.5 0.3 fusion.7
  220.8 0.3 convolution_subtract_fusion
  221.1 0.0 all-to-all-done.3
  221.1 0.7 broadcast_in_dim.40
  221.9 6.0 %all-to-all-start.4 = ((f32[16,16,256]{2,1,0:T(8,128)}), f32[16,16,256]{2,1,0:T(8,128)S(1)}, u32[]{:S(2)}, u32[]{:S(2)}) async-start(f32[16,16,256]{2,1,0:T(8,128)} %broadcast_in_dim.40), calls=%async_computation.4 | async-start | bytes 524288 | tf_op jit(solution)/shard_map/all_to_all | solution.py:219
  227.9 0.3 fusion.10
  228.2 8.6 %modes.1 = bf16[256,4,16,128]{3,2,1,0:T(8,128)(2,1)} custom-call(f32[256,256]{1,0:T(8,128)S(1)} %pad_maximum_fusion.r_ref, bf16[2,4,8,256,256]{4,3,2,1,0:T(8,128)(2,1)} %get-tuple-element.4.f_ref), custom_call_target="tpu_custom_call" | custom-call | flops 3221225472 | bytes 12582912 | tf_op jit(solution)/shard_map/modes/pallas_call | solution.py:194
  236.9 0.5 all-to-all-done.4
  237.4 0.4 fusion.15
  237.8 1.1 fusion.14
  (18 shorter events, 0.3 us)
Async XLA Ops:
  9.6 2.0 copy-start
  11.6 85.6 %copy-start.2 = (f32[16,128]{1,0:T(8,128)S(1)}, f32[16,128]{1,0:T(8,128)}, u32[]{:S(2)}) copy-start(f32[16,128]{1,0:T(8,128)} %w_ref.3) | copy-start | bytes 24580
  11.6 85.6 %all-to-all-start = ((bf16[16,16,4,16,128]{4,3,2,1,0:T(8,128)(2,1)}), bf16[16,16,4,16,128]{4,3,2,1,0:T(8,128)(2,1)}, u32[]{:S(2)}, u32[]{:S(2)}) async-start(bf16[16,16,4,16,128]{4,3,2,1,0:T(8,128)(2,1)} %copy-done), calls=%async_computation | async-start | bytes 8388608 | tf_op jit(solution)/shard_map/all_to_all | solution.py:238
  19.1 121.5 %copy-start.1 = (f32[4,16,128]{2,1,0:T(8,128)S(1)}, f32[4,16,128]{2,1,0:T(8,128)}, u32[]{:S(2)}) copy-start(f32[4,16,128]{2,1,0:T(8,128)} %d_ref.1) | copy-start | bytes 98308
  102.8 28.8 %all-to-all-start.1 = ((f32[16,16,256]{2,1,0:T(8,128)}), f32[16,16,256]{2,1,0:T(8,128)S(1)}, u32[]{:S(2)}, u32[]{:S(2)}) async-start(f32[16,16,256]{2,1,0:T(8,128)} %bitcast), calls=%async_computation.1 | async-start | bytes 524288 | tf_op jit(solution)/shard_map/all_to_all | solution.py:218
  123.5 17.1 %collective-permute-start = (bf16[16,2,4,16,128]{4,3,2,1,0:T(8,128)(2,1)S(1)}, bf16[16,2,4,16,128]{4,3,2,1,0:T(8,128)(2,1)S(1)}, u32[]{:S(2)}, u32[]{:S(2)}) collective-permute-start(bf16[16,2,4,16,128]{4,3,2,1,0:T(8,128)(2,1)S(1)} %get-tuple-element.25), channel_id=1, source_target_pairs={{0,1},{1,2},{2,3},{3,4},{4,5},{5,6},{6,7},{7,8},{8,9},{9,10},{10,1... | collective-permute-start | bytes 1572872 | tf_op jit(solution)/shard_map/ppermute | solution.py:226
  127.1 13.6 %collective-permute-start.1 = (bf16[16,2,4,16,128]{4,3,2,1,0:T(8,128)(2,1)S(1)}, bf16[16,2,4,16,128]{4,3,2,1,0:T(8,128)(2,1)S(1)}, u32[]{:S(2)}, u32[]{:S(2)}) collective-permute-start(bf16[16,2,4,16,128]{4,3,2,1,0:T(8,128)(2,1)S(1)} %get-tuple-element.24), channel_id=1, source_target_pairs={{1,0},{2,1},{3,2},{4,3},{5,4},{6,5},{7,6},{8,7},{9,8},{10,9},{11,1... | collective-permute-start | bytes 1572872 | tf_op jit(solution)/shard_map/ppermute | solution.py:226
  132.4 20.8 %all-to-all-start.2 = ((f32[16,16,256]{2,1,0:T(8,128)}), f32[16,16,256]{2,1,0:T(8,128)S(1)}, u32[]{:S(2)}, u32[]{:S(2)}) async-start(f32[16,16,256]{2,1,0:T(8,128)} %broadcast_in_dim.35), calls=%async_computation.2 | async-start | bytes 524288 | tf_op jit(solution)/shard_map/all_to_all | solution.py:219
  153.1 68.0 %all-to-all-start.3 = ((f32[16,16,256]{2,1,0:T(8,128)}), f32[16,16,256]{2,1,0:T(8,128)S(1)}, u32[]{:S(2)}, u32[]{:S(2)}) async-start(f32[16,16,256]{2,1,0:T(8,128)} %bitcast.11), calls=%async_computation.3 | async-start | bytes 524288 | tf_op jit(solution)/shard_map/all_to_all | solution.py:218
  221.9 15.5 %all-to-all-start.4 = ((f32[16,16,256]{2,1,0:T(8,128)}), f32[16,16,256]{2,1,0:T(8,128)S(1)}, u32[]{:S(2)}, u32[]{:S(2)}) async-start(f32[16,16,256]{2,1,0:T(8,128)} %broadcast_in_dim.40), calls=%async_computation.4 | async-start | bytes 524288 | tf_op jit(solution)/shard_map/all_to_all | solution.py:219

commit v2 on v1

--- a/solution.py
+++ b/solution.py
@@ -56,12 +56,35 @@
     return value.reshape(value.shape[0] * value.shape[1], value.shape[2])
 
 
-def gram_kernel(x_ref, w_ref, out_ref):
+def pack(gram):
+    half = gram.shape[0] // 2
+    sub = lax.broadcasted_iota(jnp.int32, (half, half), 0)
+    lane = lax.broadcasted_iota(jnp.int32, (half, half), 1)
+    first, last = gram[:half, :half], gram[half:, half:]
+    diagonal = jnp.sum(jnp.where(lane == sub, first, 0.0), axis=0, keepdims=True)
+    mixed = jnp.where(lane > sub, first, last)
+    top = jnp.concatenate([mixed, gram[:half, half:]], axis=1)
+    return top, jnp.broadcast_to(jnp.concatenate([diagonal, diagonal], axis=1), (16, 2 * half))
+
+
+def unpack(mixed, diagonal):
+    half = mixed.shape[0]
+    sub = lax.broadcasted_iota(jnp.int32, (half, half), 0)
+    lane = lax.broadcasted_iota(jnp.int32, (half, half), 1)
+    upper = jnp.where(lane > sub, mixed, 0.0)
+    lower = jnp.where(lane < sub, mixed, 0.0)
+    first = jnp.where(lane == sub, diagonal, upper + upper.T)
+    last = jnp.where(lane == sub, mixed, lower + lower.T)
+    return first, last
+
+
+def gram_kernel(x_ref, w_ref, out_ref, total_ref):
     rows = x_ref.shape[1]
+    size = total_ref.shape[0]
 
     @pl.when(pl.program_id(0) == 0)
     def _():
-        out_ref[...] = jnp.zeros_like(out_ref)
+        total_ref[...] = jnp.zeros_like(total_ref)
 
     total = None
     for first in range(0, rows, 4):
@@ -71,7 +94,13 @@
         high, low = split(plain.astype(jnp.float32) * weight)
         term = matmul_nt(high, plain) + matmul_nt(low, plain)
         total = term if total is None else total + term
-    out_ref[...] += total
+    total_ref[...] += total
+
+    @pl.when(pl.program_id(0) == pl.num_programs(0) - 1)
+    def _():
+        top, diagonal = pack(total_ref[...])
+        out_ref[: size // 2, :] = top
+        out_ref[size // 2 :, :] = diagonal
 
 
 def gram_of(block, weights):
@@ -84,8 +113,9 @@
             pl.BlockSpec((owners, rows, 1, count, width), lambda v: (0, 0, v, 0, 0)),
             pl.BlockSpec((rows, width), lambda v: (0, 0)),
         ],
-        out_specs=pl.BlockSpec((size, size), lambda v: (0, 0)),
-        out_shape=jax.ShapeDtypeStruct((size, size), jnp.float32),
+        out_specs=pl.BlockSpec((size // 2 + 16, size), lambda v: (0, 0)),
+        out_shape=jax.ShapeDtypeStruct((size // 2 + 16, size), jnp.float32),
+        scratch_shapes=[pltpu.VMEM((size, size), jnp.float32)],
         compiler_params=params(),
         cost_estimate=pl.CostEstimate(
             flops=4 * size * size * rows * variables * width,
@@ -176,6 +206,113 @@
     )(block, low, high, weights, diffusivity, band_matrix(width))
 
 
+PANEL = 32
+GROUP = 8
+
+
+def lanes(value, width):
+    return jnp.concatenate([value] * (width // value.shape[1]), axis=1)
+
+
+def sublanes(value, height):
+    return jnp.concatenate([value] * (height // value.shape[0]), axis=0)
+
+
+def split3(value):
+    high = value.astype(jnp.bfloat16)
+    rest = value - high.astype(jnp.float32)
+    middle = rest.astype(jnp.bfloat16)
+    return high, middle, (rest - middle.astype(jnp.float32)).astype(jnp.bfloat16)
+
+
+def eliminate(panel, start, at):
+    height, size = panel.shape
+    first = start + at
+    sub = lax.broadcasted_iota(jnp.int32, (height, size), 0)
+    lane = lax.broadcasted_iota(jnp.int32, (height, size), 1)
+    sub1 = lax.broadcasted_iota(jnp.int32, (height, 128), 0)
+    lane8 = lax.broadcasted_iota(jnp.int32, (8, size), 1)
+    span = range(GROUP)
+    columns = [jnp.broadcast_to(panel[:, first + i : first + i + 1], (height, 128)) for i in span]
+    rows = [jnp.broadcast_to(panel[at + i : at + i + 1, :], (8, size)) for i in span]
+    entry = {
+        (i, k): jnp.broadcast_to(columns[k][at + i : at + i + 1, :], (8, 128))
+        for i in span
+        for k in range(i, GROUP)
+    }
+    inverse = []
+    for i in span:
+        inverse.append(1.0 / entry[i, i])
+        rows[i] = jnp.where(lane8 == first + i, 1.0, rows[i])
+        for k in range(i + 1, GROUP):
+            factor = entry[i, k] * inverse[i]
+            rows[k] = jnp.where(lane8 == first + i, 0.0, rows[k]) - lanes(factor, size) * rows[i]
+            columns[k] = columns[k] - sublanes(factor, height) * columns[i]
+            for j in range(i + 1, k + 1):
+                entry[j, k] = entry[j, k] - factor * entry[i, j]
+    rows = [
+        jnp.where((lane8 > first + i) & (lane8 < first + GROUP), 0.0, rows[i]) for i in span
+    ]
+    done = at + GROUP
+    result = jnp.where((lane >= first) & (lane < first + GROUP) & (sub >= done), 0.0, panel)
+    for i in span:
+        factor = jnp.where(sub1 >= done, columns[i] * sublanes(inverse[i], height), 0.0)
+        result = result - lanes(factor, size) * sublanes(rows[i], height)
+    for i in span:
+        result = jnp.where(sub == at + i, sublanes(rows[i], height), result)
+    return result, [entry[i, i] for i in span]
+
+
+def rotation_kernel(scale, gram_ref, out_ref, work_ref):
+    size = out_ref.shape[0]
+    half = size // 2
+    first, last = unpack(gram_ref[:half, :half] * scale, gram_ref[half : half + 1, :half] * scale)
+    work_ref[:half, :half] = first
+    work_ref[half:, half:] = last
+    work_ref[:half, half:] = gram_ref[:half, half:] * scale
+    work_ref[half:, :half] = jnp.zeros((half, half), jnp.float32)
+    sub = lax.broadcasted_iota(jnp.int32, (PANEL, size), 0)
+    lane = lax.broadcasted_iota(jnp.int32, (PANEL, size), 1)
+    sub1 = lax.broadcasted_iota(jnp.int32, (PANEL, 128), 0)
+    for start in range(0, size, PANEL):
+        end = start + PANEL
+        panel = work_ref[start:end, :]
+        norm = jnp.zeros((PANEL, 128), jnp.float32)
+        for at in range(0, PANEL, GROUP):
+            panel, pivots = eliminate(panel, start, at)
+            for i, pivot in enumerate(pivots):
+                norm = jnp.where(sub1 == at + i, sublanes(lax.rsqrt(pivot), PANEL), norm)
+        panel = panel * lanes(norm, size)
+        panel = jnp.where((lane > start + sub) & (lane < end), 0.0, panel)
+        out_ref[start:end, :] = jnp.where(lane < end, panel, 0.0)
+        if end < size:
+            high, middle, low = split3(panel)
+            right = jnp.concatenate([high, middle, low, high, middle, high], axis=0)
+            left = jnp.concatenate(
+                [part[:, end:] for part in (high, high, high, middle, middle, low)], axis=0
+            )
+            update = lax.dot_general(
+                left, right, (((0,), (0,)), ((), ())), preferred_element_type=jnp.float32
+            )
+            rest = work_ref[end:, :]
+            place = lax.broadcasted_iota(jnp.int32, rest.shape, 1)
+            work_ref[end:, :] = jnp.where((place >= start) & (place < end), 0.0, rest) - update
+
+
+def rotation_of(packed, cell_count):
+    size = packed.shape[1]
+    return pl.pallas_call(
+        lambda *refs: rotation_kernel(1.0 / cell_count, *refs),
+        out_shape=jax.ShapeDtypeStruct((size, size), jnp.float32),
+        scratch_shapes=[pltpu.VMEM((size, size), jnp.float32)],
+        compiler_params=params(),
+        cost_estimate=pl.CostEstimate(
+            flops=1 << 33, bytes_accessed=8 * size * size, transcendentals=0
+        ),
+        name="rotation",
+    )(packed)
+
+
 def modes_kernel(r_ref, f_ref, out_ref, turn_ref):
     pairs, size, width = f_ref.shape[2], f_ref.shape[3], f_ref.shape[4] // 2
     rows = 2 * pairs
@@ -213,23 +350,28 @@
 
 def summed(value, axis):
     count = lax.axis_size(axis)
-    rows = value.shape[0] // count
-    parts = value.reshape(count, rows, value.shape[1])
-    own = jnp.sum(lax.all_to_all(parts, axis, 0, 0, tiled=True), axis=0, keepdims=True)
-    every = lax.all_to_all(jnp.broadcast_to(own, parts.shape), axis, 0, 0, tiled=True)
-    return every.reshape(value.shape)
+    if count & (count - 1) or count < 2:
+        return lax.psum(value, axis)
+    half = value.shape[0] // 2
+    odd = lax.axis_index(axis) % 2 == 1
+    first, second = value[:half], value[half:]
+
+    def swap(part, step):
+        return lax.ppermute(part, axis, [(i, i ^ step) for i in range(count)])
+
+    own = jnp.where(odd, second, first) + swap(jnp.where(odd, first, second), 1)
+    step = 2
+    while step < count:
+        own = own + swap(own, step)
+        step *= 2
+    other = swap(own, 1)
+    return jnp.concatenate([jnp.where(odd, other, own), jnp.where(odd, own, other)], axis=0)
 
 
 def shifted(value, axis, step):
     count = lax.axis_size(axis)
     pairs = [(i, i + step) for i in range(count) if 0 <= i + step < count]
     return lax.ppermute(value, axis, pairs)
-
-
-def make_rotation(gram_total):
-    lower_factor = jnp.linalg.cholesky(gram_total)
-    identity = jnp.eye(gram_total.shape[0], dtype=jnp.float32)
-    return jax.scipy.linalg.solve_triangular(lower_factor, identity, lower=True)
 
 
 def on_device(snapshots, cell_weights, diffusivity):
@@ -247,7 +389,7 @@
     cross_part, field = cross_of(block, low, high, cell_weights, diffusivity)
     gram_total = summed(gram_part, "gx")
     cross_total = summed(cross_part, "gx") / cell_count
-    rotation = make_rotation(gram_total / cell_count)
+    rotation = rotation_of(gram_total, cell_count)
     reduced = jnp.dot(
         jnp.dot(rotation, cross_total, precision=highest), rotation.T, precision=highest
     )

time: 241 us -> 182 us (0.76)
  other arithmetic: 54.8 us -> 0.87 us
  Pallas kernels: 35.7 us -> 43.5 us
  starting transfers between devices: 49.8 us -> 43.2 us
  local copies, waits for them, and re-layouts: 9.1 us -> 3.43 us
  waiting for transfers between devices: 84.5 us -> 87.7 us
    another operation x10 -> x0, other arithmetic: 54 us -> none  [the longest x6 34 us: make_rotation(): lower_factor = jnp.linalg.cholesky(gram_total)]
    all_to_all x4 -> x0, starting transfers between devices: 36.8 us -> none  [the longest x2 26.6 us: summed(): lax.all_to_all(parts, axis, 0, 0, tiled=True)]
    ppermute x0 -> x10, starting transfers between devices: none -> 26.3 us  [swap(): return lax.ppermute(part, axis, [(i, i ^ step) for i in range(count)])]
    ppermute x0 -> x10, waiting for transfers between devices: none -> 9.61 us  [swap(): return lax.ppermute(part, axis, [(i, i ^ step) for i in range(count)])]
    pallas_call x0 -> x1, Pallas kernels: none -> 8.43 us  [rotation_of(): pl.pallas_call(lambda *refs: rotation_kernel(1.0 / cell_count, *refs), ou...]
    another operation x9 -> x0, local copies, waits for them, and re-layouts: 4.1 us -> none
    ppermute x2, waiting for transfers between devices: 4.04 us -> 0.01 us  [shifted(): return lax.ppermute(value, axis, pairs)]
    ppermute x2, starting transfers between devices: 5.46 us -> 9.36 us  [shifted(): return lax.ppermute(value, axis, pairs)]
  transfers between devices with their start and end apart: 7 -> 13, of which waited for: 4 -> 6; matrix products, arithmetic and copies ran while one was open for 26% -> 0% of each run, Pallas kernels for 9% -> 19%
where the time goes in v2:
time: 182 us; the launch traced here: 181 us
  waiting for transfers between devices  87.7 us (48%)
  Pallas kernels  43.5 us (24%)
  starting transfers between devices  43.2 us (24%)
  local copies, waits for them, and re-layouts  3.43 us (2%)
    all_to_all x1, waiting for transfers between devices, on_device(): block = lax.all_to_all(relayout(snapshots, owners), 'gx', 0, 0, tiled=True)  78.1 us
    ppermute x10, starting transfers between devices, swap(): return lax.ppermute(part, axis, [(i, i ^ step) for i in range(count)])  26.3 us
    pallas_call x1, Pallas kernels, cross_of(): pl.pallas_call(cross_kernel, grid=(variables,), in_specs=[pl.BlockSpec((o...  12.5 us
    ppermute x10, waiting for transfers between devices, swap(): return lax.ppermute(part, axis, [(i, i ^ step) for i in range(count)])  9.61 us
    ppermute x2, starting transfers between devices, shifted(): return lax.ppermute(value, axis, pairs)  9.36 us
    pallas_call x1, Pallas kernels, relayout(): pl.pallas_call(relayout_kernel, grid=(owners,), in_specs=[pl.BlockSpec((c...  8.97 us
    pallas_call x1, Pallas kernels, modes_of(): pl.pallas_call(modes_kernel, grid=(variables,), in_specs=[pl.BlockSpec((s...  8.63 us
    pallas_call x1, Pallas kernels, rotation_of(): pl.pallas_call(lambda *refs: rotation_kernel(1.0 / cell_count, *refs), ou...  8.43 us
  transfers between devices with their start and end apart: 13, of which 6 were waited for; matrix products, arithmetic and copies ran while one was open for 0% of the time, Pallas kernels for 19%

profile of v2, /device:TPU:1, one launch (start us, length us, event | category | flops | bytes accessed | tf_op | source)
XLA Modules:
  0.0 181.0 jit_solution(8495313432613353141)
XLA Ops:
  0.6 9.0 %relayout.1 = bf16[16,16,4,16,128]{4,3,2,1,0:T(8,128)(2,1)S(1)} custom-call(bf16[16,4,256,128]{3,2,1,0:T(8,128)(2,1)} %in_ref.1), custom_call_target="tpu_custom_call" | custom-call | tf_op jit(solution)/shard_map/relayout/pallas_call | solution.py:43
  9.6 0.0 copy-start
  9.6 2.0 %copy-done = bf16[16,16,4,16,128]{4,3,2,1,0:T(8,128)(2,1)} copy-done((bf16[16,16,4,16,128]{4,3,2,1,0:T(8,128)(2,1)}, bf16[16,16,4,16,128]{4,3,2,1,0:T(8,128)(2,1)S(1)}, u32[]{:S(2)}) %copy-start) | copy-done | bytes 4194328
  11.6 0.0 copy-start.2
  11.6 7.5 %all-to-all-start = ((bf16[16,16,4,16,128]{4,3,2,1,0:T(8,128)(2,1)}), bf16[16,16,4,16,128]{4,3,2,1,0:T(8,128)(2,1)}, u32[]{:S(2)}, u32[]{:S(2)}) async-start(bf16[16,16,4,16,128]{4,3,2,1,0:T(8,128)(2,1)} %copy-done), calls=%async_computation | async-start | bytes 8388608 | tf_op jit(solution)/shard_map/all_to_all | solution.py:380
  19.1 78.1 %all-to-all-done.x_ref = bf16[16,16,4,16,128]{4,3,2,1,0:T(8,128)(2,1)} async-done(((bf16[16,16,4,16,128]{4,3,2,1,0:T(8,128)(2,1)}), bf16[16,16,4,16,128]{4,3,2,1,0:T(8,128)(2,1)}, u32[]{:S(2)}, u32[]{:S(2)}) %all-to-all-start) | async-done | bytes 4194336 | tf_op jit(solution)/shard_map/all_to_all | solution.py:380
  97.2 1.4 fusion.12
  98.6 7.4 %collective-permute-start.5 = (bf16[16,2,4,16,128]{4,3,2,1,0:T(8,128)(2,1)S(1)}, bf16[16,2,4,16,128]{4,3,2,1,0:T(8,128)(2,1)S(1)}, u32[]{:S(2)}, u32[]{:S(2)}) collective-permute-start(bf16[16,2,4,16,128]{4,3,2,1,0:T(8,128)(2,1)S(1)} %get-tuple-element.7), channel_id=1, source_target_pairs={{0,1},{1,2},{2,3},{3,4},{4,5},{5,6},{6,7},{7,8},{8,9},{9,10},{10,1... | collective-permute-start | bytes 1572872 | tf_op jit(solution)/shard_map/ppermute | solution.py:374
  106.0 0.0 copy-start.1
  106.1 1.9 %collective-permute-start.6 = (bf16[16,2,4,16,128]{4,3,2,1,0:T(8,128)(2,1)S(1)}, bf16[16,2,4,16,128]{4,3,2,1,0:T(8,128)(2,1)S(1)}, u32[]{:S(2)}, u32[]{:S(2)}) collective-permute-start(bf16[16,2,4,16,128]{4,3,2,1,0:T(8,128)(2,1)S(1)} %get-tuple-element.6), channel_id=1, source_target_pairs={{1,0},{2,1},{3,2},{4,3},{5,4},{6,5},{7,6},{8,7},{9,8},{10,9},{11,1... | collective-permute-start | bytes 1572872 | tf_op jit(solution)/shard_map/ppermute | solution.py:374
  108.0 0.0 copy-done.2
  108.0 5.0 %gram.1 = f32[144,256]{1,0:T(8,128)S(1)} custom-call(bf16[16,16,4,16,128]{4,3,2,1,0:T(8,128)(2,1)} %all-to-all-done.x_ref, f32[16,128]{1,0:T(8,128)S(1)} %copy-done.2), custom_call_target="tpu_custom_call" | custom-call | flops 2147483648 | bytes 4194304 | tf_op jit(solution)/shard_map/gram/pallas_call | solution.py:109
  113.0 0.1 collective-permute-start
  113.1 0.7 select_convert_fusion.band_ref
  113.8 0.6 collective-permute-done
  114.3 10.1 %collective-permute-start.1 = (f32[72,256]{1,0:T(8,128)S(1)}, f32[72,256]{1,0:T(8,128)S(1)}, u32[]{:S(2)}, u32[]{:S(2)}) collective-permute-start(f32[72,256]{1,0:T(8,128)S(1)} %select_add_fusion.1), channel_id=1, source_target_pairs={{0,2},{1,3},{2,0},{3,1},{4,6},{5,7},{6,4},{7,5},{8,10},{9,11},{10,... | collective-permute-start | bytes 221192 | tf_op jit(solution)/shard_map/ppermute | solution.py:360
  124.4 0.0 collective-permute-done.5.low_ref
  124.4 0.0 collective-permute-done.6.high_ref
  124.4 0.0 copy-done.1
  124.4 12.5 %cross.1 = (f32[256,256]{1,0:T(8,128)S(1)}, bf16[2,4,8,256,256]{4,3,2,1,0:T(8,128)(2,1)}) custom-call(bf16[16,16,4,16,128]{4,3,2,1,0:T(8,128)(2,1)} %all-to-all-done.x_ref, bf16[16,2,4,16,128]{4,3,2,1,0:T(8,128)(2,1)S(1)} %collective-permute-done.5.low_ref, bf16[16,2,4,16,128]{4,3,2,1,0:T(8,128)(2,1)S(1)} %collective-permute-done.6.high_ref, ...), custom_call_target="tpu_custom_call" | custom-call | flops 5368709120 | bytes 12582912 | tf_op jit(solution)/shard_map/cross/pallas_call | solution.py:180
  137.0 0.5 collective-permute-start.7
  137.5 0.0 collective-permute-done.1
  137.5 5.4 %collective-permute-start.2 = (f32[72,256]{1,0:T(8,128)S(1)}, f32[72,256]{1,0:T(8,128)S(1)}, u32[]{:S(2)}, u32[]{:S(2)}) collective-permute-start(f32[72,256]{1,0:T(8,128)S(1)} %add.33), channel_id=1, source_target_pairs={{0,4},{1,5},{2,6},{3,7},{4,0},{5,1},{6,2},{7,3},{8,12},{9,13},{10,... | collective-permute-start | bytes 221192 | tf_op jit(solution)/shard_map/ppermute | solution.py:360
  142.9 2.2 %collective-permute-done.2 = f32[72,256]{1,0:T(8,128)S(1)} collective-permute-done((f32[72,256]{1,0:T(8,128)S(1)}, f32[72,256]{1,0:T(8,128)S(1)}, u32[]{:S(2)}, u32[]{:S(2)}) %collective-permute-start.2) | collective-permute-done | bytes 73760 | tf_op jit(solution)/shard_map/ppermute | solution.py:360
  145.1 3.8 %collective-permute-start.3 = (f32[72,256]{1,0:T(8,128)S(1)}, f32[72,256]{1,0:T(8,128)S(1)}, u32[]{:S(2)}, u32[]{:S(2)}) collective-permute-start(f32[72,256]{1,0:T(8,128)S(1)} %add.34), channel_id=1, source_target_pairs={{0,8},{1,9},{2,10},{3,11},{4,12},{5,13},{6,14},{7,15},{8,0},{9,1},... | collective-permute-start | bytes 221192 | tf_op jit(solution)/shard_map/ppermute | solution.py:360
  149.0 0.0 collective-permute-done.7
  149.0 0.7 collective-permute-start.8
  149.7 3.0 %collective-permute-done.3 = f32[72,256]{1,0:T(8,128)S(1)} collective-permute-done((f32[72,256]{1,0:T(8,128)S(1)}, f32[72,256]{1,0:T(8,128)S(1)}, u32[]{:S(2)}, u32[]{:S(2)}) %collective-permute-start.3) | collective-permute-done | bytes 73760 | tf_op jit(solution)/shard_map/ppermute | solution.py:360
  152.7 1.1 collective-permute-start.4
  153.8 0.0 collective-permute-done.8
  153.9 0.1 collective-permute-start.9
  153.9 0.8 collective-permute-done.4
  154.8 3.0 %collective-permute-done.9 = f32[128,256]{1,0:T(8,128)S(1)} collective-permute-done((f32[128,256]{1,0:T(8,128)S(1)}, f32[128,256]{1,0:T(8,128)S(1)}, u32[]{:S(2)}, u32[]{:S(2)}) %collective-permute-start.9) | collective-permute-done | bytes 131104 | tf_op jit(solution)/shard_map/ppermute | solution.py:360
  157.8 3.4 %collective-permute-start.10 = (f32[128,256]{1,0:T(8,128)S(1)}, f32[128,256]{1,0:T(8,128)S(1)}, u32[]{:S(2)}, u32[]{:S(2)}) collective-permute-start(f32[128,256]{1,0:T(8,128)S(1)} %add.38), channel_id=1, source_target_pairs={{0,8},{1,9},{2,10},{3,11},{4,12},{5,13},{6,14},{7,15},{8,0},{9,1},... | collective-permute-start | bytes 393224 | tf_op jit(solution)/shard_map/ppermute | solution.py:360
  161.2 8.4 %rotation.1.r_ref = f32[256,256]{1,0:T(8,128)S(1)} custom-call(f32[144,256]{1,0:T(8,128)S(1)} %pad_maximum_fusion.refs_0_), custom_call_target="tpu_custom_call" | custom-call | flops 8589934592 | bytes 524288 | tf_op jit(solution)/shard_map/rotation/pallas_call | solution.py:304
  169.6 0.0 collective-permute-done.10
  169.7 1.2 collective-permute-start.11
  170.8 8.6 %modes.1 = bf16[256,4,16,128]{3,2,1,0:T(8,128)(2,1)} custom-call(f32[256,256]{1,0:T(8,128)S(1)} %rotation.1.r_ref, bf16[2,4,8,256,256]{4,3,2,1,0:T(8,128)(2,1)} %get-tuple-element.4.f_ref), custom_call_target="tpu_custom_call" | custom-call | flops 3221225472 | bytes 12582912 | tf_op jit(solution)/shard_map/modes/pallas_call | solution.py:331
  179.5 0.0 collective-permute-done.11
  179.5 0.4 fusion.6
  179.9 1.1 fusion.13
  (15 shorter events, 0.2 us)
Async XLA Ops:
  9.6 2.0 %copy-start = (bf16[16,16,4,16,128]{4,3,2,1,0:T(8,128)(2,1)}, bf16[16,16,4,16,128]{4,3,2,1,0:T(8,128)(2,1)S(1)}, u32[]{:S(2)}) copy-start(bf16[16,16,4,16,128]{4,3,2,1,0:T(8,128)(2,1)S(1)} %relayout.1) | copy-start | bytes 12582916
  11.6 96.4 %copy-start.2 = (f32[16,128]{1,0:T(8,128)S(1)}, f32[16,128]{1,0:T(8,128)}, u32[]{:S(2)}) copy-start(f32[16,128]{1,0:T(8,128)} %w_ref.3) | copy-start | bytes 24580
  11.6 85.6 %all-to-all-start = ((bf16[16,16,4,16,128]{4,3,2,1,0:T(8,128)(2,1)}), bf16[16,16,4,16,128]{4,3,2,1,0:T(8,128)(2,1)}, u32[]{:S(2)}, u32[]{:S(2)}) async-start(bf16[16,16,4,16,128]{4,3,2,1,0:T(8,128)(2,1)} %copy-done), calls=%async_computation | async-start | bytes 8388608 | tf_op jit(solution)/shard_map/all_to_all | solution.py:380
  98.6 25.8 %collective-permute-start.5 = (bf16[16,2,4,16,128]{4,3,2,1,0:T(8,128)(2,1)S(1)}, bf16[16,2,4,16,128]{4,3,2,1,0:T(8,128)(2,1)S(1)}, u32[]{:S(2)}, u32[]{:S(2)}) collective-permute-start(bf16[16,2,4,16,128]{4,3,2,1,0:T(8,128)(2,1)S(1)} %get-tuple-element.7), channel_id=1, source_target_pairs={{0,1},{1,2},{2,3},{3,4},{4,5},{5,6},{6,7},{7,8},{8,9},{9,10},{10,1... | collective-permute-start | bytes 1572872 | tf_op jit(solution)/shard_map/ppermute | solution.py:374
  106.0 18.4 %copy-start.1 = (f32[4,16,128]{2,1,0:T(8,128)S(1)}, f32[4,16,128]{2,1,0:T(8,128)}, u32[]{:S(2)}) copy-start(f32[4,16,128]{2,1,0:T(8,128)} %d_ref.1) | copy-start | bytes 98308
  106.1 18.4 %collective-permute-start.6 = (bf16[16,2,4,16,128]{4,3,2,1,0:T(8,128)(2,1)S(1)}, bf16[16,2,4,16,128]{4,3,2,1,0:T(8,128)(2,1)S(1)}, u32[]{:S(2)}, u32[]{:S(2)}) collective-permute-start(bf16[16,2,4,16,128]{4,3,2,1,0:T(8,128)(2,1)S(1)} %get-tuple-element.6), channel_id=1, source_target_pairs={{1,0},{2,1},{3,2},{4,3},{5,4},{6,5},{7,6},{8,7},{9,8},{10,9},{11,1... | collective-permute-start | bytes 1572872 | tf_op jit(solution)/shard_map/ppermute | solution.py:374
  113.0 1.3 collective-permute-start
  114.3 23.1 %collective-permute-start.1 = (f32[72,256]{1,0:T(8,128)S(1)}, f32[72,256]{1,0:T(8,128)S(1)}, u32[]{:S(2)}, u32[]{:S(2)}) collective-permute-start(f32[72,256]{1,0:T(8,128)S(1)} %select_add_fusion.1), channel_id=1, source_target_pairs={{0,2},{1,3},{2,0},{3,1},{4,6},{5,7},{6,4},{7,5},{8,10},{9,11},{10,... | collective-permute-start | bytes 221192 | tf_op jit(solution)/shard_map/ppermute | solution.py:360
  137.0 12.0 %collective-permute-start.7 = (f32[128,256]{1,0:T(8,128)S(1)}, f32[128,256]{1,0:T(8,128)S(1)}, u32[]{:S(2)}, u32[]{:S(2)}) collective-permute-start(f32[128,256]{1,0:T(8,128)S(1)} %slice_select_fusion), channel_id=1, source_target_pairs={{0,1},{1,0},{2,3},{3,2},{4,5},{5,4},{6,7},{7,6},{8,9},{9,8},{10,11... | collective-permute-start | bytes 393224 | tf_op jit(solution)/shard_map/ppermute | solution.py:360
  137.5 7.6 %collective-permute-start.2 = (f32[72,256]{1,0:T(8,128)S(1)}, f32[72,256]{1,0:T(8,128)S(1)}, u32[]{:S(2)}, u32[]{:S(2)}) collective-permute-start(f32[72,256]{1,0:T(8,128)S(1)} %add.33), channel_id=1, source_target_pairs={{0,4},{1,5},{2,6},{3,7},{4,0},{5,1},{6,2},{7,3},{8,12},{9,13},{10,... | collective-permute-start | bytes 221192 | tf_op jit(solution)/shard_map/ppermute | solution.py:360
  145.1 7.6 %collective-permute-start.3 = (f32[72,256]{1,0:T(8,128)S(1)}, f32[72,256]{1,0:T(8,128)S(1)}, u32[]{:S(2)}, u32[]{:S(2)}) collective-permute-start(f32[72,256]{1,0:T(8,128)S(1)} %add.34), channel_id=1, source_target_pairs={{0,8},{1,9},{2,10},{3,11},{4,12},{5,13},{6,14},{7,15},{8,0},{9,1},... | collective-permute-start | bytes 221192 | tf_op jit(solution)/shard_map/ppermute | solution.py:360
  149.0 4.8 %collective-permute-start.8 = (f32[128,256]{1,0:T(8,128)S(1)}, f32[128,256]{1,0:T(8,128)S(1)}, u32[]{:S(2)}, u32[]{:S(2)}) collective-permute-start(f32[128,256]{1,0:T(8,128)S(1)} %select_add_fusion), channel_id=1, source_target_pairs={{0,2},{1,3},{2,0},{3,1},{4,6},{5,7},{6,4},{7,5},{8,10},{9,11},{10,... | collective-permute-start | bytes 393224 | tf_op jit(solution)/shard_map/ppermute | solution.py:360
  152.7 2.0 %collective-permute-start.4 = (f32[72,256]{1,0:T(8,128)S(1)}, f32[72,256]{1,0:T(8,128)S(1)}, u32[]{:S(2)}, u32[]{:S(2)}) collective-permute-start(f32[72,256]{1,0:T(8,128)S(1)} %add.35), channel_id=1, source_target_pairs={{0,1},{1,0},{2,3},{3,2},{4,5},{5,4},{6,7},{7,6},{8,9},{9,8},{10,11... | collective-permute-start | bytes 221192 | tf_op jit(solution)/shard_map/ppermute | solution.py:360
  153.9 3.9 %collective-permute-start.9 = (f32[128,256]{1,0:T(8,128)S(1)}, f32[128,256]{1,0:T(8,128)S(1)}, u32[]{:S(2)}, u32[]{:S(2)}) collective-permute-start(f32[128,256]{1,0:T(8,128)S(1)} %add.37), channel_id=1, source_target_pairs={{0,4},{1,5},{2,6},{3,7},{4,0},{5,1},{6,2},{7,3},{8,12},{9,13},{10,... | collective-permute-start | bytes 393224 | tf_op jit(solution)/shard_map/ppermute | solution.py:360
  157.8 11.9 %collective-permute-start.10 = (f32[128,256]{1,0:T(8,128)S(1)}, f32[128,256]{1,0:T(8,128)S(1)}, u32[]{:S(2)}, u32[]{:S(2)}) collective-permute-start(f32[128,256]{1,0:T(8,128)S(1)} %add.38), channel_id=1, source_target_pairs={{0,8},{1,9},{2,10},{3,11},{4,12},{5,13},{6,14},{7,15},{8,0},{9,1},... | collective-permute-start | bytes 393224 | tf_op jit(solution)/shard_map/ppermute | solution.py:360
  169.7 9.8 %collective-permute-start.11 = (f32[128,256]{1,0:T(8,128)S(1)}, f32[128,256]{1,0:T(8,128)S(1)}, u32[]{:S(2)}, u32[]{:S(2)}) collective-permute-start(f32[128,256]{1,0:T(8,128)S(1)} %add.39), channel_id=1, source_target_pairs={{0,1},{1,0},{2,3},{3,2},{4,5},{5,4},{6,7},{7,6},{8,9},{9,8},{10,11... | collective-permute-start | bytes 393224 | tf_op jit(solution)/shard_map/ppermute | solution.py:360

commit v3 on v2

--- a/solution.py
+++ b/solution.py
@@ -1,3 +1,5 @@
+import functools
+
 import jax
 import jax.numpy as jnp
 from jax import lax
@@ -5,7 +7,7 @@
 from jax.experimental.pallas import tpu as pltpu
 from jax.sharding import PartitionSpec as P
 
-VMEM_LIMIT = 48 * 1024 * 1024
+VMEM_LIMIT = 24 * 1024 * 1024
 NT = (((1,), (1,)), ((), ()))
 
 
@@ -28,10 +30,11 @@
 
 
 def relayout_kernel(in_ref, out_ref):
-    variables = in_ref.shape[1]
-    for v in range(variables):
-        block = in_ref[:, v].astype(jnp.float32)
-        out_ref[0, :, v] = jnp.swapaxes(block, 0, 1).astype(out_ref.dtype)
+    owners, rows, variables = out_ref.shape[:3]
+    for owner in range(owners):
+        for v in range(variables):
+            block = in_ref[:, v, owner * rows : (owner + 1) * rows]
+            out_ref[owner, :, v] = jnp.swapaxes(block, 0, 1)
 
 
 def relayout(snapshots, owners):
@@ -40,19 +43,22 @@
     if count % 16 or rows % 16:
         block = snapshots.reshape(count, variables, owners, rows, width)
         return block.transpose(2, 3, 1, 0, 4)
+    each = owners // 2 if owners % 2 == 0 else 1
     return pl.pallas_call(
         relayout_kernel,
-        grid=(owners,),
-        in_specs=[pl.BlockSpec((count, variables, rows, width), lambda i: (0, 0, i, 0))],
-        out_specs=pl.BlockSpec((1, rows, variables, count, width), lambda i: (i, 0, 0, 0, 0)),
+        grid=(owners // each,),
+        in_specs=[pl.BlockSpec((count, variables, each * rows, width), lambda i: (0, 0, i, 0))],
+        out_specs=pl.BlockSpec(
+            (each, rows, variables, count, width), lambda i: (i, 0, 0, 0, 0)
+        ),
         out_shape=jax.ShapeDtypeStruct((owners, rows, variables, count, width), snapshots.dtype),
-        compiler_params=params(),
+        compiler_params=pltpu.CompilerParams(vmem_limit_bytes=60 * 1024 * 1024),
         name="relayout",
     )(snapshots)
 
 
-def row_of(ref, x):
-    value = ref[:, x, 0]
+def row_of(ref, x, v):
+    value = ref[:, x, v]
     return value.reshape(value.shape[0] * value.shape[1], value.shape[2])
 
 
@@ -87,13 +93,14 @@
         total_ref[...] = jnp.zeros_like(total_ref)
 
     total = None
-    for first in range(0, rows, 4):
-        group = range(first, first + 4)
-        plain = jnp.concatenate([row_of(x_ref, x) for x in group], axis=1)
-        weight = jnp.concatenate([w_ref[x : x + 1, :] for x in group], axis=1)
-        high, low = split(plain.astype(jnp.float32) * weight)
-        term = matmul_nt(high, plain) + matmul_nt(low, plain)
-        total = term if total is None else total + term
+    for v in range(x_ref.shape[2]):
+        for first in range(0, rows, 4):
+            group = range(first, first + 4)
+            plain = jnp.concatenate([row_of(x_ref, x, v) for x in group], axis=1)
+            weight = jnp.concatenate([w_ref[x : x + 1, :] for x in group], axis=1)
+            high, low = split(plain.astype(jnp.float32) * weight)
+            term = matmul_nt(high, plain) + matmul_nt(low, plain)
+            total = term if total is None else total + term
     total_ref[...] += total
 
     @pl.when(pl.program_id(0) == pl.num_programs(0) - 1)
@@ -106,11 +113,12 @@
 def gram_of(block, weights):
     owners, rows, variables, count, width = block.shape
     size = owners * count
+    each = 2 if variables % 2 == 0 else 1
     return pl.pallas_call(
         gram_kernel,
-        grid=(variables,),
+        grid=(variables // each,),
         in_specs=[
-            pl.BlockSpec((owners, rows, 1, count, width), lambda v: (0, 0, v, 0, 0)),
+            pl.BlockSpec((owners, rows, each, count, width), lambda v: (0, 0, v, 0, 0)),
             pl.BlockSpec((rows, width), lambda v: (0, 0)),
         ],
         out_specs=pl.BlockSpec((size // 2 + 16, size), lambda v: (0, 0)),
@@ -126,84 +134,67 @@
     )(block, weights)
 
 
-def cross_kernel(x_ref, low_ref, high_ref, w_ref, d_ref, band_ref, cross_ref, f_ref):
+def cross_kernel(span, odd_ref, x_ref, near_ref, far_ref, w_ref, d_ref, band_ref, cross_ref, f_ref):
     rows = x_ref.shape[1]
-
-    @pl.when(pl.program_id(0) == 0)
-    def _():
-        cross_ref[...] = jnp.zeros_like(cross_ref)
-
-    def row(x):
-        if x < 0:
-            return row_of(low_ref, x + 2)
-        if x >= rows:
-            return row_of(high_ref, x - rows)
-        return row_of(x_ref, x)
-
-    total = None
-    for x in range(0, rows, 2):
-        near = jnp.concatenate([row(x + k) for k in range(-2, 4)], axis=1)
-        plain = jnp.concatenate([row(x), row(x + 1)], axis=1)
-        scale = jnp.concatenate([d_ref[0, x : x + 1, :], d_ref[0, x + 1 : x + 2, :]], axis=1)
-        weight = jnp.concatenate([w_ref[x : x + 1, :], w_ref[x + 1 : x + 2, :]], axis=1)
-        field = matmul(near, band_ref[...]) * (scale * (1.0 / 12.0))
-        high, low = split(field)
-        f_ref[0, 0, x // 2] = high
-        f_ref[1, 0, x // 2] = low
-        high, low = split(field * weight)
-        term = matmul_nt(plain, high) + matmul_nt(plain, low)
-        total = term if total is None else total + term
-    cross_ref[...] += total
+    odd = odd_ref[0] == 1
+    cross_ref[...] = jnp.zeros_like(cross_ref)
+    for place, v in enumerate(span):
+        plain = [row_of(x_ref, x, v) for x in range(rows)]
+        near = [row_of(near_ref, x, v) for x in range(2)]
+        far = [row_of(far_ref, x, v) for x in range(2)]
+        below = [jnp.where(odd, near[x], far[x]) for x in range(2)]
+        above = [jnp.where(odd, far[x], near[x]) for x in range(2)]
+        value = [part.astype(jnp.float32) for part in below + plain + above]
+        total = None
+        for x in range(0, rows, 2):
+            pair = jnp.concatenate(plain[x : x + 2], axis=1)
+            along_x = [
+                16.0 * (value[k + 1] + value[k + 3]) - (value[k] + value[k + 4])
+                for k in (x, x + 1)
+            ]
+            scale = jnp.concatenate([d_ref[v, x : x + 1, :], d_ref[v, x + 1 : x + 2, :]], axis=1)
+            weight = jnp.concatenate([w_ref[x : x + 1, :], w_ref[x + 1 : x + 2, :]], axis=1)
+            both = matmul(pair, band_ref[...]) + jnp.concatenate(along_x, axis=1)
+            field = both * (scale * (1.0 / 12.0))
+            high, low = split(field)
+            f_ref[0, place, x // 2] = high
+            f_ref[1, place, x // 2] = low
+            term = matmul_nt(jnp.concatenate(split(field * weight), axis=0), pair)
+            term = term[: term.shape[0] // 2] + term[term.shape[0] // 2 :]
+            total = term if total is None else total + term
+        cross_ref[...] += total
 
 
 def band_matrix(width):
-    i = lax.broadcasted_iota(jnp.int32, (6, width, 2, width), 0)
-    y = lax.broadcasted_iota(jnp.int32, (6, width, 2, width), 1)
-    j = lax.broadcasted_iota(jnp.int32, (6, width, 2, width), 2)
-    z = lax.broadcasted_iota(jnp.int32, (6, width, 2, width), 3)
-    dx = jnp.abs(i - j - 2)
-    dy = jnp.abs(y - z)
-
-    def line(distance, centre):
-        return jnp.where(
-            distance == 0, centre, jnp.where(distance == 1, 16.0, jnp.where(distance == 2, -1.0, 0.0))
-        )
-
-    value = jnp.where(dx == 0, line(dy, -60.0), jnp.where(dy == 0, line(dx, 0.0), 0.0))
-    return value.reshape(6 * width, 2 * width).astype(jnp.bfloat16)
-
-
-def cross_of(block, low, high, weights, diffusivity):
+    shape = (2, width, 2, width)
+    i, y, j, z = (lax.broadcasted_iota(jnp.int32, shape, axis) for axis in range(4))
+    distance = jnp.abs(y - z)
+    line = jnp.where(
+        distance == 0, -60.0, jnp.where(distance == 1, 16.0, jnp.where(distance == 2, -1.0, 0.0))
+    )
+    return jnp.where(i == j, line, 0.0).reshape(2 * width, 2 * width).astype(jnp.bfloat16)
+
+
+def cross_of(span, odd, block, near, far, weights, diffusivity, band):
     owners, rows, variables, count, width = block.shape
     size = owners * count
-    halo = pl.BlockSpec((owners, 2, 1, count, width), lambda v: (0, 0, v, 0, 0))
+    vmem = pl.BlockSpec(memory_space=pltpu.VMEM)
     return pl.pallas_call(
-        cross_kernel,
-        grid=(variables,),
-        in_specs=[
-            pl.BlockSpec((owners, rows, 1, count, width), lambda v: (0, 0, v, 0, 0)),
-            halo,
-            halo,
-            pl.BlockSpec((rows, width), lambda v: (0, 0)),
-            pl.BlockSpec((1, rows, width), lambda v: (v, 0, 0)),
-            pl.BlockSpec((6 * width, 2 * width), lambda v: (0, 0)),
-        ],
-        out_specs=[
-            pl.BlockSpec((size, size), lambda v: (0, 0)),
-            pl.BlockSpec((2, 1, rows // 2, size, 2 * width), lambda v: (0, v, 0, 0, 0)),
-        ],
+        lambda *refs: cross_kernel(span, *refs),
+        in_specs=[pl.BlockSpec(memory_space=pltpu.SMEM)] + [vmem] * 6,
+        out_specs=[vmem, vmem],
         out_shape=[
             jax.ShapeDtypeStruct((size, size), jnp.float32),
-            jax.ShapeDtypeStruct((2, variables, rows // 2, size, 2 * width), jnp.bfloat16),
+            jax.ShapeDtypeStruct((2, len(span), rows // 2, size, 2 * width), jnp.bfloat16),
         ],
         compiler_params=params(),
         cost_estimate=pl.CostEstimate(
-            flops=10 * size * size * rows * variables * width,
-            bytes_accessed=6 * size * rows * variables * width,
+            flops=12 * size * size * rows * len(span) * width,
+            bytes_accessed=6 * size * rows * len(span) * width,
             transcendentals=0,
         ),
         name="cross",
-    )(block, low, high, weights, diffusivity, band_matrix(width))
+    )(odd, block, near, far, weights, diffusivity, band)
 
 
 PANEL = 32
@@ -313,39 +304,47 @@
     )(packed)
 
 
-def modes_kernel(r_ref, f_ref, out_ref, turn_ref):
-    pairs, size, width = f_ref.shape[2], f_ref.shape[3], f_ref.shape[4] // 2
-    rows = 2 * pairs
+def modes_kernel(r_ref, *refs):
+    fields, out_ref = refs[:-1], refs[-1]
     high, low = split(r_ref[...])
-    for p in range(pairs):
-        first, second = f_ref[0, 0, p], f_ref[1, 0, p]
-        value = matmul(high, first) + matmul(high, second) + matmul(low, first)
-        for k in range(2):
-            turn_ref[pl.ds(2 * p + k, size, stride=rows), :] = value[:, k * width : (k + 1) * width]
-    out_ref[:, 0] = turn_ref[...].reshape(size, rows, width).astype(out_ref.dtype)
-
-
-def modes_of(rotation, field):
-    _, variables, pairs, size, width = field.shape
+    at = pl.program_id(0)
+
+    def store(field, v):
+        width = field.shape[4] // 2
+        rows = []
+        for p in range(field.shape[2]):
+            first, second = field[0, v, p], field[1, v, p]
+            value = matmul(high, first) + matmul(high, second) + matmul(low, first)
+            value = value.astype(out_ref.dtype)
+            rows += [value[:, :width], value[:, width:]]
+        out_ref[:, 0] = jnp.swapaxes(jnp.stack(rows, axis=0), 0, 1)
+
+    first = 0
+    for field in fields:
+        last = first + field.shape[1]
+        pl.when((at >= first) & (at < last))(functools.partial(store, field, at - first))
+        first = last
+
+
+def modes_of(rotation, fields):
+    _, _, pairs, size, width = fields[0].shape
+    variables = sum(field.shape[1] for field in fields)
     rows, width = 2 * pairs, width // 2
+    vmem = pl.BlockSpec(memory_space=pltpu.VMEM)
     return pl.pallas_call(
         modes_kernel,
         grid=(variables,),
-        in_specs=[
-            pl.BlockSpec((size, size), lambda v: (0, 0)),
-            pl.BlockSpec((2, 1, pairs, size, 2 * width), lambda v: (0, v, 0, 0, 0)),
-        ],
+        in_specs=[pl.BlockSpec((size, size), lambda v: (0, 0))] + [vmem] * len(fields),
         out_specs=pl.BlockSpec((size, 1, rows, width), lambda v: (0, v, 0, 0)),
         out_shape=jax.ShapeDtypeStruct((size, variables, rows, width), jnp.bfloat16),
-        scratch_shapes=[pltpu.VMEM((size * rows, width), jnp.float32)],
         compiler_params=params(),
         cost_estimate=pl.CostEstimate(
-            flops=6 * size * size * rows * variables * width,
+            flops=10 * size * size * rows * variables * width,
             bytes_accessed=6 * size * rows * variables * width,
             transcendentals=0,
         ),
         name="modes",
-    )(rotation, field)
+    )(rotation, *fields)
 
 
 def summed(value, axis):
@@ -368,10 +367,16 @@
     return jnp.concatenate([jnp.where(odd, other, own), jnp.where(odd, own, other)], axis=0)
 
 
-def shifted(value, axis, step):
+def edges(block, axis):
     count = lax.axis_size(axis)
-    pairs = [(i, i + step) for i in range(count) if 0 <= i + step < count]
-    return lax.ppermute(value, axis, pairs)
+    rows = block.shape[1]
+    odd = lax.axis_index(axis) % 2 == 1
+    received = []
+    for start, first in ((jnp.where(odd, 0, rows - 2), 0), (jnp.where(odd, rows - 2, 0), 1)):
+        part = lax.dynamic_slice_in_dim(block, start, 2, axis=1)
+        pairs = [(i, i + 1) for i in range(first, count - 1, 2)]
+        received.append(lax.ppermute(part, axis, pairs + [(b, a) for a, b in pairs]))
+    return received
 
 
 def on_device(snapshots, cell_weights, diffusivity):
@@ -383,17 +388,25 @@
         block = block.transpose(1, 2, 0, 3, 4).reshape(1, rows, variables, count * each, width)
     rows, variables, width = block.shape[1], block.shape[2], block.shape[4]
     cell_count = rows * variables * width * owners
+    near, far = edges(block, "gx")
     gram_part = gram_of(block, cell_weights)
-    low = shifted(block[:, rows - 2 :], "gx", 1)
-    high = shifted(block[:, :2], "gx", -1)
-    cross_part, field = cross_of(block, low, high, cell_weights, diffusivity)
+    odd = (lax.axis_index("gx") % 2).astype(jnp.int32).reshape(1)
+    band = band_matrix(width)
+    half = variables // 2
+    crosses, fields = zip(
+        *(
+            cross_of(span, odd, block, near, far, cell_weights, diffusivity, band)
+            for span in (range(half), range(half, variables))
+            if len(span)
+        )
+    )
     gram_total = summed(gram_part, "gx")
-    cross_total = summed(cross_part, "gx") / cell_count
+    cross_total = summed(sum(crosses[1:], crosses[0]), "gx") * (1.0 / cell_count)
     rotation = rotation_of(gram_total, cell_count)
     reduced = jnp.dot(
-        jnp.dot(rotation, cross_total, precision=highest), rotation.T, precision=highest
+        jnp.dot(rotation, cross_total.T, precision=highest), rotation.T, precision=highest
     )
-    return (modes_of(rotation, field), reduced)
+    return (modes_of(rotation, fields), reduced)
 
 
 def solution(mesh):

time: 182 us -> 170 us (0.934)
  Pallas kernels: 43.5 us -> 33.6 us
  local copies, waits for them, and re-layouts: 3.43 us -> 1.43 us
    pallas_call x3 -> x4, Pallas kernels: 26.5 us -> 19.1 us  [the longest x2 10.4 us: cross_of(): pl.pallas_call(lambda *refs: cross_kernel(span, *refs), in_specs=[pl.Bloc...]
    ppermute x10, starting transfers between devices: 26.3 us -> 29.2 us  [swap(): return lax.ppermute(part, axis, [(i, i ^ step) for i in range(count)])]
    pallas_call x1, Pallas kernels: 8.63 us -> 6.01 us  [modes_of(): pl.pallas_call(modes_kernel, grid=(variables,), in_specs=[pl.BlockSpec((s...]
    unnamed x6 -> x4, local copies, waits for them, and re-layouts: 2.02 us -> 0.01 us
  transfers between devices with their start and end apart: 13 -> 13, of which waited for: 6 -> 6; matrix products, arithmetic and copies ran while one was open for 0% -> 0% of each run, Pallas kernels for 19% -> 17%
where the time goes in v3:
time: 170 us
  waiting for transfers between devices  86.8 us (51%)
  starting transfers between devices  45 us (26%)
  Pallas kernels  33.6 us (20%)
    all_to_all x1, waiting for transfers between devices, on_device(): block = lax.all_to_all(relayout(snapshots, owners), 'gx', 0, 0, tiled=True)  78.1 us
    ppermute x10, starting transfers between devices, swap(): return lax.ppermute(part, axis, [(i, i ^ step) for i in range(count)])  29.2 us
    pallas_call x2, Pallas kernels, cross_of(): pl.pallas_call(lambda *refs: cross_kernel(span, *refs), in_specs=[pl.Bloc...  10.4 us
    ppermute x10, waiting for transfers between devices, swap(): return lax.ppermute(part, axis, [(i, i ^ step) for i in range(count)])  8.72 us
    pallas_call x1, Pallas kernels, rotation_of(): pl.pallas_call(lambda *refs: rotation_kernel(1.0 / cell_count, *refs), ou...  8.43 us
    ppermute x2, starting transfers between devices, edges(): lax.ppermute(part, axis, pairs + [(b, a) for a, b in pairs])  8.37 us
    all_to_all x1, starting transfers between devices, on_device(): block = lax.all_to_all(relayout(snapshots, owners), 'gx', 0, 0, tiled=True)  7.48 us
    pallas_call x1, Pallas kernels, modes_of(): pl.pallas_call(modes_kernel, grid=(variables,), in_specs=[pl.BlockSpec((s...  6.01 us
  transfers between devices with their start and end apart: 13, of which 6 were waited for; matrix products, arithmetic and copies ran while one was open for 0% of the time, Pallas kernels for 17%

profile of v3, /device:TPU:1, one launch (start us, length us, event | category | flops | bytes accessed | tf_op | source)
XLA Modules:
  0.0 169.6 jit_solution(12702169671127525645)
XLA Ops:
  0.6 4.3 %relayout.1 = bf16[16,16,4,16,128]{4,3,2,1,0:T(8,128)(2,1)} custom-call(bf16[16,4,256,128]{3,2,1,0:T(8,128)(2,1)} %in_ref.1), custom_call_target="tpu_custom_call" | custom-call | tf_op jit(solution)/shard_map/relayout/pallas_call | solution.py:47
  4.9 0.0 copy-start.1
  4.9 7.5 %all-to-all-start = ((bf16[16,16,4,16,128]{4,3,2,1,0:T(8,128)(2,1)}), bf16[16,16,4,16,128]{4,3,2,1,0:T(8,128)(2,1)}, u32[]{:S(2)}, u32[]{:S(2)}) async-start(bf16[16,16,4,16,128]{4,3,2,1,0:T(8,128)(2,1)} %relayout.1), calls=%async_computation | async-start | bytes 8388608 | tf_op jit(solution)/shard_map/all_to_all | solution.py:385
  12.4 78.1 %all-to-all-done.x_ref.refs_1_ = bf16[16,16,4,16,128]{4,3,2,1,0:T(8,128)(2,1)} async-done(((bf16[16,16,4,16,128]{4,3,2,1,0:T(8,128)(2,1)}), bf16[16,16,4,16,128]{4,3,2,1,0:T(8,128)(2,1)}, u32[]{:S(2)}, u32[]{:S(2)}) %all-to-all-start) | async-done | bytes 4194336 | tf_op jit(solution)/shard_map/all_to_all | solution.py:385
  90.5 1.4 constant_dynamic-slice_fusion
  91.9 0.1 collective-permute-start.5
  92.0 0.0 copy-start
  92.0 8.3 %collective-permute-start.6 = (bf16[16,2,4,16,128]{4,3,2,1,0:T(8,128)(2,1)S(1)}, bf16[16,2,4,16,128]{4,3,2,1,0:T(8,128)(2,1)S(1)}, u32[]{:S(2)}, u32[]{:S(2)}) collective-permute-start(bf16[16,2,4,16,128]{4,3,2,1,0:T(8,128)(2,1)S(1)} %get-tuple-element.10), channel_id=1, source_target_pairs={{1,2},{3,4},{5,6},{7,8},{9,10},{11,12},{13,14},{2,1},{4,3},{6,5},{... | collective-permute-start | bytes 1572872 | tf_op jit(solution)/shard_map/ppermute | solution.py:378
  100.3 0.0 copy-done.1
  100.3 4.5 %gram.1 = f32[144,256]{1,0:T(8,128)S(1)} custom-call(bf16[16,16,4,16,128]{4,3,2,1,0:T(8,128)(2,1)} %all-to-all-done.x_ref.refs_1_, f32[16,128]{1,0:T(8,128)S(1)} %copy-done.1), custom_call_target="tpu_custom_call" | custom-call | flops 2147483648 | bytes 4194304 | tf_op jit(solution)/shard_map/gram/pallas_call | solution.py:117
  104.8 0.1 collective-permute-start
  104.9 0.2 select_convert_fusion.refs_6_
  105.1 1.1 collective-permute-done
  106.2 9.2 %collective-permute-start.1 = (f32[72,256]{1,0:T(8,128)S(1)}, f32[72,256]{1,0:T(8,128)S(1)}, u32[]{:S(2)}, u32[]{:S(2)}) collective-permute-start(f32[72,256]{1,0:T(8,128)S(1)} %select_add_fusion.1), channel_id=1, source_target_pairs={{0,2},{1,3},{2,0},{3,1},{4,6},{5,7},{6,4},{7,5},{8,10},{9,11},{10,... | collective-permute-start | bytes 221192 | tf_op jit(solution)/shard_map/ppermute | solution.py:359
  115.4 0.0 collective-permute-done.5.refs_2_
  115.4 0.0 collective-permute-done.6.refs_3_
  115.4 0.0 copy-done
  115.4 5.2 %cross.3 = (f32[256,256]{1,0:T(8,128)S(1)}, bf16[2,2,8,256,256]{4,3,2,1,0:T(8,128)(2,1)S(1)}) custom-call(s32[1]{0:T(128)} %bitcast.refs_0_, bf16[16,16,4,16,128]{4,3,2,1,0:T(8,128)(2,1)} %all-to-all-done.x_ref.refs_1_, bf16[16,2,4,16,128]{4,3,2,1,0:T(8,128)(2,1)S(1)} %collective-permute-done.5.refs_2_, ...), custom_call_target="tpu_custom_call" | custom-call | flops 3221225472 | bytes 6291456 | tf_op jit(solution)/shard_map/cross/pallas_call | solution.py:182
  120.6 5.2 %cross.2 = (f32[256,256]{1,0:T(8,128)S(1)}, bf16[2,2,8,256,256]{4,3,2,1,0:T(8,128)(2,1)S(1)}) custom-call(s32[1]{0:T(128)} %bitcast.refs_0_, bf16[16,16,4,16,128]{4,3,2,1,0:T(8,128)(2,1)} %all-to-all-done.x_ref.refs_1_, bf16[16,2,4,16,128]{4,3,2,1,0:T(8,128)(2,1)S(1)} %collective-permute-done.5.refs_2_, ...), custom_call_target="tpu_custom_call" | custom-call | flops 3221225472 | bytes 6291456 | tf_op jit(solution)/shard_map/cross/pallas_call | solution.py:182
  125.9 0.5 collective-permute-start.7
  126.4 0.0 collective-permute-done.1
  126.4 8.1 %collective-permute-start.2 = (f32[72,256]{1,0:T(8,128)S(1)}, f32[72,256]{1,0:T(8,128)S(1)}, u32[]{:S(2)}, u32[]{:S(2)}) collective-permute-start(f32[72,256]{1,0:T(8,128)S(1)} %add.38), channel_id=1, source_target_pairs={{0,4},{1,5},{2,6},{3,7},{4,0},{5,1},{6,2},{7,3},{8,12},{9,13},{10,... | collective-permute-start | bytes 221192 | tf_op jit(solution)/shard_map/ppermute | solution.py:359
  134.5 2.2 %collective-permute-done.2 = f32[72,256]{1,0:T(8,128)S(1)} collective-permute-done((f32[72,256]{1,0:T(8,128)S(1)}, f32[72,256]{1,0:T(8,128)S(1)}, u32[]{:S(2)}, u32[]{:S(2)}) %collective-permute-start.2) | collective-permute-done | bytes 73760 | tf_op jit(solution)/shard_map/ppermute | solution.py:359
  136.7 3.5 %collective-permute-start.3 = (f32[72,256]{1,0:T(8,128)S(1)}, f32[72,256]{1,0:T(8,128)S(1)}, u32[]{:S(2)}, u32[]{:S(2)}) collective-permute-start(f32[72,256]{1,0:T(8,128)S(1)} %add.39), channel_id=1, source_target_pairs={{0,8},{1,9},{2,10},{3,11},{4,12},{5,13},{6,14},{7,15},{8,0},{9,1},... | collective-permute-start | bytes 221192 | tf_op jit(solution)/shard_map/ppermute | solution.py:359
  140.2 0.0 collective-permute-done.7
  140.2 0.8 collective-permute-start.8
  141.0 1.7 collective-permute-done.3
  142.7 2.5 %collective-permute-start.4 = (f32[72,256]{1,0:T(8,128)S(1)}, f32[72,256]{1,0:T(8,128)S(1)}, u32[]{:S(2)}, u32[]{:S(2)}) collective-permute-start(f32[72,256]{1,0:T(8,128)S(1)} %add.40), channel_id=1, source_target_pairs={{0,1},{1,0},{2,3},{3,2},{4,5},{5,4},{6,7},{7,6},{8,9},{9,8},{10,11... | collective-permute-start | bytes 221192 | tf_op jit(solution)/shard_map/ppermute | solution.py:359
  145.2 0.0 collective-permute-done.8
  145.3 0.1 collective-permute-start.9
  145.3 0.8 collective-permute-done.4
  146.2 3.0 %collective-permute-done.9 = f32[128,256]{1,0:T(8,128)S(1)} collective-permute-done((f32[128,256]{1,0:T(8,128)S(1)}, f32[128,256]{1,0:T(8,128)S(1)}, u32[]{:S(2)}, u32[]{:S(2)}) %collective-permute-start.9) | collective-permute-done | bytes 131104 | tf_op jit(solution)/shard_map/ppermute | solution.py:359
  149.2 3.2 %collective-permute-start.10 = (f32[128,256]{1,0:T(8,128)S(1)}, f32[128,256]{1,0:T(8,128)S(1)}, u32[]{:S(2)}, u32[]{:S(2)}) collective-permute-start(f32[128,256]{1,0:T(8,128)S(1)} %add.44), channel_id=1, source_target_pairs={{0,8},{1,9},{2,10},{3,11},{4,12},{5,13},{6,14},{7,15},{8,0},{9,1},... | collective-permute-start | bytes 393224 | tf_op jit(solution)/shard_map/ppermute | solution.py:359
  152.4 8.4 %rotation.1.r_ref = f32[256,256]{1,0:T(8,128)S(1)} custom-call(f32[144,256]{1,0:T(8,128)S(1)} %pad_maximum_fusion.refs_0_), custom_call_target="tpu_custom_call" | custom-call | flops 8589934592 | bytes 524288 | tf_op jit(solution)/shard_map/rotation/pallas_call | solution.py:295
  160.8 0.0 collective-permute-done.10
  160.9 1.2 collective-permute-start.11
  162.0 6.0 %modes.1 = bf16[256,4,16,128]{3,2,1,0:T(8,128)(2,1)} custom-call(f32[256,256]{1,0:T(8,128)S(1)} %rotation.1.r_ref, bf16[2,2,8,256,256]{4,3,2,1,0:T(8,128)(2,1)S(1)} %get-tuple-element.6.refs_0_, bf16[2,2,8,256,256]{4,3,2,1,0:T(8,128)(2,1)S(1)} %get-tuple-element.7.refs_1_), custom_call_target="tpu_custom_call" | custom-call | flops 5368709120 | bytes 12582912 | tf_op jit(solution)/shard_map/modes/pallas_call | solution.py:334
  168.0 0.0 collective-permute-done.11
  168.1 0.4 fusion
  168.5 1.1 fusion.9
  (15 shorter events, 0.2 us)
Async XLA Ops:
  4.9 95.4 %copy-start.1 = (f32[16,128]{1,0:T(8,128)S(1)}, f32[16,128]{1,0:T(8,128)}, u32[]{:S(2)}) copy-start(f32[16,128]{1,0:T(8,128)} %refs_4_.3) | copy-start | bytes 24580
  4.9 85.6 %all-to-all-start = ((bf16[16,16,4,16,128]{4,3,2,1,0:T(8,128)(2,1)}), bf16[16,16,4,16,128]{4,3,2,1,0:T(8,128)(2,1)}, u32[]{:S(2)}, u32[]{:S(2)}) async-start(bf16[16,16,4,16,128]{4,3,2,1,0:T(8,128)(2,1)} %relayout.1), calls=%async_computation | async-start | bytes 8388608 | tf_op jit(solution)/shard_map/all_to_all | solution.py:385
  91.9 23.5 %collective-permute-start.5 = (bf16[16,2,4,16,128]{4,3,2,1,0:T(8,128)(2,1)S(1)}, bf16[16,2,4,16,128]{4,3,2,1,0:T(8,128)(2,1)S(1)}, u32[]{:S(2)}, u32[]{:S(2)}) collective-permute-start(bf16[16,2,4,16,128]{4,3,2,1,0:T(8,128)(2,1)S(1)} %get-tuple-element.11), channel_id=1, source_target_pairs={{0,1},{2,3},{4,5},{6,7},{8,9},{10,11},{12,13},{14,15},{1,0},{3,2},... | collective-permute-start | bytes 1572872 | tf_op jit(solution)/shard_map/ppermute | solution.py:378
  92.0 23.4 %copy-start = (f32[4,16,128]{2,1,0:T(8,128)S(1)}, f32[4,16,128]{2,1,0:T(8,128)}, u32[]{:S(2)}) copy-start(f32[4,16,128]{2,1,0:T(8,128)} %refs_5_.3) | copy-start | bytes 98308
  92.0 23.4 %collective-permute-start.6 = (bf16[16,2,4,16,128]{4,3,2,1,0:T(8,128)(2,1)S(1)}, bf16[16,2,4,16,128]{4,3,2,1,0:T(8,128)(2,1)S(1)}, u32[]{:S(2)}, u32[]{:S(2)}) collective-permute-start(bf16[16,2,4,16,128]{4,3,2,1,0:T(8,128)(2,1)S(1)} %get-tuple-element.10), channel_id=1, source_target_pairs={{1,2},{3,4},{5,6},{7,8},{9,10},{11,12},{13,14},{2,1},{4,3},{6,5},{... | collective-permute-start | bytes 1572872 | tf_op jit(solution)/shard_map/ppermute | solution.py:378
  104.8 1.3 collective-permute-start
  106.2 20.2 %collective-permute-start.1 = (f32[72,256]{1,0:T(8,128)S(1)}, f32[72,256]{1,0:T(8,128)S(1)}, u32[]{:S(2)}, u32[]{:S(2)}) collective-permute-start(f32[72,256]{1,0:T(8,128)S(1)} %select_add_fusion.1), channel_id=1, source_target_pairs={{0,2},{1,3},{2,0},{3,1},{4,6},{5,7},{6,4},{7,5},{8,10},{9,11},{10,... | collective-permute-start | bytes 221192 | tf_op jit(solution)/shard_map/ppermute | solution.py:359
  125.9 14.3 %collective-permute-start.7 = (f32[128,256]{1,0:T(8,128)S(1)}, f32[128,256]{1,0:T(8,128)S(1)}, u32[]{:S(2)}, u32[]{:S(2)}) collective-permute-start(f32[128,256]{1,0:T(8,128)S(1)} %slice_select_fusion), channel_id=1, source_target_pairs={{0,1},{1,0},{2,3},{3,2},{4,5},{5,4},{6,7},{7,6},{8,9},{9,8},{10,11... | collective-permute-start | bytes 393224 | tf_op jit(solution)/shard_map/ppermute | solution.py:359
  126.4 10.3 %collective-permute-start.2 = (f32[72,256]{1,0:T(8,128)S(1)}, f32[72,256]{1,0:T(8,128)S(1)}, u32[]{:S(2)}, u32[]{:S(2)}) collective-permute-start(f32[72,256]{1,0:T(8,128)S(1)} %add.38), channel_id=1, source_target_pairs={{0,4},{1,5},{2,6},{3,7},{4,0},{5,1},{6,2},{7,3},{8,12},{9,13},{10,... | collective-permute-start | bytes 221192 | tf_op jit(solution)/shard_map/ppermute | solution.py:359
  136.7 6.0 %collective-permute-start.3 = (f32[72,256]{1,0:T(8,128)S(1)}, f32[72,256]{1,0:T(8,128)S(1)}, u32[]{:S(2)}, u32[]{:S(2)}) collective-permute-start(f32[72,256]{1,0:T(8,128)S(1)} %add.39), channel_id=1, source_target_pairs={{0,8},{1,9},{2,10},{3,11},{4,12},{5,13},{6,14},{7,15},{8,0},{9,1},... | collective-permute-start | bytes 221192 | tf_op jit(solution)/shard_map/ppermute | solution.py:359
  140.2 5.1 %collective-permute-start.8 = (f32[128,256]{1,0:T(8,128)S(1)}, f32[128,256]{1,0:T(8,128)S(1)}, u32[]{:S(2)}, u32[]{:S(2)}) collective-permute-start(f32[128,256]{1,0:T(8,128)S(1)} %select_add_fusion), channel_id=1, source_target_pairs={{0,2},{1,3},{2,0},{3,1},{4,6},{5,7},{6,4},{7,5},{8,10},{9,11},{10,... | collective-permute-start | bytes 393224 | tf_op jit(solution)/shard_map/ppermute | solution.py:359
  142.7 3.4 %collective-permute-start.4 = (f32[72,256]{1,0:T(8,128)S(1)}, f32[72,256]{1,0:T(8,128)S(1)}, u32[]{:S(2)}, u32[]{:S(2)}) collective-permute-start(f32[72,256]{1,0:T(8,128)S(1)} %add.40), channel_id=1, source_target_pairs={{0,1},{1,0},{2,3},{3,2},{4,5},{5,4},{6,7},{7,6},{8,9},{9,8},{10,11... | collective-permute-start | bytes 221192 | tf_op jit(solution)/shard_map/ppermute | solution.py:359
  145.3 3.9 %collective-permute-start.9 = (f32[128,256]{1,0:T(8,128)S(1)}, f32[128,256]{1,0:T(8,128)S(1)}, u32[]{:S(2)}, u32[]{:S(2)}) collective-permute-start(f32[128,256]{1,0:T(8,128)S(1)} %add.43), channel_id=1, source_target_pairs={{0,4},{1,5},{2,6},{3,7},{4,0},{5,1},{6,2},{7,3},{8,12},{9,13},{10,... | collective-permute-start | bytes 393224 | tf_op jit(solution)/shard_map/ppermute | solution.py:359
  149.2 11.7 %collective-permute-start.10 = (f32[128,256]{1,0:T(8,128)S(1)}, f32[128,256]{1,0:T(8,128)S(1)}, u32[]{:S(2)}, u32[]{:S(2)}) collective-permute-start(f32[128,256]{1,0:T(8,128)S(1)} %add.44), channel_id=1, source_target_pairs={{0,8},{1,9},{2,10},{3,11},{4,12},{5,13},{6,14},{7,15},{8,0},{9,1},... | collective-permute-start | bytes 393224 | tf_op jit(solution)/shard_map/ppermute | solution.py:359
  160.9 7.2 %collective-permute-start.11 = (f32[128,256]{1,0:T(8,128)S(1)}, f32[128,256]{1,0:T(8,128)S(1)}, u32[]{:S(2)}, u32[]{:S(2)}) collective-permute-start(f32[128,256]{1,0:T(8,128)S(1)} %add.45), channel_id=1, source_target_pairs={{0,1},{1,0},{2,3},{3,2},{4,5},{5,4},{6,7},{7,6},{8,9},{9,8},{10,11... | collective-permute-start | bytes 393224 | tf_op jit(solution)/shard_map/ppermute | solution.py:359

commit v4 on v3

v4 whole, which is shorter than its diff:
```python
import functools

import jax
import jax.numpy as jnp
from jax import lax
from jax.experimental import pallas as pl
from jax.experimental.pallas import tpu as pltpu
from jax.sharding import PartitionSpec as P

VMEM_LIMIT = 24 * 1024 * 1024
NT = (((1,), (1,)), ((), ()))


def cost(flops):
    return pl.CostEstimate(flops=int(flops), bytes_accessed=1, transcendentals=0)


VMEM = pl.BlockSpec(memory_space=pltpu.VMEM)


def params():
    return pltpu.CompilerParams(vmem_limit_bytes=VMEM_LIMIT)


def split(value):
    high = value.astype(jnp.bfloat16)
    low = (value - high.astype(jnp.float32)).astype(jnp.bfloat16)
    return high, low


def matmul(a, b):
    return jnp.dot(a, b, preferred_element_type=jnp.float32)


def matmul_nt(a, b):
    return lax.dot_general(a, b, NT, preferred_element_type=jnp.float32)


def relayout_kernel(in_ref, out_ref):
    owners, rows, variables = out_ref.shape[:3]
    for owner in range(owners):
        for v in range(variables):
            block = in_ref[:, v, owner * rows : (owner + 1) * rows]
            out_ref[owner, :, v] = jnp.swapaxes(block, 0, 1)


def relayout(snapshots, owners):
    count, variables, cells, width = snapshots.shape
    rows = cells // owners
    if count % 16 or rows % 16:
        block = snapshots.reshape(count, variables, owners, rows, width)
        return block.transpose(2, 3, 1, 0, 4)
    each = owners // 2 if owners % 2 == 0 else 1
    return pl.pallas_call(
        relayout_kernel,
        grid=(owners // each,),
        in_specs=[pl.BlockSpec((count, variables, each * rows, width), lambda i: (0, 0, i, 0))],
        out_specs=pl.BlockSpec(
            (each, rows, variables, count, width), lambda i: (i, 0, 0, 0, 0)
        ),
        out_shape=jax.ShapeDtypeStruct((owners, rows, variables, count, width), snapshots.dtype),
        compiler_params=pltpu.CompilerParams(vmem_limit_bytes=60 * 1024 * 1024),
        name="relayout",
    )(snapshots)


def row_of(ref, x, v):
    value = ref[:, x, v]
    return value.reshape(value.shape[0] * value.shape[1], value.shape[2])


def pack(gram):
    half = gram.shape[0] // 2
    sub = lax.broadcasted_iota(jnp.int32, (half, half), 0)
    lane = lax.broadcasted_iota(jnp.int32, (half, half), 1)
    first, last = gram[:half, :half], gram[half:, half:]
    diagonal = jnp.sum(jnp.where(lane == sub, first, 0.0), axis=0, keepdims=True)
    mixed = jnp.where(lane > sub, first, last)
    top = jnp.concatenate([mixed, gram[:half, half:]], axis=1)
    return top, jnp.broadcast_to(jnp.concatenate([diagonal, diagonal], axis=1), (16, 2 * half))


def unpack(mixed, diagonal):
    half = mixed.shape[0]
    sub = lax.broadcasted_iota(jnp.int32, (half, half), 0)
    lane = lax.broadcasted_iota(jnp.int32, (half, half), 1)
    upper = jnp.where(lane > sub, mixed, 0.0)
    lower = jnp.where(lane < sub, mixed, 0.0)
    first = jnp.where(lane == sub, diagonal, upper + upper.T)
    last = jnp.where(lane == sub, mixed, lower + lower.T)
    return first, last


def gram_kernel(x_ref, w_ref, out_ref, keep_ref, total_ref):
    rows, each = x_ref.shape[1:3]
    size = total_ref.shape[0]

    @pl.when(pl.program_id(0) == 0)
    def _():
        total_ref[...] = jnp.zeros_like(total_ref)

    total = None
    for v in range(each):
        for first in range(0, rows, 4):
            group = range(first, first + 4)
            plain = [row_of(x_ref, x, v) for x in group]
            at = pl.program_id(0) * each + v
            for x in group:
                keep_ref[at, x] = plain[x - first]
            plain = jnp.concatenate(plain, axis=1)
            weight = jnp.concatenate([w_ref[x : x + 1, :] for x in group], axis=1)
            high, low = split(plain.astype(jnp.float32) * weight)
            term = matmul_nt(high, plain) + matmul_nt(low, plain)
            total = term if total is None else total + term
    total_ref[...] += total

    @pl.when(pl.program_id(0) == pl.num_programs(0) - 1)
    def _():
        top, diagonal = pack(total_ref[...])
        out_ref[: size // 2, :] = top
        out_ref[size // 2 :, :] = diagonal


def gram_of(block, weights):
    owners, rows, variables, count, width = block.shape
    size = owners * count
    each = 2 if variables % 2 == 0 else 1
    return pl.pallas_call(
        gram_kernel,
        grid=(variables // each,),
        in_specs=[
            pl.BlockSpec((owners, rows, each, count, width), lambda v: (0, 0, v, 0, 0)),
            pl.BlockSpec((rows, width), lambda v: (0, 0)),
        ],
        out_specs=[pl.BlockSpec((size // 2 + 16, size), lambda v: (0, 0)), VMEM],
        out_shape=[
            jax.ShapeDtypeStruct((size // 2 + 16, size), jnp.float32),
            jax.ShapeDtypeStruct((variables, rows, size, width), block.dtype),
        ],
        scratch_shapes=[pltpu.VMEM((size, size), jnp.float32)],
        compiler_params=params(),
        cost_estimate=cost(2e9),
        name="gram",
    )(block, weights)


def along_x(lower, upper, centre):
    near = [part for part in (lower[1], upper[0]) if part is not None]
    far = [part for part in (lower[0], upper[1]) if part is not None]
    value = 16.0 * sum(near[1:], near[0]) if near else jnp.zeros_like(centre)
    return value - sum(far[1:], far[0]) if far else value


def two(ref, x):
    return jnp.concatenate([ref[x : x + 1, :], ref[x + 1 : x + 2, :]], axis=1)


def stencil(value, x, pair, d_ref, band_ref):
    sides = [
        along_x((value.get(k - 2), value.get(k - 1)), (value.get(k + 1), value.get(k + 2)), value[k])
        for k in (x, x + 1)
    ]
    both = matmul(pair, band_ref[...]) + jnp.concatenate(sides, axis=1)
    return both * (two(d_ref, x) * (1.0 / 12.0))


def products(left, right):
    term = matmul_nt(jnp.concatenate(split(left), axis=0), right)
    half = term.shape[0] // 2
    return term[:half] + term[half:]


def store(f_ref, v, p, field):
    f_ref[0, v, p], f_ref[1, v, p] = split(field)


def inner_kernel(span, x_ref, w_ref, d_ref, band_ref, before_ref, cross_ref, f_ref):
    rows = x_ref.shape[1]
    cross_ref[...] = before_ref[...]
    for place, v in enumerate(span):
        plain = [x_ref[v, x] for x in range(rows)]
        value = {x: part.astype(jnp.float32) for x, part in enumerate(plain)}
        total = None
        for x in range(2, rows, 2):
            pair = jnp.concatenate(plain[x : x + 2], axis=1)
            field = stencil(value, x, pair, d_ref.at[v], band_ref)
            if x < rows - 2:
                store(f_ref, place, x // 2 - 1, field)
            term = products(field * two(w_ref, x), pair)
            total = term if total is None else total + term
        cross_ref[...] += total


def lower_kernel(odd_ref, x_ref, near_ref, far_ref, w_ref, d_ref, band_ref, before_ref, cross_ref, f_ref):
    variables, owners = x_ref.shape[0], near_ref.shape[0] - 1
    odd = odd_ref[0] == 1
    cross_ref[...] = before_ref[...]
    for v in range(variables):
        plain = {x: x_ref[v, x] for x in range(4)}
        for x in range(2):
            near, far = (row_of(ref.at[:owners], x, v) for ref in (near_ref, far_ref))
            plain[x - 2] = jnp.where(odd, near, far)
        value = {x: part.astype(jnp.float32) for x, part in plain.items()}
        pair = jnp.concatenate([plain[0], plain[1]], axis=1)
        field = stencil(value, 0, pair, d_ref.at[v], band_ref)
        store(f_ref, v, 0, field)
        total = products(field * two(w_ref, 0), pair)
        factor = []
        for x in range(2):
            near, far = (ref[owners, x, v].astype(jnp.float32) for ref in (near_ref, far_ref))
            parts = jnp.where(odd, near, far)
            factor.append(parts[0:1] + parts[1:2] + parts[2:3])
        joined = jnp.concatenate(
            [-value[0] * factor[0], (16.0 * value[0] - value[1]) * factor[1]], axis=1
        )
        total = total + products(joined, jnp.concatenate([plain[-2], plain[-1]], axis=1))
        cross_ref[...] += total


def upper_kernel(odd_ref, x_ref, near_ref, far_ref, d_ref, band_ref, f_ref):
    variables, rows = x_ref.shape[:2]
    owners = near_ref.shape[0] - 1
    odd = odd_ref[0] == 1
    for v in range(variables):
        plain = {x: x_ref[v, x] for x in range(rows - 4, rows)}
        for x in range(2):
            near, far = (row_of(ref.at[:owners], x, v) for ref in (near_ref, far_ref))
            plain[rows + x] = jnp.where(odd, far, near)
        value = {x: part.astype(jnp.float32) for x, part in plain.items()}
        pair = jnp.concatenate([plain[rows - 2], plain[rows - 1]], axis=1)
        store(f_ref, v, 0, stencil(value, rows - 2, pair, d_ref.at[v], band_ref))


def band_matrix(width):
    shape = (2, width, 2, width)
    i, y, j, z = (lax.broadcasted_iota(jnp.int32, shape, axis) for axis in range(4))
    distance = jnp.abs(y - z)
    line = jnp.where(
        distance == 0, -60.0, jnp.where(distance == 1, 16.0, jnp.where(distance == 2, -1.0, 0.0))
    )
    return jnp.where(i == j, line, 0.0).reshape(2 * width, 2 * width).astype(jnp.bfloat16)


COST = {"inner": 1, "lower": 1, "upper": 1}


def stencil_call(kernel, name, block, span, pairs, cross, *operands, odd=None):
    _, _, size, width = block.shape
    field = jax.ShapeDtypeStruct((2, span, pairs, size, 2 * width), jnp.bfloat16)
    total = jax.ShapeDtypeStruct((size, size), jnp.float32)
    flags = [] if odd is None else [odd]
    return pl.pallas_call(
        kernel,
        in_specs=[pl.BlockSpec(memory_space=pltpu.SMEM)] * len(flags) + [VMEM] * (1 + len(operands)),
        out_specs=[VMEM, VMEM] if cross else VMEM,
        out_shape=[total, field] if cross else field,
        compiler_params=params(),
        cost_estimate=cost(COST[name]),
        name=name,
    )(*flags, block, *operands)


PANEL = 32
GROUP = 8


def lanes(value, width):
    return jnp.concatenate([value] * (width // value.shape[1]), axis=1)


def sublanes(value, height):
    return jnp.concatenate([value] * (height // value.shape[0]), axis=0)


def split3(value):
    high = value.astype(jnp.bfloat16)
    rest = value - high.astype(jnp.float32)
    middle = rest.astype(jnp.bfloat16)
    return high, middle, (rest - middle.astype(jnp.float32)).astype(jnp.bfloat16)


def eliminate(panel, start, at):
    height, size = panel.shape
    first = start + at
    sub = lax.broadcasted_iota(jnp.int32, (height, size), 0)
    lane = lax.broadcasted_iota(jnp.int32, (height, size), 1)
    sub1 = lax.broadcasted_iota(jnp.int32, (height, 128), 0)
    lane8 = lax.broadcasted_iota(jnp.int32, (8, size), 1)
    span = range(GROUP)
    columns = [jnp.broadcast_to(panel[:, first + i : first + i + 1], (height, 128)) for i in span]
    rows = [jnp.broadcast_to(panel[at + i : at + i + 1, :], (8, size)) for i in span]
    entry = {
        (i, k): jnp.broadcast_to(columns[k][at + i : at + i + 1, :], (8, 128))
        for i in span
        for k in range(i, GROUP)
    }
    inverse = []
    for i in span:
        inverse.append(1.0 / entry[i, i])
        rows[i] = jnp.where(lane8 == first + i, 1.0, rows[i])
        for k in range(i + 1, GROUP):
            factor = entry[i, k] * inverse[i]
            rows[k] = jnp.where(lane8 == first + i, 0.0, rows[k]) - lanes(factor, size) * rows[i]
            columns[k] = columns[k] - sublanes(factor, height) * columns[i]
            for j in range(i + 1, k + 1):
                entry[j, k] = entry[j, k] - factor * entry[i, j]
    rows = [
        jnp.where((lane8 > first + i) & (lane8 < first + GROUP), 0.0, rows[i]) for i in span
    ]
    done = at + GROUP
    result = jnp.where((lane >= first) & (lane < first + GROUP) & (sub >= done), 0.0, panel)
    for i in span:
        factor = jnp.where(sub1 >= done, columns[i] * sublanes(inverse[i], height), 0.0)
        result = result - lanes(factor, size) * sublanes(rows[i], height)
    for i in span:
        result = jnp.where(sub == at + i, sublanes(rows[i], height), result)
    return result, [entry[i, i] for i in span]


def rotation_panels(begin, stop, out_ref, work_ref):
    size = work_ref.shape[0]
    sub = lax.broadcasted_iota(jnp.int32, (PANEL, size), 0)
    lane = lax.broadcasted_iota(jnp.int32, (PANEL, size), 1)
    sub1 = lax.broadcasted_iota(jnp.int32, (PANEL, 128), 0)
    for start in range(begin, stop, PANEL):
        end = start + PANEL
        panel = work_ref[start:end, :]
        norm = jnp.zeros((PANEL, 128), jnp.float32)
        for at in range(0, PANEL, GROUP):
            panel, pivots = eliminate(panel, start, at)
            for i, pivot in enumerate(pivots):
                norm = jnp.where(sub1 == at + i, sublanes(lax.rsqrt(pivot), PANEL), norm)
        panel = panel * lanes(norm, size)
        panel = jnp.where((lane > start + sub) & (lane < end), 0.0, panel)
        out_ref[start:end, :] = jnp.where(lane < end, panel, 0.0)
        if end < size:
            high, middle, low = split3(panel)
            right = jnp.concatenate([high, middle, low, high, middle, high], axis=0)
            left = jnp.concatenate(
                [part[:, end:] for part in (high, high, high, middle, middle, low)], axis=0
            )
            update = lax.dot_general(
                left, right, (((0,), (0,)), ((), ())), preferred_element_type=jnp.float32
            )
            rest = work_ref[end:, :]
            place = lax.broadcasted_iota(jnp.int32, rest.shape, 1)
            work_ref[end:, :] = jnp.where((place >= start) & (place < end), 0.0, rest) - update


def rotation_first_kernel(scale, gram_ref, out_ref, work_ref):
    size = work_ref.shape[0]
    half = size // 2
    first, last = unpack(gram_ref[:half, :half] * scale, gram_ref[half : half + 1, :half] * scale)
    work_ref[:half, :half] = first
    work_ref[half:, half:] = last
    work_ref[:half, half:] = gram_ref[:half, half:] * scale
    work_ref[half:, :half] = jnp.zeros((half, half), jnp.float32)
    rotation_panels(0, half, out_ref, work_ref)


def rotation_last_kernel(before_ref, state_ref, out_ref, work_ref):
    size = work_ref.shape[0]
    half = size // 2
    out_ref[:half, :] = before_ref[...]
    work_ref[half:, :] = state_ref[half:, :]
    rotation_panels(half, size, out_ref, work_ref)


def rotation_first(packed, cell_count):
    size = packed.shape[1]
    return pl.pallas_call(
        lambda *refs: rotation_first_kernel(1.0 / cell_count, *refs),
        in_specs=[VMEM],
        out_specs=[VMEM, VMEM],
        out_shape=[
            jax.ShapeDtypeStruct((size // 2, size), jnp.float32),
            jax.ShapeDtypeStruct((size, size), jnp.float32),
        ],
        compiler_params=params(),
        cost_estimate=cost(1),
        name="rotation_first",
    )(packed)


def rotation_last(before, state):
    size = state.shape[0]
    return pl.pallas_call(
        rotation_last_kernel,
        in_specs=[VMEM, VMEM],
        out_specs=VMEM,
        out_shape=jax.ShapeDtypeStruct((size, size), jnp.float32),
        scratch_shapes=[pltpu.VMEM((size, size), jnp.float32)],
        compiler_params=params(),
        cost_estimate=cost(1),
        name="rotation_last",
    )(before, state)


def modes_kernel(first, r_ref, low_ref, mid_ref, top_ref, *refs):
    out_ref = refs[-1]
    high, low = split(r_ref[...])
    v = pl.program_id(0)
    width = mid_ref.shape[4] // 2
    places = [(low_ref, first + v, 0)]
    places += [(mid_ref, v, p) for p in range(mid_ref.shape[2])]
    places += [(top_ref, first + v, 0)]
    rows = []
    for ref, at, p in places:
        large, small = ref[0, at, p], ref[1, at, p]
        value = matmul(high, large) + matmul(high, small) + matmul(low, large)
        value = value.astype(out_ref.dtype)
        rows += [value[:, :width], value[:, width:]]
    out_ref[:, 0] = jnp.swapaxes(jnp.stack(rows, axis=0), 0, 1)


def modes_of(rotation, low, mid, top, first, before):
    variables, (_, span, pairs, size, width) = low.shape[1], mid.shape
    rows, width = 2 * pairs + 4, width // 2
    earlier = [] if before is None else [before]
    return pl.pallas_call(
        lambda *refs: modes_kernel(first, *refs),
        grid=(span,),
        in_specs=[pl.BlockSpec((size, size), lambda v: (0, 0))]
        + [VMEM] * 3
        + [pl.BlockSpec(memory_space=pl.ANY)] * len(earlier),
        out_specs=pl.BlockSpec((size, 1, rows, width), lambda v: (0, first + v, 0, 0)),
        out_shape=jax.ShapeDtypeStruct((size, variables, rows, width), jnp.bfloat16),
        input_output_aliases={4: 0} if earlier else {},
        compiler_params=params(),
        cost_estimate=cost(1 if before is None else 10 * size * size * rows * span * width),
        name="modes",
    )(rotation, low, mid, top, *earlier)


class Sum:
    def __init__(self, value, axis):
        self.axis, self.count = axis, lax.axis_size(axis)
        self.butterfly = self.count >= 2 and not self.count & (self.count - 1)
        if not self.butterfly:
            self.own = value
            return
        half = value.shape[0] // 2
        self.odd = lax.axis_index(axis) % 2 == 1
        first, second = value[:half], value[half:]
        self.own = jnp.where(self.odd, second, first) + self.swap(
            jnp.where(self.odd, first, second), 1
        )

    def swap(self, part, step):
        return lax.ppermute(part, self.axis, [(i, i ^ step) for i in range(self.count)])

    def steps(self):
        return [1 << k for k in range(1, self.count.bit_length() - 1)] if self.butterfly else []

    def add(self, step):
        self.own = self.own + self.swap(self.own, step)

    def result(self):
        if not self.butterfly:
            return lax.psum(self.own, self.axis)
        other = self.swap(self.own, 1)
        low, high = jnp.where(self.odd, other, self.own), jnp.where(self.odd, self.own, other)
        return jnp.concatenate([low, high], axis=0)


def shifted(value, axis, step):
    count = lax.axis_size(axis)
    pairs = [(i, i + step) for i in range(count) if 0 <= i + step < count]
    return lax.ppermute(value, axis, pairs)


def swapped(block, weights, diffusivity, axis):
    devices = lax.axis_size(axis)
    _, rows, variables, count, width = block.shape
    odd = lax.axis_index(axis) % 2 == 1
    factor = weights[None, rows - 2 :] * (diffusivity[:, rows - 2 :] * (1.0 / 12.0))
    top = lax.reduce_precision(factor, 8, 7)
    middle = lax.reduce_precision(factor - top, 8, 7)
    parts = jnp.stack([top, middle, factor - top - middle], axis=2).astype(block.dtype)
    parts = parts.transpose(1, 0, 2, 3)
    parts = jnp.pad(parts, ((0, 0), (0, 0), (0, count - 3), (0, 0)))[None]
    sent = [
        jnp.concatenate([lax.dynamic_slice_in_dim(block, start, 2, axis=1), parts], axis=0)
        for start in (jnp.where(odd, 0, rows - 2), jnp.where(odd, rows - 2, 0))
    ]
    *sent, block = lax.optimization_barrier((*sent, block))
    received = []
    for first, part in enumerate(sent):
        pairs = [(i, i + 1) for i in range(first, devices - 1, 2)]
        received.append(lax.ppermute(part, axis, pairs + [(b, a) for a, b in pairs]))
    return block, received


def on_device(snapshots, cell_weights, diffusivity):
    highest = lax.Precision.HIGHEST
    together = lax.optimization_barrier
    owners = lax.axis_size("gx")
    block = lax.all_to_all(relayout(snapshots, owners), "gx", 0, 0, tiled=True)
    if snapshots.shape[0] % 16:
        count, rows, variables, each, width = block.shape
        block = block.transpose(1, 2, 0, 3, 4).reshape(1, rows, variables, count * each, width)
    _, rows, variables, count, width = block.shape
    size, cell_count = block.shape[0] * count, rows * variables * width * owners
    band = band_matrix(width)
    half = variables // 2
    spans = [span for span in (range(half), range(half, variables)) if len(span)]

    odd = (lax.axis_index("gx") % 2).astype(jnp.int32).reshape(1)
    block, (near, far) = swapped(block, cell_weights, diffusivity, "gx")
    block, near = together((block, near))
    packed, kept = gram_of(block, cell_weights)
    cross = jnp.zeros((size, size), jnp.float32)
    mids = []

    def inner(span, kept, cross):
        cross, mid = stencil_call(
            functools.partial(inner_kernel, span), "inner", kept, len(span), rows // 2 - 2, True,
            cell_weights, diffusivity, band, cross,
        )
        mids.append(mid)
        return cross

    gram = Sum(packed, "gx")
    steps = gram.steps()
    kept, gram.own = together((kept, gram.own))
    for span in spans:
        cross = inner(span, kept, cross)
    cross, bottom = stencil_call(
        lower_kernel, "lower", kept, variables, 1, True,
        near, far, cell_weights, diffusivity, band, cross, odd=odd,
    )
    if steps:
        gram.add(steps.pop(0))
    cross, gram.own = together((cross, gram.own))
    cross = Sum(cross, "gx")
    while steps:
        gram.add(steps.pop(0))
    steps = cross.steps()
    if steps:
        cross.add(steps.pop(0))
    top = stencil_call(
        upper_kernel, "upper", kept, variables, 1, False, near, far, diffusivity, band, odd=odd
    )
    gram.own, cross.own, top = together((gram.own, cross.own, top))
    state = rotation_first(gram.result(), cell_count)
    if steps:
        cross.add(steps.pop(0))
    state, cross.own = together((state, cross.own))
    rotation = rotation_last(*state)
    while steps:
        cross.add(steps.pop(0))
    modes = None
    for span, mid in zip(spans, mids):
        if modes is not None:
            modes, cross.own = together((modes, cross.own))
        modes = modes_of(rotation, bottom, mid, top, span[0], modes)
    cross_total = cross.result() * (1.0 / cell_count)
    reduced = jnp.dot(
        jnp.dot(rotation, cross_total.T, precision=highest), rotation.T, precision=highest
    )
    return (modes, reduced)


def solution(mesh):
    in_specs = (
        P("gx", None, "groups", None),
        P(("groups", "gx"), None),
        P(None, ("groups", "gx"), None),
    )
    out_specs = (P(None, None, ("groups", "gx"), None), P("groups", None))
    return jax.shard_map(
        on_device, mesh=mesh, in_specs=in_specs, out_specs=out_specs, check_vma=False
    )
```

time: 170 us -> 158 us (0.929)
  starting transfers between devices: 45 us -> 39.5 us
  waiting for transfers between devices: 86.8 us -> 82.1 us
  Pallas kernels: 33.6 us -> 31.9 us
    ppermute x12, starting transfers between devices: 37.5 us -> 32 us  [the longest x10 23.7 us: swap(): lax.ppermute(part, self.axis, [(i, i ^ step) for i in range(self.count)])]
    ppermute x12, waiting for transfers between devices: 8.73 us -> 4.13 us  [the longest x10 4.12 us: swap(): lax.ppermute(part, self.axis, [(i, i ^ step) for i in range(self.count)])]
    pallas_call x4 -> x8, Pallas kernels: 24.8 us -> 23 us  [the longest x4 7.48 us: stencil_call(): pl.pallas_call(kernel, in_specs=[pl.BlockSpec(memory_space=pltpu.SMEM)] *...]
  transfers between devices with their start and end apart: 13 -> 13, of which waited for: 6 -> 4; matrix products, arithmetic and copies ran while one was open for 0% -> 0% of each run, Pallas kernels for 17% -> 18%
where the time goes in v4:
time: 158 us
  waiting for transfers between devices  82.1 us (52%)
  starting transfers between devices  39.5 us (25%)
  Pallas kernels  31.9 us (20%)
    all_to_all x1, waiting for transfers between devices, on_device(): block = lax.all_to_all(relayout(snapshots, owners), 'gx', 0, 0, tiled=True)  78 us
    ppermute x10, starting transfers between devices, swap(): lax.ppermute(part, self.axis, [(i, i ^ step) for i in range(self.count)])  23.7 us
    ppermute x2, starting transfers between devices, swapped(): lax.ppermute(part, axis, pairs + [(b, a) for a, b in pairs])  8.25 us
    pallas_call x4, Pallas kernels, stencil_call(): pl.pallas_call(kernel, in_specs=[pl.BlockSpec(memory_space=pltpu.SMEM)] *...  7.48 us
    all_to_all x1, starting transfers between devices, on_device(): block = lax.all_to_all(relayout(snapshots, owners), 'gx', 0, 0, tiled=True)  7.48 us
    pallas_call x2, Pallas kernels, modes_of(): pl.pallas_call(lambda *refs: modes_kernel(first, *refs), grid=(span,), in...  6.81 us
    pallas_call x1, Pallas kernels, gram_of(): pl.pallas_call(gram_kernel, grid=(variables // each,), in_specs=[pl.Block...  4.71 us
    pallas_call x1, Pallas kernels, rotation_first(): pl.pallas_call(lambda *refs: rotation_first_kernel(1.0 / cell_count, *ref...  4.39 us
  transfers between devices with their start and end apart: 13, of which 4 were waited for; matrix products, arithmetic and copies ran while one was open for 0% of the time, Pallas kernels for 18%

profile of v4, /device:TPU:1, one launch (start us, length us, event | category | flops | bytes accessed | tf_op | source)
XLA Modules:
  0.0 157.9 jit_solution(13183927398110279539)
XLA Ops:
  0.6 4.3 %relayout.1 = bf16[16,16,4,16,128]{4,3,2,1,0:T(8,128)(2,1)} custom-call(bf16[16,4,256,128]{3,2,1,0:T(8,128)(2,1)} %in_ref.1), custom_call_target="tpu_custom_call" | custom-call | tf_op jit(solution)/shard_map/relayout/pallas_call | solution.py:54
  4.9 0.0 copy-start.1
  4.9 0.0 copy-start
  4.9 7.5 %all-to-all-start = ((bf16[16,16,4,16,128]{4,3,2,1,0:T(8,128)(2,1)}), bf16[16,16,4,16,128]{4,3,2,1,0:T(8,128)(2,1)}, u32[]{:S(2)}, u32[]{:S(2)}) async-start(bf16[16,16,4,16,128]{4,3,2,1,0:T(8,128)(2,1)} %relayout.1), calls=%async_computation | async-start | bytes 8388608 | tf_op jit(solution)/shard_map/all_to_all | solution.py:498
  12.4 0.0 copy-done.1
  12.4 0.0 copy-done
  12.5 78.0 %all-to-all-done.x_ref = bf16[16,16,4,16,128]{4,3,2,1,0:T(8,128)(2,1)} async-done(((bf16[16,16,4,16,128]{4,3,2,1,0:T(8,128)(2,1)}), bf16[16,16,4,16,128]{4,3,2,1,0:T(8,128)(2,1)}, u32[]{:S(2)}, u32[]{:S(2)}) %all-to-all-start) | async-done | bytes 4194336 | tf_op jit(solution)/shard_map/all_to_all | solution.py:498
  90.5 1.4 constant_dynamic-slice_fusion
  91.9 0.1 pad_maximum_fusion
  92.0 0.1 collective-permute-start
  92.1 8.2 %collective-permute-start.2 = (bf16[17,2,4,16,128]{4,3,2,1,0:T(8,128)(2,1)S(1)}, bf16[17,2,4,16,128]{4,3,2,1,0:T(8,128)(2,1)S(1)}, u32[]{:S(2)}, u32[]{:S(2)}) collective-permute-start(bf16[17,2,4,16,128]{4,3,2,1,0:T(8,128)(2,1)S(1)} %get-tuple-element.36), channel_id=1, source_target_pairs={{1,2},{3,4},{5,6},{7,8},{9,10},{11,12},{13,14},{2,1},{4,3},{6,5},{... | collective-permute-start | bytes 1671176 | tf_op jit(solution)/shard_map/ppermute | solution.py:490
  100.3 0.0 collective-permute-done.near_ref
  100.3 4.7 %gram.1 = (f32[144,256]{1,0:T(8,128)S(1)}, bf16[4,16,256,128]{3,2,1,0:T(8,128)(2,1)S(1)}) custom-call(bf16[16,16,4,16,128]{4,3,2,1,0:T(8,128)(2,1)} %all-to-all-done.x_ref, f32[16,128]{1,0:T(8,128)S(1)} %copy-done.1), custom_call_target="tpu_custom_call" | custom-call | flops 2000000000 | bytes 1 | tf_op jit(solution)/shard_map/gram/pallas_call | solution.py:128
  105.0 0.1 collective-permute-start.1
  105.1 1.2 collective-permute-done.1
  106.4 9.3 %collective-permute-start.3 = (f32[72,256]{1,0:T(8,128)S(1)}, f32[72,256]{1,0:T(8,128)S(1)}, u32[]{:S(2)}, u32[]{:S(2)}) collective-permute-start(f32[72,256]{1,0:T(8,128)S(1)} %select_add_fusion.1), channel_id=1, source_target_pairs={{0,2},{1,3},{2,0},{3,1},{4,6},{5,7},{6,4},{7,5},{8,10},{9,11},{10,... | collective-permute-start | bytes 221192 | tf_op jit(solution)/shard_map/ppermute | solution.py:450
  115.7 0.2 select_convert_fusion.band_ref
  115.9 2.7 %inner.2 = (f32[256,256]{1,0:T(8,128)S(1)}, bf16[2,2,6,256,256]{4,3,2,1,0:T(8,128)(2,1)S(1)}) custom-call(bf16[4,16,256,128]{3,2,1,0:T(8,128)(2,1)S(1)} %get-tuple-element.34.x_ref, f32[16,128]{1,0:T(8,128)S(1)} %copy-done.1, f32[4,16,128]{2,1,0:T(8,128)S(1)} %copy-done, bf16[256,256]{1,0:T(8,128)(2,1)S(1)} %select_convert_fusion.band_ref, ...), custom_call_target="tpu_custom_call" | custom-call | flops 1 | bytes 1 | tf_op jit(solution)/shard_map/inner/pallas_call | solution.py:252
  118.6 2.7 %inner.3 = (f32[256,256]{1,0:T(8,128)S(1)}, bf16[2,2,6,256,256]{4,3,2,1,0:T(8,128)(2,1)S(1)}) custom-call(bf16[4,16,256,128]{3,2,1,0:T(8,128)(2,1)S(1)} %get-tuple-element.34.x_ref, f32[16,128]{1,0:T(8,128)S(1)} %copy-done.1, f32[4,16,128]{2,1,0:T(8,128)S(1)} %copy-done, bf16[256,256]{1,0:T(8,128)(2,1)S(1)} %select_convert_fusion.band_ref, ...), custom_call_target="tpu_custom_call" | custom-call | flops 1 | bytes 1 | tf_op jit(solution)/shard_map/inner/pallas_call | solution.py:252
  121.3 0.0 collective-permute-done.2.far_ref
  121.3 1.5 lower.1
  122.8 0.0 collective-permute-done.3
  122.9 0.5 collective-permute-start.6
  123.4 3.1 %collective-permute-start.4 = (f32[72,256]{1,0:T(8,128)S(1)}, f32[72,256]{1,0:T(8,128)S(1)}, u32[]{:S(2)}, u32[]{:S(2)}) collective-permute-start(f32[72,256]{1,0:T(8,128)S(1)} %add.37), channel_id=1, source_target_pairs={{0,4},{1,5},{2,6},{3,7},{4,0},{5,1},{6,2},{7,3},{8,12},{9,13},{10,... | collective-permute-start | bytes 221192 | tf_op jit(solution)/shard_map/ppermute | solution.py:450
  126.4 0.0 collective-permute-done.6
  126.5 2.4 %collective-permute-start.7 = (f32[128,256]{1,0:T(8,128)S(1)}, f32[128,256]{1,0:T(8,128)S(1)}, u32[]{:S(2)}, u32[]{:S(2)}) collective-permute-start(f32[128,256]{1,0:T(8,128)S(1)} %select_add_fusion), channel_id=1, source_target_pairs={{0,2},{1,3},{2,0},{3,1},{4,6},{5,7},{6,4},{7,5},{8,10},{9,11},{10,... | collective-permute-start | bytes 393224 | tf_op jit(solution)/shard_map/ppermute | solution.py:450
  128.9 0.0 collective-permute-done.4
  128.9 3.0 %collective-permute-start.5 = (f32[72,256]{1,0:T(8,128)S(1)}, f32[72,256]{1,0:T(8,128)S(1)}, u32[]{:S(2)}, u32[]{:S(2)}) collective-permute-start(f32[72,256]{1,0:T(8,128)S(1)} %add.38), channel_id=1, source_target_pairs={{0,8},{1,9},{2,10},{3,11},{4,12},{5,13},{6,14},{7,15},{8,0},{9,1},... | collective-permute-start | bytes 221192 | tf_op jit(solution)/shard_map/ppermute | solution.py:450
  131.9 0.6 upper.1.refs_3_
  132.5 1.9 %collective-permute-done.5 = f32[72,256]{1,0:T(8,128)S(1)} collective-permute-done((f32[72,256]{1,0:T(8,128)S(1)}, f32[72,256]{1,0:T(8,128)S(1)}, u32[]{:S(2)}, u32[]{:S(2)}) %collective-permute-start.5) | collective-permute-done | bytes 73760 | tf_op jit(solution)/shard_map/ppermute | solution.py:450
  134.5 0.0 collective-permute-done.7
  134.5 2.5 %collective-permute-start.8 = (f32[72,256]{1,0:T(8,128)S(1)}, f32[72,256]{1,0:T(8,128)S(1)}, u32[]{:S(2)}, u32[]{:S(2)}) collective-permute-start(f32[72,256]{1,0:T(8,128)S(1)} %add.39), channel_id=1, source_target_pairs={{0,1},{1,0},{2,3},{3,2},{4,5},{5,4},{6,7},{7,6},{8,9},{9,8},{10,11... | collective-permute-start | bytes 221192 | tf_op jit(solution)/shard_map/ppermute | solution.py:450
  137.0 0.0 collective-permute-start.9
  137.0 0.9 collective-permute-done.8
  138.0 4.4 %rotation_first.1 = (f32[128,256]{1,0:T(8,128)S(1)}, f32[256,256]{1,0:T(8,128)S(1)}) custom-call(f32[144,256]{1,0:T(8,128)S(1)} %pad_maximum_fusion.2.refs_0_), custom_call_target="tpu_custom_call" | custom-call | flops 1 | bytes 1 | tf_op jit(solution)/shard_map/rotation_first/pallas_call | solution.py:371
  142.4 0.0 collective-permute-done.9
  142.4 1.9 %collective-permute-start.10 = (f32[128,256]{1,0:T(8,128)S(1)}, f32[128,256]{1,0:T(8,128)S(1)}, u32[]{:S(2)}, u32[]{:S(2)}) collective-permute-start(f32[128,256]{1,0:T(8,128)S(1)} %add.42), channel_id=1, source_target_pairs={{0,8},{1,9},{2,10},{3,11},{4,12},{5,13},{6,14},{7,15},{8,0},{9,1},... | collective-permute-start | bytes 393224 | tf_op jit(solution)/shard_map/ppermute | solution.py:450
  144.3 4.3 %rotation_last.1.refs_0_ = f32[256,256]{1,0:T(8,128)S(1)} custom-call(f32[128,256]{1,0:T(8,128)S(1)} %get-tuple-element.47.before_ref, f32[256,256]{1,0:T(8,128)S(1)} %get-tuple-element.48.state_ref), custom_call_target="tpu_custom_call" | custom-call | flops 1 | bytes 1 | tf_op jit(solution)/shard_map/rotation_last/pallas_call | solution.py:387
  148.6 3.4 %modes.2.refs_4_ = bf16[256,4,16,128]{3,2,1,0:T(8,128)(2,1)} custom-call(f32[256,256]{1,0:T(8,128)S(1)} %rotation_last.1.refs_0_, bf16[2,4,1,256,256]{4,3,2,1,0:T(8,128)(2,1)S(1)} %get-tuple-element.49.refs_1_, bf16[2,2,6,256,256]{4,3,2,1,0:T(8,128)(2,1)S(1)} %get-tuple-element.52.refs_2_, bf16[2,4,1,256,256]{4,3,2,1,0:T(8,128)(2,1)S(1)} %upper.1.refs_3_), custom_call_target="tpu_custom_call" | custom-call | flops 1 | bytes 1 | tf_op jit(solution)/shard_map/modes/pallas_call | solution.py:420
  152.0 0.0 collective-permute-done.10
  152.0 0.9 collective-permute-start.11
  152.9 3.4 %modes.3 = bf16[256,4,16,128]{3,2,1,0:T(8,128)(2,1)} custom-call(f32[256,256]{1,0:T(8,128)S(1)} %rotation_last.1.refs_0_, bf16[2,4,1,256,256]{4,3,2,1,0:T(8,128)(2,1)S(1)} %get-tuple-element.49.refs_1_, bf16[2,2,6,256,256]{4,3,2,1,0:T(8,128)(2,1)S(1)} %get-tuple-element.50.refs_2_, ...), custom_call_target="tpu_custom_call", output_to_operand_aliasing={{}: (4, {})} | custom-call | flops 2684354560 | bytes 1 | tf_op jit(solution)/shard_map/modes/pallas_call | solution.py:420
  156.3 0.0 collective-permute-done.11
  156.4 0.4 fusion
  156.8 1.1 fusion.13
  (22 shorter events, 0.3 us)
Async XLA Ops:
  4.9 7.5 %copy-start.1 = (f32[16,128]{1,0:T(8,128)S(1)}, f32[16,128]{1,0:T(8,128)}, u32[]{:S(2)}) copy-start(f32[16,128]{1,0:T(8,128)} %w_ref.7) | copy-start | bytes 24580
  4.9 7.5 %copy-start = (f32[4,16,128]{2,1,0:T(8,128)S(1)}, f32[4,16,128]{2,1,0:T(8,128)}, u32[]{:S(2)}) copy-start(f32[4,16,128]{2,1,0:T(8,128)} %d_ref.7) | copy-start | bytes 98308
  4.9 85.6 %all-to-all-start = ((bf16[16,16,4,16,128]{4,3,2,1,0:T(8,128)(2,1)}), bf16[16,16,4,16,128]{4,3,2,1,0:T(8,128)(2,1)}, u32[]{:S(2)}, u32[]{:S(2)}) async-start(bf16[16,16,4,16,128]{4,3,2,1,0:T(8,128)(2,1)} %relayout.1), calls=%async_computation | async-start | bytes 8388608 | tf_op jit(solution)/shard_map/all_to_all | solution.py:498
  92.0 8.3 %collective-permute-start = (bf16[17,2,4,16,128]{4,3,2,1,0:T(8,128)(2,1)S(1)}, bf16[17,2,4,16,128]{4,3,2,1,0:T(8,128)(2,1)S(1)}, u32[]{:S(2)}, u32[]{:S(2)}) collective-permute-start(bf16[17,2,4,16,128]{4,3,2,1,0:T(8,128)(2,1)S(1)} %get-tuple-element.30), channel_id=1, source_target_pairs={{0,1},{2,3},{4,5},{6,7},{8,9},{10,11},{12,13},{14,15},{1,0},{3,2},... | collective-permute-start | bytes 1671176 | tf_op jit(solution)/shard_map/ppermute | solution.py:490
  92.1 29.2 %collective-permute-start.2 = (bf16[17,2,4,16,128]{4,3,2,1,0:T(8,128)(2,1)S(1)}, bf16[17,2,4,16,128]{4,3,2,1,0:T(8,128)(2,1)S(1)}, u32[]{:S(2)}, u32[]{:S(2)}) collective-permute-start(bf16[17,2,4,16,128]{4,3,2,1,0:T(8,128)(2,1)S(1)} %get-tuple-element.36), channel_id=1, source_target_pairs={{1,2},{3,4},{5,6},{7,8},{9,10},{11,12},{13,14},{2,1},{4,3},{6,5},{... | collective-permute-start | bytes 1671176 | tf_op jit(solution)/shard_map/ppermute | solution.py:490
  105.0 1.3 collective-permute-start.1
  106.4 16.5 %collective-permute-start.3 = (f32[72,256]{1,0:T(8,128)S(1)}, f32[72,256]{1,0:T(8,128)S(1)}, u32[]{:S(2)}, u32[]{:S(2)}) collective-permute-start(f32[72,256]{1,0:T(8,128)S(1)} %select_add_fusion.1), channel_id=1, source_target_pairs={{0,2},{1,3},{2,0},{3,1},{4,6},{5,7},{6,4},{7,5},{8,10},{9,11},{10,... | collective-permute-start | bytes 221192 | tf_op jit(solution)/shard_map/ppermute | solution.py:450
  122.9 3.6 %collective-permute-start.6 = (f32[128,256]{1,0:T(8,128)S(1)}, f32[128,256]{1,0:T(8,128)S(1)}, u32[]{:S(2)}, u32[]{:S(2)}) collective-permute-start(f32[128,256]{1,0:T(8,128)S(1)} %slice_select_fusion), channel_id=1, source_target_pairs={{0,1},{1,0},{2,3},{3,2},{4,5},{5,4},{6,7},{7,6},{8,9},{9,8},{10,11... | collective-permute-start | bytes 393224 | tf_op jit(solution)/shard_map/ppermute | solution.py:450
  123.4 5.5 %collective-permute-start.4 = (f32[72,256]{1,0:T(8,128)S(1)}, f32[72,256]{1,0:T(8,128)S(1)}, u32[]{:S(2)}, u32[]{:S(2)}) collective-permute-start(f32[72,256]{1,0:T(8,128)S(1)} %add.37), channel_id=1, source_target_pairs={{0,4},{1,5},{2,6},{3,7},{4,0},{5,1},{6,2},{7,3},{8,12},{9,13},{10,... | collective-permute-start | bytes 221192 | tf_op jit(solution)/shard_map/ppermute | solution.py:450
  126.5 8.0 %collective-permute-start.7 = (f32[128,256]{1,0:T(8,128)S(1)}, f32[128,256]{1,0:T(8,128)S(1)}, u32[]{:S(2)}, u32[]{:S(2)}) collective-permute-start(f32[128,256]{1,0:T(8,128)S(1)} %select_add_fusion), channel_id=1, source_target_pairs={{0,2},{1,3},{2,0},{3,1},{4,6},{5,7},{6,4},{7,5},{8,10},{9,11},{10,... | collective-permute-start | bytes 393224 | tf_op jit(solution)/shard_map/ppermute | solution.py:450
  128.9 5.5 %collective-permute-start.5 = (f32[72,256]{1,0:T(8,128)S(1)}, f32[72,256]{1,0:T(8,128)S(1)}, u32[]{:S(2)}, u32[]{:S(2)}) collective-permute-start(f32[72,256]{1,0:T(8,128)S(1)} %add.38), channel_id=1, source_target_pairs={{0,8},{1,9},{2,10},{3,11},{4,12},{5,13},{6,14},{7,15},{8,0},{9,1},... | collective-permute-start | bytes 221192 | tf_op jit(solution)/shard_map/ppermute | solution.py:450
  134.5 3.4 %collective-permute-start.8 = (f32[72,256]{1,0:T(8,128)S(1)}, f32[72,256]{1,0:T(8,128)S(1)}, u32[]{:S(2)}, u32[]{:S(2)}) collective-permute-start(f32[72,256]{1,0:T(8,128)S(1)} %add.39), channel_id=1, source_target_pairs={{0,1},{1,0},{2,3},{3,2},{4,5},{5,4},{6,7},{7,6},{8,9},{9,8},{10,11... | collective-permute-start | bytes 221192 | tf_op jit(solution)/shard_map/ppermute | solution.py:450
  137.0 5.3 %collective-permute-start.9 = (f32[128,256]{1,0:T(8,128)S(1)}, f32[128,256]{1,0:T(8,128)S(1)}, u32[]{:S(2)}, u32[]{:S(2)}) collective-permute-start(f32[128,256]{1,0:T(8,128)S(1)} %add.41), channel_id=1, source_target_pairs={{0,4},{1,5},{2,6},{3,7},{4,0},{5,1},{6,2},{7,3},{8,12},{9,13},{10,... | collective-permute-start | bytes 393224 | tf_op jit(solution)/shard_map/ppermute | solution.py:450
  142.4 9.6 %collective-permute-start.10 = (f32[128,256]{1,0:T(8,128)S(1)}, f32[128,256]{1,0:T(8,128)S(1)}, u32[]{:S(2)}, u32[]{:S(2)}) collective-permute-start(f32[128,256]{1,0:T(8,128)S(1)} %add.42), channel_id=1, source_target_pairs={{0,8},{1,9},{2,10},{3,11},{4,12},{5,13},{6,14},{7,15},{8,0},{9,1},... | collective-permute-start | bytes 393224 | tf_op jit(solution)/shard_map/ppermute | solution.py:450
  152.0 4.3 %collective-permute-start.11 = (f32[128,256]{1,0:T(8,128)S(1)}, f32[128,256]{1,0:T(8,128)S(1)}, u32[]{:S(2)}, u32[]{:S(2)}) collective-permute-start(f32[128,256]{1,0:T(8,128)S(1)} %add.43), channel_id=1, source_target_pairs={{0,1},{1,0},{2,3},{3,2},{4,5},{5,4},{6,7},{7,6},{8,9},{9,8},{10,11... | collective-permute-start | bytes 393224 | tf_op jit(solution)/shard_map/ppermute | solution.py:450

commit v5 on v4

--- a/solution.py
+++ b/solution.py
@@ -91,7 +91,7 @@
     return first, last
 
 
-def gram_kernel(x_ref, w_ref, out_ref, keep_ref, total_ref):
+def gram_kernel(x_ref, w_ref, out_ref, keep_ref, first_ref, total_ref):
     rows, each = x_ref.shape[1:3]
     size = total_ref.shape[0]
 
@@ -107,6 +107,8 @@
             at = pl.program_id(0) * each + v
             for x in group:
                 keep_ref[at, x] = plain[x - first]
+                if x < 2:
+                    first_ref[x, at] = plain[x - first]
             plain = jnp.concatenate(plain, axis=1)
             weight = jnp.concatenate([w_ref[x : x + 1, :] for x in group], axis=1)
             high, low = split(plain.astype(jnp.float32) * weight)
@@ -132,10 +134,11 @@
             pl.BlockSpec((owners, rows, each, count, width), lambda v: (0, 0, v, 0, 0)),
             pl.BlockSpec((rows, width), lambda v: (0, 0)),
         ],
-        out_specs=[pl.BlockSpec((size // 2 + 16, size), lambda v: (0, 0)), VMEM],
+        out_specs=[pl.BlockSpec((size // 2 + 16, size), lambda v: (0, 0)), VMEM, VMEM],
         out_shape=[
             jax.ShapeDtypeStruct((size // 2 + 16, size), jnp.float32),
             jax.ShapeDtypeStruct((variables, rows, size, width), block.dtype),
+            jax.ShapeDtypeStruct((2, variables, size, width), block.dtype),
         ],
         scratch_shapes=[pltpu.VMEM((size, size), jnp.float32)],
         compiler_params=params(),
@@ -224,8 +227,8 @@
     for v in range(variables):
         plain = {x: x_ref[v, x] for x in range(rows - 4, rows)}
         for x in range(2):
-            near, far = (row_of(ref.at[:owners], x, v) for ref in (near_ref, far_ref))
-            plain[rows + x] = jnp.where(odd, far, near)
+            near = row_of(near_ref.at[:owners], x, v)
+            plain[rows + x] = jnp.where(odd, far_ref[x, v], near)
         value = {x: part.astype(jnp.float32) for x, part in plain.items()}
         pair = jnp.concatenate([plain[rows - 2], plain[rows - 1]], axis=1)
         store(f_ref, v, 0, stencil(value, rows - 2, pair, d_ref.at[v], band_ref))
@@ -469,7 +472,14 @@
     return lax.ppermute(value, axis, pairs)
 
 
-def swapped(block, weights, diffusivity, axis):
+def hop(value, axis, first, step):
+    devices = lax.axis_size(axis)
+    return lax.ppermute(
+        value, axis, [(i, i + step) for i in range(first, devices, 2) if 0 <= i + step < devices]
+    )
+
+
+def lower_rows(block, weights, diffusivity, axis):
     devices = lax.axis_size(axis)
     _, rows, variables, count, width = block.shape
     odd = lax.axis_index(axis) % 2 == 1
@@ -479,16 +489,14 @@
     parts = jnp.stack([top, middle, factor - top - middle], axis=2).astype(block.dtype)
     parts = parts.transpose(1, 0, 2, 3)
     parts = jnp.pad(parts, ((0, 0), (0, 0), (0, count - 3), (0, 0)))[None]
-    sent = [
+    near, far = [
         jnp.concatenate([lax.dynamic_slice_in_dim(block, start, 2, axis=1), parts], axis=0)
-        for start in (jnp.where(odd, 0, rows - 2), jnp.where(odd, rows - 2, 0))
+        for start in (jnp.where(odd, 0, rows - 2), rows - 2)
     ]
-    *sent, block = lax.optimization_barrier((*sent, block))
-    received = []
-    for first, part in enumerate(sent):
-        pairs = [(i, i + 1) for i in range(first, devices - 1, 2)]
-        received.append(lax.ppermute(part, axis, pairs + [(b, a) for a, b in pairs]))
-    return block, received
+    near, far, block = lax.optimization_barrier((near, far, block))
+    pairs = [(i, i + 1) for i in range(0, devices - 1, 2)]
+    near = lax.ppermute(near, axis, pairs + [(b, a) for a, b in pairs])
+    return block, near, hop(far, axis, 1, 1)
 
 
 def on_device(snapshots, cell_weights, diffusivity):
@@ -502,13 +510,13 @@
     _, rows, variables, count, width = block.shape
     size, cell_count = block.shape[0] * count, rows * variables * width * owners
     band = band_matrix(width)
-    half = variables // 2
+    half = variables - variables // 4
     spans = [span for span in (range(half), range(half, variables)) if len(span)]
 
     odd = (lax.axis_index("gx") % 2).astype(jnp.int32).reshape(1)
-    block, (near, far) = swapped(block, cell_weights, diffusivity, "gx")
+    block, near, far = lower_rows(block, cell_weights, diffusivity, "gx")
     block, near = together((block, near))
-    packed, kept = gram_of(block, cell_weights)
+    packed, kept, first_rows = gram_of(block, cell_weights)
     cross = jnp.zeros((size, size), jnp.float32)
     mids = []
 
@@ -522,16 +530,19 @@
 
     gram = Sum(packed, "gx")
     steps = gram.steps()
-    kept, gram.own = together((kept, gram.own))
+    kept, first_rows, gram.own = together((kept, first_rows, gram.own))
+    above = hop(first_rows, "gx", 0, -1)
     for span in spans:
+        if mids:
+            kept, cross, gram.own = together((kept, cross, gram.own))
         cross = inner(span, kept, cross)
+        if steps:
+            gram.add(steps.pop(0))
+    kept, cross, gram.own = together((kept, cross, gram.own))
     cross, bottom = stencil_call(
         lower_kernel, "lower", kept, variables, 1, True,
         near, far, cell_weights, diffusivity, band, cross, odd=odd,
     )
-    if steps:
-        gram.add(steps.pop(0))
-    cross, gram.own = together((cross, gram.own))
     cross = Sum(cross, "gx")
     while steps:
         gram.add(steps.pop(0))
@@ -539,10 +550,11 @@
     if steps:
         cross.add(steps.pop(0))
     top = stencil_call(
-        upper_kernel, "upper", kept, variables, 1, False, near, far, diffusivity, band, odd=odd
-    )
-    gram.own, cross.own, top = together((gram.own, cross.own, top))
-    state = rotation_first(gram.result(), cell_count)
+        upper_kernel, "upper", kept, variables, 1, False, near, above, diffusivity, band, odd=odd
+    )
+    gram.own, top = together((gram.own, top))
+    packed, cross.own = together((gram.result(), cross.own))
+    state = rotation_first(packed, cell_count)
     if steps:
         cross.add(steps.pop(0))
     state, cross.own = together((state, cross.own))

time: 158 us -> 158 us (level)
  waiting for transfers between devices: 82.1 us -> 84.5 us
  starting transfers between devices: 39.5 us -> 37.1 us
    ppermute x10, starting transfers between devices: 23.7 us -> 19.9 us  [swap(): lax.ppermute(part, self.axis, [(i, i ^ step) for i in range(self.count)])]
    ppermute x2 -> x3, waiting for transfers between devices: 0.01 us -> 2.31 us  [the longest x2 2.3 us: hop(): lax.ppermute(value, axis, [(i, i + step) for i in range(first, devices, 2...]
    ppermute x2 -> x3, starting transfers between devices: 8.25 us -> 9.74 us  [the longest x2 9.67 us: hop(): lax.ppermute(value, axis, [(i, i + step) for i in range(first, devices, 2...]
  transfers between devices with their start and end apart: 13 -> 14, of which waited for: 4 -> 6; matrix products, arithmetic and copies ran while one was open for 0% -> 0% of each run, Pallas kernels for 18% -> 17%
where the time goes in v5:
time: 158 us
  waiting for transfers between devices  84.5 us (53%)
  starting transfers between devices  37.1 us (23%)
  Pallas kernels  31.6 us (20%)
    all_to_all x1, waiting for transfers between devices, on_device(): block = lax.all_to_all(relayout(snapshots, owners), 'gx', 0, 0, tiled=True)  77.9 us
    ppermute x10, starting transfers between devices, swap(): lax.ppermute(part, self.axis, [(i, i ^ step) for i in range(self.count)])  19.9 us
    ppermute x2, starting transfers between devices, hop(): lax.ppermute(value, axis, [(i, i + step) for i in range(first, devices, 2...  9.67 us
    all_to_all x1, starting transfers between devices, on_device(): block = lax.all_to_all(relayout(snapshots, owners), 'gx', 0, 0, tiled=True)  7.48 us
    pallas_call x4, Pallas kernels, stencil_call(): pl.pallas_call(kernel, in_specs=[pl.BlockSpec(memory_space=pltpu.SMEM)] *...  7.31 us
    pallas_call x2, Pallas kernels, modes_of(): pl.pallas_call(lambda *refs: modes_kernel(first, *refs), grid=(span,), in...  6.99 us
    pallas_call x1, Pallas kernels, gram_of(): pl.pallas_call(gram_kernel, grid=(variables // each,), in_specs=[pl.Block...  4.59 us
    pallas_call x1, Pallas kernels, rotation_first(): pl.pallas_call(lambda *refs: rotation_first_kernel(1.0 / cell_count, *ref...  4.38 us
  transfers between devices with their start and end apart: 14, of which 6 were waited for; matrix products, arithmetic and copies ran while one was open for 0% of the time, Pallas kernels for 17%

profile of v5, /device:TPU:1, one launch (start us, length us, event | category | flops | bytes accessed | tf_op | source)
XLA Modules:
  0.0 157.6 jit_solution(2828598245856445666)
XLA Ops:
  0.6 4.3 %relayout.1 = bf16[16,16,4,16,128]{4,3,2,1,0:T(8,128)(2,1)} custom-call(bf16[16,4,256,128]{3,2,1,0:T(8,128)(2,1)} %in_ref.1), custom_call_target="tpu_custom_call" | custom-call | tf_op jit(solution)/shard_map/relayout/pallas_call | solution.py:54
  4.9 0.0 copy-start.1
  4.9 0.0 copy-start
  4.9 7.5 %all-to-all-start = ((bf16[16,16,4,16,128]{4,3,2,1,0:T(8,128)(2,1)}), bf16[16,16,4,16,128]{4,3,2,1,0:T(8,128)(2,1)}, u32[]{:S(2)}, u32[]{:S(2)}) async-start(bf16[16,16,4,16,128]{4,3,2,1,0:T(8,128)(2,1)} %relayout.1), calls=%async_computation | async-start | bytes 8388608 | tf_op jit(solution)/shard_map/all_to_all | solution.py:506
  12.4 0.0 copy-done.1
  12.4 0.0 copy-done
  12.5 77.9 %all-to-all-done.x_ref = bf16[16,16,4,16,128]{4,3,2,1,0:T(8,128)(2,1)} async-done(((bf16[16,16,4,16,128]{4,3,2,1,0:T(8,128)(2,1)}), bf16[16,16,4,16,128]{4,3,2,1,0:T(8,128)(2,1)}, u32[]{:S(2)}, u32[]{:S(2)}) %all-to-all-start) | async-done | bytes 4194336 | tf_op jit(solution)/shard_map/all_to_all | solution.py:506
  90.5 1.4 fusion.13
  91.9 0.1 pad_maximum_fusion
  92.0 0.1 collective-permute-start
  92.1 8.2 %collective-permute-start.7 = (bf16[17,2,4,16,128]{4,3,2,1,0:T(8,128)(2,1)S(1)}, bf16[17,2,4,16,128]{4,3,2,1,0:T(8,128)(2,1)S(1)}, u32[]{:S(2)}, u32[]{:S(2)}) collective-permute-start(bf16[17,2,4,16,128]{4,3,2,1,0:T(8,128)(2,1)S(1)} %get-tuple-element.54), channel_id=1, source_target_pairs={{1,2},{3,4},{5,6},{7,8},{9,10},{11,12},{13,14},{17,18},{19,20},{21... | collective-permute-start | bytes 1671176 | tf_op jit(solution)/shard_map/ppermute | solution.py:477
  100.3 0.0 collective-permute-done.near_ref
  100.3 4.6 %gram.1 = (f32[144,256]{1,0:T(8,128)S(1)}, bf16[4,16,256,128]{3,2,1,0:T(8,128)(2,1)S(1)}, bf16[2,4,256,128]{3,2,1,0:T(8,128)(2,1)S(1)}) custom-call(bf16[16,16,4,16,128]{4,3,2,1,0:T(8,128)(2,1)} %all-to-all-done.x_ref, f32[16,128]{1,0:T(8,128)S(1)} %copy-done.1), custom_call_target="tpu_custom_call" | custom-call | flops 2000000000 | bytes 1 | tf_op jit(solution)/shard_map/gram/pallas_call | solution.py:130
  104.9 0.1 collective-permute-start.1
  105.0 1.2 collective-permute-done.1
  106.3 9.3 %collective-permute-start.2 = (f32[72,256]{1,0:T(8,128)S(1)}, f32[72,256]{1,0:T(8,128)S(1)}, u32[]{:S(2)}, u32[]{:S(2)}) collective-permute-start(f32[72,256]{1,0:T(8,128)S(1)} %select_add_fusion.1), channel_id=1, source_target_pairs={{0,2},{1,3},{2,0},{3,1},{4,6},{5,7},{6,4},{7,5},{8,10},{9,11},{10,... | collective-permute-start | bytes 221192 | tf_op jit(solution)/shard_map/ppermute | solution.py:453
  115.6 0.2 select_convert_fusion.band_ref
  115.8 3.9 %inner.2 = (f32[256,256]{1,0:T(8,128)S(1)}, bf16[2,3,6,256,256]{4,3,2,1,0:T(8,128)(2,1)S(1)}) custom-call(bf16[4,16,256,128]{3,2,1,0:T(8,128)(2,1)S(1)} %get-tuple-element.50.x_ref, f32[16,128]{1,0:T(8,128)S(1)} %copy-done.1, f32[4,16,128]{2,1,0:T(8,128)S(1)} %copy-done, bf16[256,256]{1,0:T(8,128)(2,1)S(1)} %select_convert_fusion.band_ref, ...), custom_call_target="tpu_custom_call" | custom-call | flops 1 | bytes 1 | tf_op jit(solution)/shard_map/inner/pallas_call | solution.py:255
  119.7 0.0 collective-permute-done.2
  119.8 3.1 %collective-permute-start.3 = (f32[72,256]{1,0:T(8,128)S(1)}, f32[72,256]{1,0:T(8,128)S(1)}, u32[]{:S(2)}, u32[]{:S(2)}) collective-permute-start(f32[72,256]{1,0:T(8,128)S(1)} %add.36), channel_id=1, source_target_pairs={{0,4},{1,5},{2,6},{3,7},{4,0},{5,1},{6,2},{7,3},{8,12},{9,13},{10,... | collective-permute-start | bytes 221192 | tf_op jit(solution)/shard_map/ppermute | solution.py:453
  122.9 1.5 collective-permute-start.5
  124.3 1.3 inner.3
  125.7 0.0 collective-permute-done.3
  125.7 0.0 collective-permute-done.7.far_ref
  125.7 1.5 lower.1
  127.2 0.5 collective-permute-start.8
  127.7 1.8 %collective-permute-start.4 = (f32[72,256]{1,0:T(8,128)S(1)}, f32[72,256]{1,0:T(8,128)S(1)}, u32[]{:S(2)}, u32[]{:S(2)}) collective-permute-start(f32[72,256]{1,0:T(8,128)S(1)} %add.37), channel_id=1, source_target_pairs={{0,8},{1,9},{2,10},{3,11},{4,12},{5,13},{6,14},{7,15},{8,0},{9,1},... | collective-permute-start | bytes 221192 | tf_op jit(solution)/shard_map/ppermute | solution.py:453
  129.5 0.0 collective-permute-done.8
  129.5 1.4 collective-permute-start.9
  130.9 1.8 %collective-permute-done.4 = f32[72,256]{1,0:T(8,128)S(1)} collective-permute-done((f32[72,256]{1,0:T(8,128)S(1)}, f32[72,256]{1,0:T(8,128)S(1)}, u32[]{:S(2)}, u32[]{:S(2)}) %collective-permute-start.4) | collective-permute-done | bytes 73760 | tf_op jit(solution)/shard_map/ppermute | solution.py:453
  132.7 2.3 %collective-permute-done.5.far_ref = bf16[2,4,256,128]{3,2,1,0:T(8,128)(2,1)S(1)} collective-permute-done((bf16[2,4,256,128]{3,2,1,0:T(8,128)(2,1)S(1)}, bf16[2,4,256,128]{3,2,1,0:T(8,128)(2,1)S(1)}, u32[]{:S(2)}, u32[]{:S(2)}) %collective-permute-start.5) | collective-permute-done | bytes 524320 | tf_op jit(solution)/shard_map/ppermute | solution.py:477
  135.0 0.6 upper.1.refs_3_
  135.6 2.0 %collective-permute-start.6 = (f32[72,256]{1,0:T(8,128)S(1)}, f32[72,256]{1,0:T(8,128)S(1)}, u32[]{:S(2)}, u32[]{:S(2)}) collective-permute-start(f32[72,256]{1,0:T(8,128)S(1)} %add.38), channel_id=1, source_target_pairs={{0,1},{1,0},{2,3},{3,2},{4,5},{5,4},{6,7},{7,6},{8,9},{9,8},{10,11... | collective-permute-start | bytes 221192 | tf_op jit(solution)/shard_map/ppermute | solution.py:453
  137.5 0.0 collective-permute-done.9
  137.6 0.9 collective-permute-done.6
  138.5 0.1 collective-permute-start.10
  138.6 4.4 %rotation_first.1 = (f32[128,256]{1,0:T(8,128)S(1)}, f32[256,256]{1,0:T(8,128)S(1)}) custom-call(f32[144,256]{1,0:T(8,128)S(1)} %pad_maximum_fusion.2.refs_0_), custom_call_target="tpu_custom_call" | custom-call | flops 1 | bytes 1 | tf_op jit(solution)/shard_map/rotation_first/pallas_call | solution.py:374
  143.0 0.3 collective-permute-done.10
  143.3 0.7 collective-permute-start.11
  144.0 4.1 %rotation_last.1.refs_0_ = f32[256,256]{1,0:T(8,128)S(1)} custom-call(f32[128,256]{1,0:T(8,128)S(1)} %get-tuple-element.61.before_ref, f32[256,256]{1,0:T(8,128)S(1)} %get-tuple-element.62.state_ref), custom_call_target="tpu_custom_call" | custom-call | flops 1 | bytes 1 | tf_op jit(solution)/shard_map/rotation_last/pallas_call | solution.py:390
  148.1 4.8 %modes.2.refs_4_ = bf16[256,4,16,128]{3,2,1,0:T(8,128)(2,1)} custom-call(f32[256,256]{1,0:T(8,128)S(1)} %rotation_last.1.refs_0_, bf16[2,4,1,256,256]{4,3,2,1,0:T(8,128)(2,1)S(1)} %get-tuple-element.63.refs_1_, bf16[2,3,6,256,256]{4,3,2,1,0:T(8,128)(2,1)S(1)} %get-tuple-element.66.refs_2_, bf16[2,4,1,256,256]{4,3,2,1,0:T(8,128)(2,1)S(1)} %upper.1.refs_3_), custom_call_target="tpu_custom_call" | custom-call | flops 1 | bytes 1 | tf_op jit(solution)/shard_map/modes/pallas_call | solution.py:423
  152.9 0.0 collective-permute-done.11
  152.9 1.0 collective-permute-start.12
  153.9 2.2 %modes.3 = bf16[256,4,16,128]{3,2,1,0:T(8,128)(2,1)} custom-call(f32[256,256]{1,0:T(8,128)S(1)} %rotation_last.1.refs_0_, bf16[2,4,1,256,256]{4,3,2,1,0:T(8,128)(2,1)S(1)} %get-tuple-element.63.refs_1_, bf16[2,1,6,256,256]{4,3,2,1,0:T(8,128)(2,1)S(1)} %get-tuple-element.64.refs_2_, ...), custom_call_target="tpu_custom_call", output_to_operand_aliasing={{}: (4, {})} | custom-call | flops 1342177280 | bytes 1 | tf_op jit(solution)/shard_map/modes/pallas_call | solution.py:423
  156.1 0.0 collective-permute-done.12
  156.1 0.4 fusion
  156.5 1.1 fusion.14
  (22 shorter events, 0.3 us)
Async XLA Ops:
  4.9 7.5 %copy-start.1 = (f32[16,128]{1,0:T(8,128)S(1)}, f32[16,128]{1,0:T(8,128)}, u32[]{:S(2)}) copy-start(f32[16,128]{1,0:T(8,128)} %w_ref.7) | copy-start | bytes 24580
  4.9 7.5 %copy-start = (f32[4,16,128]{2,1,0:T(8,128)S(1)}, f32[4,16,128]{2,1,0:T(8,128)}, u32[]{:S(2)}) copy-start(f32[4,16,128]{2,1,0:T(8,128)} %d_ref.7) | copy-start | bytes 98308
  4.9 85.6 %all-to-all-start = ((bf16[16,16,4,16,128]{4,3,2,1,0:T(8,128)(2,1)}), bf16[16,16,4,16,128]{4,3,2,1,0:T(8,128)(2,1)}, u32[]{:S(2)}, u32[]{:S(2)}) async-start(bf16[16,16,4,16,128]{4,3,2,1,0:T(8,128)(2,1)} %relayout.1), calls=%async_computation | async-start | bytes 8388608 | tf_op jit(solution)/shard_map/all_to_all | solution.py:506
  92.0 8.3 %collective-permute-start = (bf16[17,2,4,16,128]{4,3,2,1,0:T(8,128)(2,1)S(1)}, bf16[17,2,4,16,128]{4,3,2,1,0:T(8,128)(2,1)S(1)}, u32[]{:S(2)}, u32[]{:S(2)}) collective-permute-start(bf16[17,2,4,16,128]{4,3,2,1,0:T(8,128)(2,1)S(1)} %get-tuple-element.37), channel_id=1, source_target_pairs={{0,1},{2,3},{4,5},{6,7},{8,9},{10,11},{12,13},{14,15},{1,0},{3,2},... | collective-permute-start | bytes 1671176 | tf_op jit(solution)/shard_map/ppermute | solution.py:498
  92.1 33.7 %collective-permute-start.7 = (bf16[17,2,4,16,128]{4,3,2,1,0:T(8,128)(2,1)S(1)}, bf16[17,2,4,16,128]{4,3,2,1,0:T(8,128)(2,1)S(1)}, u32[]{:S(2)}, u32[]{:S(2)}) collective-permute-start(bf16[17,2,4,16,128]{4,3,2,1,0:T(8,128)(2,1)S(1)} %get-tuple-element.54), channel_id=1, source_target_pairs={{1,2},{3,4},{5,6},{7,8},{9,10},{11,12},{13,14},{17,18},{19,20},{21... | collective-permute-start | bytes 1671176 | tf_op jit(solution)/shard_map/ppermute | solution.py:477
  104.9 1.3 collective-permute-start.1
  106.3 13.5 %collective-permute-start.2 = (f32[72,256]{1,0:T(8,128)S(1)}, f32[72,256]{1,0:T(8,128)S(1)}, u32[]{:S(2)}, u32[]{:S(2)}) collective-permute-start(f32[72,256]{1,0:T(8,128)S(1)} %select_add_fusion.1), channel_id=1, source_target_pairs={{0,2},{1,3},{2,0},{3,1},{4,6},{5,7},{6,4},{7,5},{8,10},{9,11},{10,... | collective-permute-start | bytes 221192 | tf_op jit(solution)/shard_map/ppermute | solution.py:453
  119.8 5.9 %collective-permute-start.3 = (f32[72,256]{1,0:T(8,128)S(1)}, f32[72,256]{1,0:T(8,128)S(1)}, u32[]{:S(2)}, u32[]{:S(2)}) collective-permute-start(f32[72,256]{1,0:T(8,128)S(1)} %add.36), channel_id=1, source_target_pairs={{0,4},{1,5},{2,6},{3,7},{4,0},{5,1},{6,2},{7,3},{8,12},{9,13},{10,... | collective-permute-start | bytes 221192 | tf_op jit(solution)/shard_map/ppermute | solution.py:453
  122.9 12.1 %collective-permute-start.5 = (bf16[2,4,256,128]{3,2,1,0:T(8,128)(2,1)S(1)}, bf16[2,4,256,128]{3,2,1,0:T(8,128)(2,1)S(1)}, u32[]{:S(2)}, u32[]{:S(2)}) collective-permute-start(bf16[2,4,256,128]{3,2,1,0:T(8,128)(2,1)S(1)} %get-tuple-element.52), channel_id=1, source_target_pairs={{2,1},{4,3},{6,5},{8,7},{10,9},{12,11},{14,13},{18,17},{20,19},{22... | collective-permute-start | bytes 1572872 | tf_op jit(solution)/shard_map/ppermute | solution.py:477
  127.2 2.2 %collective-permute-start.8 = (f32[128,256]{1,0:T(8,128)S(1)}, f32[128,256]{1,0:T(8,128)S(1)}, u32[]{:S(2)}, u32[]{:S(2)}) collective-permute-start(f32[128,256]{1,0:T(8,128)S(1)} %slice_select_fusion), channel_id=1, source_target_pairs={{0,1},{1,0},{2,3},{3,2},{4,5},{5,4},{6,7},{7,6},{8,9},{9,8},{10,11... | collective-permute-start | bytes 393224 | tf_op jit(solution)/shard_map/ppermute | solution.py:453
  127.7 5.0 %collective-permute-start.4 = (f32[72,256]{1,0:T(8,128)S(1)}, f32[72,256]{1,0:T(8,128)S(1)}, u32[]{:S(2)}, u32[]{:S(2)}) collective-permute-start(f32[72,256]{1,0:T(8,128)S(1)} %add.37), channel_id=1, source_target_pairs={{0,8},{1,9},{2,10},{3,11},{4,12},{5,13},{6,14},{7,15},{8,0},{9,1},... | collective-permute-start | bytes 221192 | tf_op jit(solution)/shard_map/ppermute | solution.py:453
  129.5 8.0 %collective-permute-start.9 = (f32[128,256]{1,0:T(8,128)S(1)}, f32[128,256]{1,0:T(8,128)S(1)}, u32[]{:S(2)}, u32[]{:S(2)}) collective-permute-start(f32[128,256]{1,0:T(8,128)S(1)} %select_add_fusion), channel_id=1, source_target_pairs={{0,2},{1,3},{2,0},{3,1},{4,6},{5,7},{6,4},{7,5},{8,10},{9,11},{10,... | collective-permute-start | bytes 393224 | tf_op jit(solution)/shard_map/ppermute | solution.py:453
  135.6 2.9 %collective-permute-start.6 = (f32[72,256]{1,0:T(8,128)S(1)}, f32[72,256]{1,0:T(8,128)S(1)}, u32[]{:S(2)}, u32[]{:S(2)}) collective-permute-start(f32[72,256]{1,0:T(8,128)S(1)} %add.38), channel_id=1, source_target_pairs={{0,1},{1,0},{2,3},{3,2},{4,5},{5,4},{6,7},{7,6},{8,9},{9,8},{10,11... | collective-permute-start | bytes 221192 | tf_op jit(solution)/shard_map/ppermute | solution.py:453
  138.5 4.8 %collective-permute-start.10 = (f32[128,256]{1,0:T(8,128)S(1)}, f32[128,256]{1,0:T(8,128)S(1)}, u32[]{:S(2)}, u32[]{:S(2)}) collective-permute-start(f32[128,256]{1,0:T(8,128)S(1)} %add.40), channel_id=1, source_target_pairs={{0,4},{1,5},{2,6},{3,7},{4,0},{5,1},{6,2},{7,3},{8,12},{9,13},{10,... | collective-permute-start | bytes 393224 | tf_op jit(solution)/shard_map/ppermute | solution.py:453
  143.3 9.6 %collective-permute-start.11 = (f32[128,256]{1,0:T(8,128)S(1)}, f32[128,256]{1,0:T(8,128)S(1)}, u32[]{:S(2)}, u32[]{:S(2)}) collective-permute-start(f32[128,256]{1,0:T(8,128)S(1)} %add.41), channel_id=1, source_target_pairs={{0,8},{1,9},{2,10},{3,11},{4,12},{5,13},{6,14},{7,15},{8,0},{9,1},... | collective-permute-start | bytes 393224 | tf_op jit(solution)/shard_map/ppermute | solution.py:453
  152.9 3.1 %collective-permute-start.12 = (f32[128,256]{1,0:T(8,128)S(1)}, f32[128,256]{1,0:T(8,128)S(1)}, u32[]{:S(2)}, u32[]{:S(2)}) collective-permute-start(f32[128,256]{1,0:T(8,128)S(1)} %add.42), channel_id=1, source_target_pairs={{0,1},{1,0},{2,3},{3,2},{4,5},{5,4},{6,7},{7,6},{8,9},{9,8},{10,11... | collective-permute-start | bytes 393224 | tf_op jit(solution)/shard_map/ppermute | solution.py:453

commit v6 on v5

--- a/solution.py
+++ b/solution.py
@@ -1,4 +1,5 @@
 import functools
+import math
 
 import jax
 import jax.numpy as jnp
@@ -36,12 +37,29 @@
     return lax.dot_general(a, b, NT, preferred_element_type=jnp.float32)
 
 
-def relayout_kernel(in_ref, out_ref):
-    owners, rows, variables = out_ref.shape[:3]
-    for owner in range(owners):
-        for v in range(variables):
-            block = in_ref[:, v, owner * rows : (owner + 1) * rows]
-            out_ref[owner, :, v] = jnp.swapaxes(block, 0, 1)
+def relayout_kernel(reads, writes, in_ref, out_ref, from_ref, to_ref, read_sems, write_sems):
+    owners, rows, variables = to_ref.shape[:3]
+    each_read, each_write = owners // reads, owners // writes
+    arriving = []
+    for i in range(reads):
+        span = pl.ds(i * each_read * rows, each_read * rows)
+        arriving.append(
+            pltpu.make_async_copy(in_ref.at[:, :, span], from_ref.at[:, :, span], read_sems.at[i])
+        )
+        arriving[i].start()
+    leaving = []
+    for i in range(writes):
+        for owner in range(i * each_write, (i + 1) * each_write):
+            if owner % each_read == 0:
+                arriving[owner // each_read].wait()
+            for v in range(variables):
+                block = from_ref[:, v, owner * rows : (owner + 1) * rows]
+                to_ref[owner, :, v] = jnp.swapaxes(block, 0, 1)
+        span = pl.ds(i * each_write, each_write)
+        leaving.append(pltpu.make_async_copy(to_ref.at[span], out_ref.at[span], write_sems.at[i]))
+        leaving[i].start()
+    for copy in leaving:
+        copy.wait()
 
 
 def relayout(snapshots, owners):
@@ -50,15 +68,19 @@
     if count % 16 or rows % 16:
         block = snapshots.reshape(count, variables, owners, rows, width)
         return block.transpose(2, 3, 1, 0, 4)
-    each = owners // 2 if owners % 2 == 0 else 1
+    reads, writes = math.gcd(owners, 4), math.gcd(owners, 8)
+    shape = (owners, rows, variables, count, width)
     return pl.pallas_call(
-        relayout_kernel,
-        grid=(owners // each,),
-        in_specs=[pl.BlockSpec((count, variables, each * rows, width), lambda i: (0, 0, i, 0))],
-        out_specs=pl.BlockSpec(
-            (each, rows, variables, count, width), lambda i: (i, 0, 0, 0, 0)
-        ),
-        out_shape=jax.ShapeDtypeStruct((owners, rows, variables, count, width), snapshots.dtype),
+        functools.partial(relayout_kernel, reads, writes),
+        in_specs=[pl.BlockSpec(memory_space=pl.ANY)],
+        out_specs=pl.BlockSpec(memory_space=pl.ANY),
+        out_shape=jax.ShapeDtypeStruct(shape, snapshots.dtype),
+        scratch_shapes=[
+            pltpu.VMEM(snapshots.shape, snapshots.dtype),
+            pltpu.VMEM(shape, snapshots.dtype),
+            pltpu.SemaphoreType.DMA((reads,)),
+            pltpu.SemaphoreType.DMA((writes,)),
+        ],
         compiler_params=pltpu.CompilerParams(vmem_limit_bytes=60 * 1024 * 1024),
         name="relayout",
     )(snapshots)

time: 158 us -> 157 us (level)
  no operation moved by 1% of the time
where the time goes in v6:
time: 157 us
  waiting for transfers between devices  84.5 us (54%)
  starting transfers between devices  37 us (24%)
  Pallas kernels  30.8 us (20%)
    all_to_all x1, waiting for transfers between devices, on_device(): block = lax.all_to_all(relayout(snapshots, owners), 'gx', 0, 0, tiled=True)  77.9 us
    ppermute x10, starting transfers between devices, swap(): lax.ppermute(part, self.axis, [(i, i ^ step) for i in range(self.count)])  19.9 us
    ppermute x2, starting transfers between devices, hop(): lax.ppermute(value, axis, [(i, i + step) for i in range(first, devices, 2...  9.67 us
    all_to_all x1, starting transfers between devices, on_device(): block = lax.all_to_all(relayout(snapshots, owners), 'gx', 0, 0, tiled=True)  7.36 us
    pallas_call x4, Pallas kernels, stencil_call(): pl.pallas_call(kernel, in_specs=[pl.BlockSpec(memory_space=pltpu.SMEM)] *...  7.31 us
    pallas_call x2, Pallas kernels, modes_of(): pl.pallas_call(lambda *refs: modes_kernel(first, *refs), grid=(span,), in...  6.99 us
    pallas_call x1, Pallas kernels, gram_of(): pl.pallas_call(gram_kernel, grid=(variables // each,), in_specs=[pl.Block...  4.59 us
    pallas_call x1, Pallas kernels, rotation_first(): pl.pallas_call(lambda *refs: rotation_first_kernel(1.0 / cell_count, *ref...  4.38 us
  transfers between devices with their start and end apart: 14, of which 6 were waited for; matrix products, arithmetic and copies ran while one was open for 0% of the time, Pallas kernels for 17%

profile of v6, /device:TPU:1, one launch (start us, length us, event | category | flops | bytes accessed | tf_op | source)
XLA Modules:
  0.0 156.8 jit_solution(10092958164795535209)
XLA Ops:
  0.6 3.5 %relayout.1 = bf16[16,16,4,16,128]{4,3,2,1,0:T(8,128)(2,1)} custom-call(bf16[16,4,256,128]{3,2,1,0:T(8,128)(2,1)} %in_ref.1), custom_call_target="tpu_custom_call" | custom-call | tf_op jit(solution)/shard_map/relayout/pallas_call | solution.py:73
  4.1 0.0 copy-start.1
  4.1 0.0 copy-start
  4.2 7.4 %all-to-all-start = ((bf16[16,16,4,16,128]{4,3,2,1,0:T(8,128)(2,1)}), bf16[16,16,4,16,128]{4,3,2,1,0:T(8,128)(2,1)}, u32[]{:S(2)}, u32[]{:S(2)}) async-start(bf16[16,16,4,16,128]{4,3,2,1,0:T(8,128)(2,1)} %relayout.1), calls=%async_computation | async-start | bytes 8388608 | tf_op jit(solution)/shard_map/all_to_all | solution.py:528
  11.5 0.0 copy-done.1
  11.5 0.0 copy-done
  11.7 77.9 %all-to-all-done.x_ref = bf16[16,16,4,16,128]{4,3,2,1,0:T(8,128)(2,1)} async-done(((bf16[16,16,4,16,128]{4,3,2,1,0:T(8,128)(2,1)}), bf16[16,16,4,16,128]{4,3,2,1,0:T(8,128)(2,1)}, u32[]{:S(2)}, u32[]{:S(2)}) %all-to-all-start) | async-done | bytes 4194336 | tf_op jit(solution)/shard_map/all_to_all | solution.py:528
  89.6 1.4 fusion.13
  91.0 0.1 pad_maximum_fusion
  91.1 0.1 collective-permute-start
  91.2 8.2 %collective-permute-start.7 = (bf16[17,2,4,16,128]{4,3,2,1,0:T(8,128)(2,1)S(1)}, bf16[17,2,4,16,128]{4,3,2,1,0:T(8,128)(2,1)S(1)}, u32[]{:S(2)}, u32[]{:S(2)}) collective-permute-start(bf16[17,2,4,16,128]{4,3,2,1,0:T(8,128)(2,1)S(1)} %get-tuple-element.54), channel_id=1, source_target_pairs={{1,2},{3,4},{5,6},{7,8},{9,10},{11,12},{13,14},{17,18},{19,20},{21... | collective-permute-start | bytes 1671176 | tf_op jit(solution)/shard_map/ppermute | solution.py:499
  99.4 0.0 collective-permute-done.near_ref
  99.4 4.6 %gram.1 = (f32[144,256]{1,0:T(8,128)S(1)}, bf16[4,16,256,128]{3,2,1,0:T(8,128)(2,1)S(1)}, bf16[2,4,256,128]{3,2,1,0:T(8,128)(2,1)S(1)}) custom-call(bf16[16,16,4,16,128]{4,3,2,1,0:T(8,128)(2,1)} %all-to-all-done.x_ref, f32[16,128]{1,0:T(8,128)S(1)} %copy-done.1), custom_call_target="tpu_custom_call" | custom-call | flops 2000000000 | bytes 1 | tf_op jit(solution)/shard_map/gram/pallas_call | solution.py:152
  104.1 0.1 collective-permute-start.1
  104.2 1.2 collective-permute-done.1
  105.4 9.3 %collective-permute-start.2 = (f32[72,256]{1,0:T(8,128)S(1)}, f32[72,256]{1,0:T(8,128)S(1)}, u32[]{:S(2)}, u32[]{:S(2)}) collective-permute-start(f32[72,256]{1,0:T(8,128)S(1)} %select_add_fusion.1), channel_id=1, source_target_pairs={{0,2},{1,3},{2,0},{3,1},{4,6},{5,7},{6,4},{7,5},{8,10},{9,11},{10,... | collective-permute-start | bytes 221192 | tf_op jit(solution)/shard_map/ppermute | solution.py:475
  114.8 0.2 select_convert_fusion.band_ref
  115.0 3.9 %inner.2 = (f32[256,256]{1,0:T(8,128)S(1)}, bf16[2,3,6,256,256]{4,3,2,1,0:T(8,128)(2,1)S(1)}) custom-call(bf16[4,16,256,128]{3,2,1,0:T(8,128)(2,1)S(1)} %get-tuple-element.50.x_ref, f32[16,128]{1,0:T(8,128)S(1)} %copy-done.1, f32[4,16,128]{2,1,0:T(8,128)S(1)} %copy-done, bf16[256,256]{1,0:T(8,128)(2,1)S(1)} %select_convert_fusion.band_ref, ...), custom_call_target="tpu_custom_call" | custom-call | flops 1 | bytes 1 | tf_op jit(solution)/shard_map/inner/pallas_call | solution.py:277
  118.9 0.0 collective-permute-done.2
  118.9 3.1 %collective-permute-start.3 = (f32[72,256]{1,0:T(8,128)S(1)}, f32[72,256]{1,0:T(8,128)S(1)}, u32[]{:S(2)}, u32[]{:S(2)}) collective-permute-start(f32[72,256]{1,0:T(8,128)S(1)} %add.36), channel_id=1, source_target_pairs={{0,4},{1,5},{2,6},{3,7},{4,0},{5,1},{6,2},{7,3},{8,12},{9,13},{10,... | collective-permute-start | bytes 221192 | tf_op jit(solution)/shard_map/ppermute | solution.py:475
  122.0 1.5 collective-permute-start.5
  123.5 1.3 inner.3
  124.8 0.0 collective-permute-done.3
  124.9 0.0 collective-permute-done.7.far_ref
  124.9 1.5 lower.1
  126.4 0.5 collective-permute-start.8
  126.9 1.8 %collective-permute-start.4 = (f32[72,256]{1,0:T(8,128)S(1)}, f32[72,256]{1,0:T(8,128)S(1)}, u32[]{:S(2)}, u32[]{:S(2)}) collective-permute-start(f32[72,256]{1,0:T(8,128)S(1)} %add.37), channel_id=1, source_target_pairs={{0,8},{1,9},{2,10},{3,11},{4,12},{5,13},{6,14},{7,15},{8,0},{9,1},... | collective-permute-start | bytes 221192 | tf_op jit(solution)/shard_map/ppermute | solution.py:475
  128.6 0.0 collective-permute-done.8
  128.7 1.4 collective-permute-start.9
  130.1 1.8 %collective-permute-done.4 = f32[72,256]{1,0:T(8,128)S(1)} collective-permute-done((f32[72,256]{1,0:T(8,128)S(1)}, f32[72,256]{1,0:T(8,128)S(1)}, u32[]{:S(2)}, u32[]{:S(2)}) %collective-permute-start.4) | collective-permute-done | bytes 73760 | tf_op jit(solution)/shard_map/ppermute | solution.py:475
  131.8 2.3 %collective-permute-done.5.far_ref = bf16[2,4,256,128]{3,2,1,0:T(8,128)(2,1)S(1)} collective-permute-done((bf16[2,4,256,128]{3,2,1,0:T(8,128)(2,1)S(1)}, bf16[2,4,256,128]{3,2,1,0:T(8,128)(2,1)S(1)}, u32[]{:S(2)}, u32[]{:S(2)}) %collective-permute-start.5) | collective-permute-done | bytes 524320 | tf_op jit(solution)/shard_map/ppermute | solution.py:499
  134.1 0.6 upper.1.refs_3_
  134.7 2.0 %collective-permute-start.6 = (f32[72,256]{1,0:T(8,128)S(1)}, f32[72,256]{1,0:T(8,128)S(1)}, u32[]{:S(2)}, u32[]{:S(2)}) collective-permute-start(f32[72,256]{1,0:T(8,128)S(1)} %add.38), channel_id=1, source_target_pairs={{0,1},{1,0},{2,3},{3,2},{4,5},{5,4},{6,7},{7,6},{8,9},{9,8},{10,11... | collective-permute-start | bytes 221192 | tf_op jit(solution)/shard_map/ppermute | solution.py:475
  136.7 0.0 collective-permute-done.9
  136.7 0.9 collective-permute-done.6
  137.6 0.1 collective-permute-start.10
  137.7 4.4 %rotation_first.1 = (f32[128,256]{1,0:T(8,128)S(1)}, f32[256,256]{1,0:T(8,128)S(1)}) custom-call(f32[144,256]{1,0:T(8,128)S(1)} %pad_maximum_fusion.2.refs_0_), custom_call_target="tpu_custom_call" | custom-call | flops 1 | bytes 1 | tf_op jit(solution)/shard_map/rotation_first/pallas_call | solution.py:396
  142.1 0.3 collective-permute-done.10
  142.5 0.7 collective-permute-start.11
  143.2 4.1 %rotation_last.1.refs_0_ = f32[256,256]{1,0:T(8,128)S(1)} custom-call(f32[128,256]{1,0:T(8,128)S(1)} %get-tuple-element.61.before_ref, f32[256,256]{1,0:T(8,128)S(1)} %get-tuple-element.62.state_ref), custom_call_target="tpu_custom_call" | custom-call | flops 1 | bytes 1 | tf_op jit(solution)/shard_map/rotation_last/pallas_call | solution.py:412
  147.2 4.8 %modes.2.refs_4_ = bf16[256,4,16,128]{3,2,1,0:T(8,128)(2,1)} custom-call(f32[256,256]{1,0:T(8,128)S(1)} %rotation_last.1.refs_0_, bf16[2,4,1,256,256]{4,3,2,1,0:T(8,128)(2,1)S(1)} %get-tuple-element.63.refs_1_, bf16[2,3,6,256,256]{4,3,2,1,0:T(8,128)(2,1)S(1)} %get-tuple-element.66.refs_2_, bf16[2,4,1,256,256]{4,3,2,1,0:T(8,128)(2,1)S(1)} %upper.1.refs_3_), custom_call_target="tpu_custom_call" | custom-call | flops 1 | bytes 1 | tf_op jit(solution)/shard_map/modes/pallas_call | solution.py:445
  152.1 0.0 collective-permute-done.11
  152.1 1.0 collective-permute-start.12
  153.0 2.2 %modes.3 = bf16[256,4,16,128]{3,2,1,0:T(8,128)(2,1)} custom-call(f32[256,256]{1,0:T(8,128)S(1)} %rotation_last.1.refs_0_, bf16[2,4,1,256,256]{4,3,2,1,0:T(8,128)(2,1)S(1)} %get-tuple-element.63.refs_1_, bf16[2,1,6,256,256]{4,3,2,1,0:T(8,128)(2,1)S(1)} %get-tuple-element.64.refs_2_, ...), custom_call_target="tpu_custom_call", output_to_operand_aliasing={{}: (4, {})} | custom-call | flops 1342177280 | bytes 1 | tf_op jit(solution)/shard_map/modes/pallas_call | solution.py:445
  155.2 0.0 collective-permute-done.12
  155.2 0.4 fusion
  155.7 1.1 fusion.14
  (22 shorter events, 0.3 us)
Async XLA Ops:
  4.1 7.4 %copy-start.1 = (f32[16,128]{1,0:T(8,128)S(1)}, f32[16,128]{1,0:T(8,128)}, u32[]{:S(2)}) copy-start(f32[16,128]{1,0:T(8,128)} %w_ref.7) | copy-start | bytes 24580
  4.1 7.4 %copy-start = (f32[4,16,128]{2,1,0:T(8,128)S(1)}, f32[4,16,128]{2,1,0:T(8,128)}, u32[]{:S(2)}) copy-start(f32[4,16,128]{2,1,0:T(8,128)} %d_ref.7) | copy-start | bytes 98308
  4.2 85.4 %all-to-all-start = ((bf16[16,16,4,16,128]{4,3,2,1,0:T(8,128)(2,1)}), bf16[16,16,4,16,128]{4,3,2,1,0:T(8,128)(2,1)}, u32[]{:S(2)}, u32[]{:S(2)}) async-start(bf16[16,16,4,16,128]{4,3,2,1,0:T(8,128)(2,1)} %relayout.1), calls=%async_computation | async-start | bytes 8388608 | tf_op jit(solution)/shard_map/all_to_all | solution.py:528
  91.1 8.3 %collective-permute-start = (bf16[17,2,4,16,128]{4,3,2,1,0:T(8,128)(2,1)S(1)}, bf16[17,2,4,16,128]{4,3,2,1,0:T(8,128)(2,1)S(1)}, u32[]{:S(2)}, u32[]{:S(2)}) collective-permute-start(bf16[17,2,4,16,128]{4,3,2,1,0:T(8,128)(2,1)S(1)} %get-tuple-element.37), channel_id=1, source_target_pairs={{0,1},{2,3},{4,5},{6,7},{8,9},{10,11},{12,13},{14,15},{1,0},{3,2},... | collective-permute-start | bytes 1671176 | tf_op jit(solution)/shard_map/ppermute | solution.py:520
  91.2 33.7 %collective-permute-start.7 = (bf16[17,2,4,16,128]{4,3,2,1,0:T(8,128)(2,1)S(1)}, bf16[17,2,4,16,128]{4,3,2,1,0:T(8,128)(2,1)S(1)}, u32[]{:S(2)}, u32[]{:S(2)}) collective-permute-start(bf16[17,2,4,16,128]{4,3,2,1,0:T(8,128)(2,1)S(1)} %get-tuple-element.54), channel_id=1, source_target_pairs={{1,2},{3,4},{5,6},{7,8},{9,10},{11,12},{13,14},{17,18},{19,20},{21... | collective-permute-start | bytes 1671176 | tf_op jit(solution)/shard_map/ppermute | solution.py:499
  104.1 1.3 collective-permute-start.1
  105.4 13.5 %collective-permute-start.2 = (f32[72,256]{1,0:T(8,128)S(1)}, f32[72,256]{1,0:T(8,128)S(1)}, u32[]{:S(2)}, u32[]{:S(2)}) collective-permute-start(f32[72,256]{1,0:T(8,128)S(1)} %select_add_fusion.1), channel_id=1, source_target_pairs={{0,2},{1,3},{2,0},{3,1},{4,6},{5,7},{6,4},{7,5},{8,10},{9,11},{10,... | collective-permute-start | bytes 221192 | tf_op jit(solution)/shard_map/ppermute | solution.py:475
  118.9 5.9 %collective-permute-start.3 = (f32[72,256]{1,0:T(8,128)S(1)}, f32[72,256]{1,0:T(8,128)S(1)}, u32[]{:S(2)}, u32[]{:S(2)}) collective-permute-start(f32[72,256]{1,0:T(8,128)S(1)} %add.36), channel_id=1, source_target_pairs={{0,4},{1,5},{2,6},{3,7},{4,0},{5,1},{6,2},{7,3},{8,12},{9,13},{10,... | collective-permute-start | bytes 221192 | tf_op jit(solution)/shard_map/ppermute | solution.py:475
  122.0 12.1 %collective-permute-start.5 = (bf16[2,4,256,128]{3,2,1,0:T(8,128)(2,1)S(1)}, bf16[2,4,256,128]{3,2,1,0:T(8,128)(2,1)S(1)}, u32[]{:S(2)}, u32[]{:S(2)}) collective-permute-start(bf16[2,4,256,128]{3,2,1,0:T(8,128)(2,1)S(1)} %get-tuple-element.52), channel_id=1, source_target_pairs={{2,1},{4,3},{6,5},{8,7},{10,9},{12,11},{14,13},{18,17},{20,19},{22... | collective-permute-start | bytes 1572872 | tf_op jit(solution)/shard_map/ppermute | solution.py:499
  126.4 2.2 %collective-permute-start.8 = (f32[128,256]{1,0:T(8,128)S(1)}, f32[128,256]{1,0:T(8,128)S(1)}, u32[]{:S(2)}, u32[]{:S(2)}) collective-permute-start(f32[128,256]{1,0:T(8,128)S(1)} %slice_select_fusion), channel_id=1, source_target_pairs={{0,1},{1,0},{2,3},{3,2},{4,5},{5,4},{6,7},{7,6},{8,9},{9,8},{10,11... | collective-permute-start | bytes 393224 | tf_op jit(solution)/shard_map/ppermute | solution.py:475
  126.9 5.0 %collective-permute-start.4 = (f32[72,256]{1,0:T(8,128)S(1)}, f32[72,256]{1,0:T(8,128)S(1)}, u32[]{:S(2)}, u32[]{:S(2)}) collective-permute-start(f32[72,256]{1,0:T(8,128)S(1)} %add.37), channel_id=1, source_target_pairs={{0,8},{1,9},{2,10},{3,11},{4,12},{5,13},{6,14},{7,15},{8,0},{9,1},... | collective-permute-start | bytes 221192 | tf_op jit(solution)/shard_map/ppermute | solution.py:475
  128.7 8.0 %collective-permute-start.9 = (f32[128,256]{1,0:T(8,128)S(1)}, f32[128,256]{1,0:T(8,128)S(1)}, u32[]{:S(2)}, u32[]{:S(2)}) collective-permute-start(f32[128,256]{1,0:T(8,128)S(1)} %select_add_fusion), channel_id=1, source_target_pairs={{0,2},{1,3},{2,0},{3,1},{4,6},{5,7},{6,4},{7,5},{8,10},{9,11},{10,... | collective-permute-start | bytes 393224 | tf_op jit(solution)/shard_map/ppermute | solution.py:475
  134.7 2.9 %collective-permute-start.6 = (f32[72,256]{1,0:T(8,128)S(1)}, f32[72,256]{1,0:T(8,128)S(1)}, u32[]{:S(2)}, u32[]{:S(2)}) collective-permute-start(f32[72,256]{1,0:T(8,128)S(1)} %add.38), channel_id=1, source_target_pairs={{0,1},{1,0},{2,3},{3,2},{4,5},{5,4},{6,7},{7,6},{8,9},{9,8},{10,11... | collective-permute-start | bytes 221192 | tf_op jit(solution)/shard_map/ppermute | solution.py:475
  137.6 4.8 %collective-permute-start.10 = (f32[128,256]{1,0:T(8,128)S(1)}, f32[128,256]{1,0:T(8,128)S(1)}, u32[]{:S(2)}, u32[]{:S(2)}) collective-permute-start(f32[128,256]{1,0:T(8,128)S(1)} %add.40), channel_id=1, source_target_pairs={{0,4},{1,5},{2,6},{3,7},{4,0},{5,1},{6,2},{7,3},{8,12},{9,13},{10,... | collective-permute-start | bytes 393224 | tf_op jit(solution)/shard_map/ppermute | solution.py:475
  142.5 9.6 %collective-permute-start.11 = (f32[128,256]{1,0:T(8,128)S(1)}, f32[128,256]{1,0:T(8,128)S(1)}, u32[]{:S(2)}, u32[]{:S(2)}) collective-permute-start(f32[128,256]{1,0:T(8,128)S(1)} %add.41), channel_id=1, source_target_pairs={{0,8},{1,9},{2,10},{3,11},{4,12},{5,13},{6,14},{7,15},{8,0},{9,1},... | collective-permute-start | bytes 393224 | tf_op jit(solution)/shard_map/ppermute | solution.py:475
  152.1 3.1 %collective-permute-start.12 = (f32[128,256]{1,0:T(8,128)S(1)}, f32[128,256]{1,0:T(8,128)S(1)}, u32[]{:S(2)}, u32[]{:S(2)}) collective-permute-start(f32[128,256]{1,0:T(8,128)S(1)} %add.42), channel_id=1, source_target_pairs={{0,1},{1,0},{2,3},{3,2},{4,5},{5,4},{6,7},{7,6},{8,9},{9,8},{10,11... | collective-permute-start | bytes 393224 | tf_op jit(solution)/shard_map/ppermute | solution.py:475

commit v7 on v6

--- a/solution.py
+++ b/solution.py
@@ -372,7 +372,7 @@
             work_ref[end:, :] = jnp.where((place >= start) & (place < end), 0.0, rest) - update
 
 
-def rotation_first_kernel(scale, gram_ref, out_ref, work_ref):
+def rotation_kernel(scale, gram_ref, out_ref, work_ref):
     size = work_ref.shape[0]
     half = size // 2
     first, last = unpack(gram_ref[:half, :half] * scale, gram_ref[half : half + 1, :half] * scale)
@@ -380,45 +380,21 @@
     work_ref[half:, half:] = last
     work_ref[:half, half:] = gram_ref[:half, half:] * scale
     work_ref[half:, :half] = jnp.zeros((half, half), jnp.float32)
-    rotation_panels(0, half, out_ref, work_ref)
-
-
-def rotation_last_kernel(before_ref, state_ref, out_ref, work_ref):
-    size = work_ref.shape[0]
-    half = size // 2
-    out_ref[:half, :] = before_ref[...]
-    work_ref[half:, :] = state_ref[half:, :]
-    rotation_panels(half, size, out_ref, work_ref)
-
-
-def rotation_first(packed, cell_count):
+    rotation_panels(0, size, out_ref, work_ref)
+
+
+def rotation_of(packed, cell_count):
     size = packed.shape[1]
     return pl.pallas_call(
-        lambda *refs: rotation_first_kernel(1.0 / cell_count, *refs),
+        lambda *refs: rotation_kernel(1.0 / cell_count, *refs),
         in_specs=[VMEM],
-        out_specs=[VMEM, VMEM],
-        out_shape=[
-            jax.ShapeDtypeStruct((size // 2, size), jnp.float32),
-            jax.ShapeDtypeStruct((size, size), jnp.float32),
-        ],
-        compiler_params=params(),
-        cost_estimate=cost(1),
-        name="rotation_first",
-    )(packed)
-
-
-def rotation_last(before, state):
-    size = state.shape[0]
-    return pl.pallas_call(
-        rotation_last_kernel,
-        in_specs=[VMEM, VMEM],
         out_specs=VMEM,
         out_shape=jax.ShapeDtypeStruct((size, size), jnp.float32),
         scratch_shapes=[pltpu.VMEM((size, size), jnp.float32)],
         compiler_params=params(),
         cost_estimate=cost(1),
-        name="rotation_last",
-    )(before, state)
+        name="rotation",
+    )(packed)
 
 
 def modes_kernel(first, r_ref, low_ref, mid_ref, top_ref, *refs):
@@ -576,11 +552,10 @@
     )
     gram.own, top = together((gram.own, top))
     packed, cross.own = together((gram.result(), cross.own))
-    state = rotation_first(packed, cell_count)
+    rotation = rotation_of(packed, cell_count)
     if steps:
-        cross.add(steps.pop(0))
-    state, cross.own = together((state, cross.own))
-    rotation = rotation_last(*state)
+        cross.add(steps.pop())
+    rotation, cross.own = together((rotation, cross.own))
     while steps:
         cross.add(steps.pop(0))
     modes = None

time: 157 us -> 157 us (level)
    pallas_call x2 -> x1, Pallas kernels: 8.44 us -> 8.43 us  [rotation_of(): pl.pallas_call(lambda *refs: rotation_kernel(1.0 / cell_count, *refs), in...]
where the time goes in v7:
time: 157 us
  waiting for transfers between devices  84.5 us (54%)
  starting transfers between devices  37 us (24%)
  Pallas kernels  30.6 us (19%)
    all_to_all x1, waiting for transfers between devices, on_device(): block = lax.all_to_all(relayout(snapshots, owners), 'gx', 0, 0, tiled=True)  77.9 us
    ppermute x10, starting transfers between devices, swap(): lax.ppermute(part, self.axis, [(i, i ^ step) for i in range(self.count)])  19.9 us
    ppermute x2, starting transfers between devices, hop(): lax.ppermute(value, axis, [(i, i + step) for i in range(first, devices, 2...  9.67 us
    pallas_call x1, Pallas kernels, rotation_of(): pl.pallas_call(lambda *refs: rotation_kernel(1.0 / cell_count, *refs), in...  8.43 us
    all_to_all x1, starting transfers between devices, on_device(): block = lax.all_to_all(relayout(snapshots, owners), 'gx', 0, 0, tiled=True)  7.36 us
    pallas_call x4, Pallas kernels, stencil_call(): pl.pallas_call(kernel, in_specs=[pl.BlockSpec(memory_space=pltpu.SMEM)] *...  7.31 us
    pallas_call x2, Pallas kernels, modes_of(): pl.pallas_call(lambda *refs: modes_kernel(first, *refs), grid=(span,), in...  6.74 us
    pallas_call x1, Pallas kernels, gram_of(): pl.pallas_call(gram_kernel, grid=(variables // each,), in_specs=[pl.Block...  4.59 us
  transfers between devices with their start and end apart: 14, of which 6 were waited for; matrix products, arithmetic and copies ran while one was open for 0% of the time, Pallas kernels for 17%

profile of v7, /device:TPU:1, one launch (start us, length us, event | category | flops | bytes accessed | tf_op | source)
XLA Modules:
  0.0 156.5 jit_solution(7611985452640011851)
XLA Ops:
  0.6 3.5 %relayout.1 = bf16[16,16,4,16,128]{4,3,2,1,0:T(8,128)(2,1)} custom-call(bf16[16,4,256,128]{3,2,1,0:T(8,128)(2,1)} %in_ref.1), custom_call_target="tpu_custom_call" | custom-call | tf_op jit(solution)/shard_map/relayout/pallas_call | solution.py:73
  4.1 0.0 copy-start.1
  4.1 0.0 copy-start
  4.2 7.4 %all-to-all-start = ((bf16[16,16,4,16,128]{4,3,2,1,0:T(8,128)(2,1)}), bf16[16,16,4,16,128]{4,3,2,1,0:T(8,128)(2,1)}, u32[]{:S(2)}, u32[]{:S(2)}) async-start(bf16[16,16,4,16,128]{4,3,2,1,0:T(8,128)(2,1)} %relayout.1), calls=%async_computation | async-start | bytes 8388608 | tf_op jit(solution)/shard_map/all_to_all | solution.py:504
  11.5 0.0 copy-done.1
  11.5 0.0 copy-done
  11.7 77.9 %all-to-all-done.x_ref = bf16[16,16,4,16,128]{4,3,2,1,0:T(8,128)(2,1)} async-done(((bf16[16,16,4,16,128]{4,3,2,1,0:T(8,128)(2,1)}), bf16[16,16,4,16,128]{4,3,2,1,0:T(8,128)(2,1)}, u32[]{:S(2)}, u32[]{:S(2)}) %all-to-all-start) | async-done | bytes 4194336 | tf_op jit(solution)/shard_map/all_to_all | solution.py:504
  89.6 1.4 fusion.13
  91.0 0.1 pad_maximum_fusion
  91.1 0.1 collective-permute-start
  91.2 8.2 %collective-permute-start.7 = (bf16[17,2,4,16,128]{4,3,2,1,0:T(8,128)(2,1)S(1)}, bf16[17,2,4,16,128]{4,3,2,1,0:T(8,128)(2,1)S(1)}, u32[]{:S(2)}, u32[]{:S(2)}) collective-permute-start(bf16[17,2,4,16,128]{4,3,2,1,0:T(8,128)(2,1)S(1)} %get-tuple-element.51), channel_id=1, source_target_pairs={{1,2},{3,4},{5,6},{7,8},{9,10},{11,12},{13,14},{17,18},{19,20},{21... | collective-permute-start | bytes 1671176 | tf_op jit(solution)/shard_map/ppermute | solution.py:475
  99.4 0.0 collective-permute-done.near_ref
  99.4 4.6 %gram.1 = (f32[144,256]{1,0:T(8,128)S(1)}, bf16[4,16,256,128]{3,2,1,0:T(8,128)(2,1)S(1)}, bf16[2,4,256,128]{3,2,1,0:T(8,128)(2,1)S(1)}) custom-call(bf16[16,16,4,16,128]{4,3,2,1,0:T(8,128)(2,1)} %all-to-all-done.x_ref, f32[16,128]{1,0:T(8,128)S(1)} %copy-done.1), custom_call_target="tpu_custom_call" | custom-call | flops 2000000000 | bytes 1 | tf_op jit(solution)/shard_map/gram/pallas_call | solution.py:152
  104.1 0.1 collective-permute-start.1
  104.2 1.2 collective-permute-done.1
  105.4 9.3 %collective-permute-start.2 = (f32[72,256]{1,0:T(8,128)S(1)}, f32[72,256]{1,0:T(8,128)S(1)}, u32[]{:S(2)}, u32[]{:S(2)}) collective-permute-start(f32[72,256]{1,0:T(8,128)S(1)} %select_add_fusion.1), channel_id=1, source_target_pairs={{0,2},{1,3},{2,0},{3,1},{4,6},{5,7},{6,4},{7,5},{8,10},{9,11},{10,... | collective-permute-start | bytes 221192 | tf_op jit(solution)/shard_map/ppermute | solution.py:451
  114.8 0.2 select_convert_fusion.band_ref
  115.0 3.9 %inner.2 = (f32[256,256]{1,0:T(8,128)S(1)}, bf16[2,3,6,256,256]{4,3,2,1,0:T(8,128)(2,1)S(1)}) custom-call(bf16[4,16,256,128]{3,2,1,0:T(8,128)(2,1)S(1)} %get-tuple-element.47.x_ref, f32[16,128]{1,0:T(8,128)S(1)} %copy-done.1, f32[4,16,128]{2,1,0:T(8,128)S(1)} %copy-done, bf16[256,256]{1,0:T(8,128)(2,1)S(1)} %select_convert_fusion.band_ref, ...), custom_call_target="tpu_custom_call" | custom-call | flops 1 | bytes 1 | tf_op jit(solution)/shard_map/inner/pallas_call | solution.py:277
  118.9 0.0 collective-permute-done.2
  118.9 3.1 %collective-permute-start.3 = (f32[72,256]{1,0:T(8,128)S(1)}, f32[72,256]{1,0:T(8,128)S(1)}, u32[]{:S(2)}, u32[]{:S(2)}) collective-permute-start(f32[72,256]{1,0:T(8,128)S(1)} %add.36), channel_id=1, source_target_pairs={{0,4},{1,5},{2,6},{3,7},{4,0},{5,1},{6,2},{7,3},{8,12},{9,13},{10,... | collective-permute-start | bytes 221192 | tf_op jit(solution)/shard_map/ppermute | solution.py:451
  122.0 1.5 collective-permute-start.5
  123.5 1.3 inner.3
  124.8 0.0 collective-permute-done.3
  124.9 0.0 collective-permute-done.7.far_ref
  124.9 1.5 lower.1
  126.4 0.5 collective-permute-start.8
  126.9 1.8 %collective-permute-start.4 = (f32[72,256]{1,0:T(8,128)S(1)}, f32[72,256]{1,0:T(8,128)S(1)}, u32[]{:S(2)}, u32[]{:S(2)}) collective-permute-start(f32[72,256]{1,0:T(8,128)S(1)} %add.37), channel_id=1, source_target_pairs={{0,8},{1,9},{2,10},{3,11},{4,12},{5,13},{6,14},{7,15},{8,0},{9,1},... | collective-permute-start | bytes 221192 | tf_op jit(solution)/shard_map/ppermute | solution.py:451
  128.6 0.0 collective-permute-done.8
  128.7 1.4 collective-permute-start.9
  130.1 1.8 %collective-permute-done.4 = f32[72,256]{1,0:T(8,128)S(1)} collective-permute-done((f32[72,256]{1,0:T(8,128)S(1)}, f32[72,256]{1,0:T(8,128)S(1)}, u32[]{:S(2)}, u32[]{:S(2)}) %collective-permute-start.4) | collective-permute-done | bytes 73760 | tf_op jit(solution)/shard_map/ppermute | solution.py:451
  131.8 2.3 %collective-permute-done.5.far_ref = bf16[2,4,256,128]{3,2,1,0:T(8,128)(2,1)S(1)} collective-permute-done((bf16[2,4,256,128]{3,2,1,0:T(8,128)(2,1)S(1)}, bf16[2,4,256,128]{3,2,1,0:T(8,128)(2,1)S(1)}, u32[]{:S(2)}, u32[]{:S(2)}) %collective-permute-start.5) | collective-permute-done | bytes 524320 | tf_op jit(solution)/shard_map/ppermute | solution.py:475
  134.1 0.6 upper.1.refs_3_
  134.7 2.0 %collective-permute-start.6 = (f32[72,256]{1,0:T(8,128)S(1)}, f32[72,256]{1,0:T(8,128)S(1)}, u32[]{:S(2)}, u32[]{:S(2)}) collective-permute-start(f32[72,256]{1,0:T(8,128)S(1)} %add.38), channel_id=1, source_target_pairs={{0,1},{1,0},{2,3},{3,2},{4,5},{5,4},{6,7},{7,6},{8,9},{9,8},{10,11... | collective-permute-start | bytes 221192 | tf_op jit(solution)/shard_map/ppermute | solution.py:451
  136.7 0.0 collective-permute-done.9
  136.7 0.9 collective-permute-done.6
  137.6 0.1 collective-permute-start.10
  137.7 8.4 %rotation.1.refs_0_ = f32[256,256]{1,0:T(8,128)S(1)} custom-call(f32[144,256]{1,0:T(8,128)S(1)} %pad_maximum_fusion.2.refs_0_), custom_call_target="tpu_custom_call" | custom-call | flops 1 | bytes 1 | tf_op jit(solution)/shard_map/rotation/pallas_call | solution.py:388
  146.2 0.3 collective-permute-done.10
  146.5 0.7 collective-permute-start.11
  147.2 4.6 %modes.2.refs_4_ = bf16[256,4,16,128]{3,2,1,0:T(8,128)(2,1)} custom-call(f32[256,256]{1,0:T(8,128)S(1)} %rotation.1.refs_0_, bf16[2,4,1,256,256]{4,3,2,1,0:T(8,128)(2,1)S(1)} %get-tuple-element.57.refs_1_, bf16[2,3,6,256,256]{4,3,2,1,0:T(8,128)(2,1)S(1)} %get-tuple-element.60.refs_2_, bf16[2,4,1,256,256]{4,3,2,1,0:T(8,128)(2,1)S(1)} %upper.1.refs_3_), custom_call_target="tpu_custom_call" | custom-call | flops 1 | bytes 1 | tf_op jit(solution)/shard_map/modes/pallas_call | solution.py:421
  151.8 0.0 collective-permute-done.11
  151.8 1.0 collective-permute-start.12
  152.8 2.2 %modes.3 = bf16[256,4,16,128]{3,2,1,0:T(8,128)(2,1)} custom-call(f32[256,256]{1,0:T(8,128)S(1)} %rotation.1.refs_0_, bf16[2,4,1,256,256]{4,3,2,1,0:T(8,128)(2,1)S(1)} %get-tuple-element.57.refs_1_, bf16[2,1,6,256,256]{4,3,2,1,0:T(8,128)(2,1)S(1)} %get-tuple-element.58.refs_2_, ...), custom_call_target="tpu_custom_call", output_to_operand_aliasing={{}: (4, {})} | custom-call | flops 1342177280 | bytes 1 | tf_op jit(solution)/shard_map/modes/pallas_call | solution.py:421
  154.9 0.0 collective-permute-done.12
  155.0 0.4 fusion
  155.4 1.1 fusion.14
  (22 shorter events, 0.3 us)
Async XLA Ops:
  4.1 7.4 %copy-start.1 = (f32[16,128]{1,0:T(8,128)S(1)}, f32[16,128]{1,0:T(8,128)}, u32[]{:S(2)}) copy-start(f32[16,128]{1,0:T(8,128)} %w_ref.7) | copy-start | bytes 24580
  4.1 7.4 %copy-start = (f32[4,16,128]{2,1,0:T(8,128)S(1)}, f32[4,16,128]{2,1,0:T(8,128)}, u32[]{:S(2)}) copy-start(f32[4,16,128]{2,1,0:T(8,128)} %d_ref.7) | copy-start | bytes 98308
  4.2 85.4 %all-to-all-start = ((bf16[16,16,4,16,128]{4,3,2,1,0:T(8,128)(2,1)}), bf16[16,16,4,16,128]{4,3,2,1,0:T(8,128)(2,1)}, u32[]{:S(2)}, u32[]{:S(2)}) async-start(bf16[16,16,4,16,128]{4,3,2,1,0:T(8,128)(2,1)} %relayout.1), calls=%async_computation | async-start | bytes 8388608 | tf_op jit(solution)/shard_map/all_to_all | solution.py:504
  91.1 8.3 %collective-permute-start = (bf16[17,2,4,16,128]{4,3,2,1,0:T(8,128)(2,1)S(1)}, bf16[17,2,4,16,128]{4,3,2,1,0:T(8,128)(2,1)S(1)}, u32[]{:S(2)}, u32[]{:S(2)}) collective-permute-start(bf16[17,2,4,16,128]{4,3,2,1,0:T(8,128)(2,1)S(1)} %get-tuple-element.34), channel_id=1, source_target_pairs={{0,1},{2,3},{4,5},{6,7},{8,9},{10,11},{12,13},{14,15},{1,0},{3,2},... | collective-permute-start | bytes 1671176 | tf_op jit(solution)/shard_map/ppermute | solution.py:496
  91.2 33.7 %collective-permute-start.7 = (bf16[17,2,4,16,128]{4,3,2,1,0:T(8,128)(2,1)S(1)}, bf16[17,2,4,16,128]{4,3,2,1,0:T(8,128)(2,1)S(1)}, u32[]{:S(2)}, u32[]{:S(2)}) collective-permute-start(bf16[17,2,4,16,128]{4,3,2,1,0:T(8,128)(2,1)S(1)} %get-tuple-element.51), channel_id=1, source_target_pairs={{1,2},{3,4},{5,6},{7,8},{9,10},{11,12},{13,14},{17,18},{19,20},{21... | collective-permute-start | bytes 1671176 | tf_op jit(solution)/shard_map/ppermute | solution.py:475
  104.1 1.3 collective-permute-start.1
  105.4 13.5 %collective-permute-start.2 = (f32[72,256]{1,0:T(8,128)S(1)}, f32[72,256]{1,0:T(8,128)S(1)}, u32[]{:S(2)}, u32[]{:S(2)}) collective-permute-start(f32[72,256]{1,0:T(8,128)S(1)} %select_add_fusion.1), channel_id=1, source_target_pairs={{0,2},{1,3},{2,0},{3,1},{4,6},{5,7},{6,4},{7,5},{8,10},{9,11},{10,... | collective-permute-start | bytes 221192 | tf_op jit(solution)/shard_map/ppermute | solution.py:451
  118.9 5.9 %collective-permute-start.3 = (f32[72,256]{1,0:T(8,128)S(1)}, f32[72,256]{1,0:T(8,128)S(1)}, u32[]{:S(2)}, u32[]{:S(2)}) collective-permute-start(f32[72,256]{1,0:T(8,128)S(1)} %add.36), channel_id=1, source_target_pairs={{0,4},{1,5},{2,6},{3,7},{4,0},{5,1},{6,2},{7,3},{8,12},{9,13},{10,... | collective-permute-start | bytes 221192 | tf_op jit(solution)/shard_map/ppermute | solution.py:451
  122.0 12.1 %collective-permute-start.5 = (bf16[2,4,256,128]{3,2,1,0:T(8,128)(2,1)S(1)}, bf16[2,4,256,128]{3,2,1,0:T(8,128)(2,1)S(1)}, u32[]{:S(2)}, u32[]{:S(2)}) collective-permute-start(bf16[2,4,256,128]{3,2,1,0:T(8,128)(2,1)S(1)} %get-tuple-element.49), channel_id=1, source_target_pairs={{2,1},{4,3},{6,5},{8,7},{10,9},{12,11},{14,13},{18,17},{20,19},{22... | collective-permute-start | bytes 1572872 | tf_op jit(solution)/shard_map/ppermute | solution.py:475
  126.4 2.2 %collective-permute-start.8 = (f32[128,256]{1,0:T(8,128)S(1)}, f32[128,256]{1,0:T(8,128)S(1)}, u32[]{:S(2)}, u32[]{:S(2)}) collective-permute-start(f32[128,256]{1,0:T(8,128)S(1)} %slice_select_fusion), channel_id=1, source_target_pairs={{0,1},{1,0},{2,3},{3,2},{4,5},{5,4},{6,7},{7,6},{8,9},{9,8},{10,11... | collective-permute-start | bytes 393224 | tf_op jit(solution)/shard_map/ppermute | solution.py:451
  126.9 5.0 %collective-permute-start.4 = (f32[72,256]{1,0:T(8,128)S(1)}, f32[72,256]{1,0:T(8,128)S(1)}, u32[]{:S(2)}, u32[]{:S(2)}) collective-permute-start(f32[72,256]{1,0:T(8,128)S(1)} %add.37), channel_id=1, source_target_pairs={{0,8},{1,9},{2,10},{3,11},{4,12},{5,13},{6,14},{7,15},{8,0},{9,1},... | collective-permute-start | bytes 221192 | tf_op jit(solution)/shard_map/ppermute | solution.py:451
  128.7 8.0 %collective-permute-start.9 = (f32[128,256]{1,0:T(8,128)S(1)}, f32[128,256]{1,0:T(8,128)S(1)}, u32[]{:S(2)}, u32[]{:S(2)}) collective-permute-start(f32[128,256]{1,0:T(8,128)S(1)} %select_add_fusion), channel_id=1, source_target_pairs={{0,2},{1,3},{2,0},{3,1},{4,6},{5,7},{6,4},{7,5},{8,10},{9,11},{10,... | collective-permute-start | bytes 393224 | tf_op jit(solution)/shard_map/ppermute | solution.py:451
  134.7 2.9 %collective-permute-start.6 = (f32[72,256]{1,0:T(8,128)S(1)}, f32[72,256]{1,0:T(8,128)S(1)}, u32[]{:S(2)}, u32[]{:S(2)}) collective-permute-start(f32[72,256]{1,0:T(8,128)S(1)} %add.38), channel_id=1, source_target_pairs={{0,1},{1,0},{2,3},{3,2},{4,5},{5,4},{6,7},{7,6},{8,9},{9,8},{10,11... | collective-permute-start | bytes 221192 | tf_op jit(solution)/shard_map/ppermute | solution.py:451
  137.6 8.8 %collective-permute-start.10 = (f32[128,256]{1,0:T(8,128)S(1)}, f32[128,256]{1,0:T(8,128)S(1)}, u32[]{:S(2)}, u32[]{:S(2)}) collective-permute-start(f32[128,256]{1,0:T(8,128)S(1)} %add.40), channel_id=1, source_target_pairs={{0,8},{1,9},{2,10},{3,11},{4,12},{5,13},{6,14},{7,15},{8,0},{9,1},... | collective-permute-start | bytes 393224 | tf_op jit(solution)/shard_map/ppermute | solution.py:451
  146.5 5.3 %collective-permute-start.11 = (f32[128,256]{1,0:T(8,128)S(1)}, f32[128,256]{1,0:T(8,128)S(1)}, u32[]{:S(2)}, u32[]{:S(2)}) collective-permute-start(f32[128,256]{1,0:T(8,128)S(1)} %add.41), channel_id=1, source_target_pairs={{0,4},{1,5},{2,6},{3,7},{4,0},{5,1},{6,2},{7,3},{8,12},{9,13},{10,... | collective-permute-start | bytes 393224 | tf_op jit(solution)/shard_map/ppermute | solution.py:451
  151.8 3.1 %collective-permute-start.12 = (f32[128,256]{1,0:T(8,128)S(1)}, f32[128,256]{1,0:T(8,128)S(1)}, u32[]{:S(2)}, u32[]{:S(2)}) collective-permute-start(f32[128,256]{1,0:T(8,128)S(1)} %add.42), channel_id=1, source_target_pairs={{0,1},{1,0},{2,3},{3,2},{4,5},{5,4},{6,7},{7,6},{8,9},{9,8},{10,11... | collective-permute-start | bytes 393224 | tf_op jit(solution)/shard_map/ppermute | solution.py:451
